TPU v7x, 32 devices: a whole 2x2x4 slice. The times are simulated.
32 devices in a mesh: leaf: 8 (over y, x, core), front: 4 (over z).
Axes of the slice: x: 2, y: 2, z: 4, core: 2. Of those that a mesh axis runs over, the one named last changes fastest.
Arguments:
- leaf_contrib: float32 [8192, 1024], P(('leaf', 'front')), may hold values from -1 to 7, as said below
- entries_lower: float32 [8192, 1024], P(('leaf', 'front')), may hold values from -1 to 4, as said below
- entries_middle: float32 [4096, 1024], P(('leaf', 'front')), may hold values from -1 to 4, as said below
- entries_upper: float32 [2048, 1024], P(('leaf', 'front')), may hold values from -1 to 4, as said below
- assembly_lower: int32 [4, 2, 8], replicated, may hold values from 0 to 15, as said below
- assembly_middle: int32 [2, 2, 8], replicated, may hold values from 0 to 15, as said below
- assembly_upper: int32 [1, 2, 8], replicated, may hold values from 0 to 15, as said below
Outputs:
- factor_lower: float32 [8192, 1024], P(('leaf', 'front'))
- factor_middle: float32 [4096, 1024], P(('leaf', 'front'))
- factor_upper: float32 [2048, 1024], P(('leaf', 'front'))
- top_update: float32 [1024, 1024], P(('leaf', 'front'))
Inputs may be any that keep to these rules, and one draw needn't show every extreme that they name: `leaf_contrib`: in natural row order each leaf's block is symmetric positive definite. `entries_lower`: in natural row order the first 1024 rows of each front's entries form a symmetric positive definite block. `entries_middle`: in natural row order the first 1024 rows of each front's entries form a symmetric positive definite block. `entries_upper`: in natural row order the first 1024 rows of each front's entries form a symmetric positive definite block. `assembly_lower`: each child's block j goes to parent block j or j + 8, and at least one of the two children sends its block j to j + 8. `assembly_middle`: each child's block j goes to parent block j or j + 8, and at least one of the two children sends its block j to j + 8. `assembly_upper`: each child's block j goes to parent block j or j + 8, and at least one of the two children sends its block j to j + 8.
All inputs are finite; a program needn't handle non-finite values.
Results may differ from a plain program's by a relative error of at most 0.0003.
Values sent between devices are 32-bit elements; how exact they have to be, the bound alone decides.
No kernel may reach another device: no remote copies, remote signals or barrier semaphores. Data moves between devices by JAX's collectives and lax.ppermute only.
A program may use at most 128 MiB of HBM per device.

v0:
```python
import jax
import jax.numpy as jnp
from jax import lax
from jax.sharding import PartitionSpec as P

BLK = 128
PIVOT_BLOCKS = 8


def partner_2(value, axis, stride):
    mask = 2**stride
    pairs = [(source, source ^ mask) for source in range(lax.axis_size(axis))]
    return lax.ppermute(value, axis, pairs)


def product(left, right):
    return jnp.dot(left, right, precision=lax.Precision.HIGHEST, preferred_element_type=jnp.float32)


def factor_inverse(matrix):
    order_size = matrix.shape[0]
    if order_size <= 128 or order_size % 2 != 0:
        lower_factor = jnp.linalg.cholesky(matrix)
        identity = jnp.eye(order_size, dtype=jnp.float32)
        inverse = jax.scipy.linalg.solve_triangular(lower_factor, identity, lower=True)
        return (lower_factor, inverse)
    half = order_size // 2
    first_factor, first_inverse = factor_inverse(matrix[:half, :half])
    coupling = product(matrix[half:, :half], first_inverse.T)
    second_factor, second_inverse = factor_inverse(
        matrix[half:, half:] - product(coupling, coupling.T)
    )
    corner = -product(second_inverse, product(coupling, first_inverse))
    zeros_block = jnp.zeros((half, half), jnp.float32)
    lower_factor = jnp.concatenate(
        [
            jnp.concatenate([first_factor, zeros_block], 1),
            jnp.concatenate([coupling, second_factor], 1),
        ],
        0,
    )
    inverse = jnp.concatenate(
        [
            jnp.concatenate([first_inverse, zeros_block], 1),
            jnp.concatenate([corner, second_inverse], 1),
        ],
        0,
    )
    return (lower_factor, inverse)


def reversed_bits(number, bit_count):
    result = jnp.zeros((), jnp.int32)
    for bit_index in range(bit_count):
        result = result + (number >> bit_index & 1) * (1 << bit_count - 1 - bit_index)
    return result


def join_pieces(mine, theirs, bit_index, axis_index):
    upper_bit = lax.axis_index("leaf") >> bit_index & 1
    return jnp.where(
        upper_bit == 0,
        jnp.concatenate([mine, theirs], axis_index),
        jnp.concatenate([theirs, mine], axis_index),
    )


def group_gather(pieces, height):
    gathered = lax.all_gather(pieces[:, None], "front", axis=1, tiled=True)
    for bit_index in reversed(range(height)):
        partner = partner_2(gathered, "leaf", bit_index)
        gathered = join_pieces(gathered, partner, bit_index, 2)
    return gathered


def spread_columns(rows_in, upper_mask):
    blocks = rows_in.reshape(rows_in.shape[0], rows_in.shape[1], upper_mask.shape[0], -1)
    to_pivot = blocks * (1.0 - upper_mask)[None, None, :, None]
    to_update = blocks * upper_mask[None, None, :, None]
    return jnp.concatenate([to_pivot, to_update], axis=2).reshape(
        rows_in.shape[0], rows_in.shape[1], -1
    )


def own_rows(whole, front_index, piece_index, piece_rows):
    chosen = lax.dynamic_index_in_dim(whole, front_index, 1, keepdims=False)
    return lax.dynamic_slice_in_dim(chosen, piece_index * piece_rows, piece_rows, 1)


def local(
    leaf_contrib,
    entries_lower,
    entries_middle,
    entries_upper,
    assembly_lower,
    assembly_middle,
    assembly_upper,
):
    front_count = lax.axis_size("front")
    local_count = PIVOT_BLOCKS // front_count
    leaf_index = lax.axis_index("leaf")
    front_index = lax.axis_index("front")
    pivot_size = leaf_contrib.shape[1]
    update = leaf_contrib.reshape(local_count, BLK, pivot_size)
    my_blocks = front_index + front_count * jnp.arange(local_count, dtype=jnp.int32)
    selector = (jnp.arange(PIVOT_BLOCKS, dtype=jnp.int32)[None, :] == my_blocks[:, None]).astype(
        jnp.float32
    )
    results = []
    for height, entries, routes in (
        (1, entries_lower, assembly_lower),
        (2, entries_middle, assembly_middle),
        (3, entries_upper, assembly_upper),
    ):
        piece_rows = BLK // 2**height
        child_bit = leaf_index >> height - 1 & 1
        low_rows = update[:, :piece_rows]
        high_rows = update[:, piece_rows:]
        kept = jnp.where(child_bit == 0, low_rows, high_rows)
        outgoing = jnp.where(child_bit == 0, high_rows, low_rows)
        received = partner_2(outgoing, "leaf", height - 1)
        route_pair = lax.dynamic_index_in_dim(routes, leaf_index >> height, 0, keepdims=False)
        upper_masks = (route_pair >= PIVOT_BLOCKS).astype(jnp.float32)
        own_mask = jnp.where(child_bit == 0, upper_masks[0], upper_masks[1])
        other_mask = jnp.where(child_bit == 0, upper_masks[1], upper_masks[0])
        slab_rows = local_count * piece_rows
        pivot_slab = entries[:slab_rows].reshape(local_count, piece_rows, pivot_size)
        update_slab = jnp.zeros((local_count, piece_rows, 2 * pivot_size), jnp.float32)
        update_slab = update_slab.at[:, :, :pivot_size].set(
            entries[slab_rows:].reshape(local_count, piece_rows, pivot_size)
        )
        for contribution, column_mask in ((kept, own_mask), (received, other_mask)):
            spread = spread_columns(contribution, column_mask)
            row_upper = jnp.sum(selector * column_mask[None, :], axis=1)
            pivot_slab = pivot_slab + (1.0 - row_upper)[:, None, None] * spread[:, :, :pivot_size]
            update_slab = update_slab + row_upper[:, None, None] * spread
        piece_index = reversed_bits(leaf_index & 2**height - 1, height)
        update_pivot = update_slab[:, :, :pivot_size]
        whole_pivot = group_gather(pivot_slab, height).reshape(pivot_size, pivot_size)
        lower_factor, factor_inv = factor_inverse(whole_pivot)
        own_panel = product(update_pivot.reshape(-1, pivot_size), factor_inv.T)
        all_panel = group_gather(
            own_panel.reshape(local_count, piece_rows, pivot_size), height
        ).reshape(pivot_size, pivot_size)
        own_factor = own_rows(
            lower_factor.reshape(local_count, front_count, BLK, pivot_size),
            front_index,
            piece_index,
            piece_rows,
        ).reshape(-1, pivot_size)
        results.append(jnp.concatenate([own_factor, own_panel], axis=0))
        schur_rows = update_slab[:, :, pivot_size:].reshape(-1, pivot_size) - product(
            own_panel, all_panel.T
        )
        update = schur_rows.reshape(local_count, piece_rows, pivot_size)
    return (results[0], results[1], results[2], update.reshape(-1, pivot_size))


def solution(mesh):
    in_specs = (
        P(("leaf", "front"), None),
        P(("leaf", "front"), None),
        P(("leaf", "front"), None),
        P(("leaf", "front"), None),
        P(),
        P(),
        P(),
    )
    out_specs = (
        P(("leaf", "front"), None),
        P(("leaf", "front"), None),
        P(("leaf", "front"), None),
        P(("leaf", "front"), None),
    )
    return jax.shard_map(local, mesh=mesh, in_specs=in_specs, out_specs=out_specs, check_vma=False)
```

profile of v0, /device:TPU:0, one launch (start us, length us, event | category | flops | bytes accessed | tf_op | source)
XLA Modules:
  0.0 1209.6 jit_solution(2684180828487091180)
XLA Ops:
  20.6 48.4 %all-gather.12.cloned.1.call-done = f32[2,256,1024]{2,1,0:T(8,128)} async-done(((f32[2,64,1024]{2,1,0:T(8,128)}), f32[2,256,1024]{2,1,0:T(8,128)}) %all-gather.12.cloned.1.call-update) | async-done | bytes 2097168 | tf_op jit(solution)/shard_map/all_gather | solution.py:69
  77.2 11.7 cholesky.374
  103.9 11.7 cholesky.385
  130.8 11.7 cholesky.396
  157.4 11.9 cholesky.407
  189.0 11.9 cholesky.418
  280.3 11.9 cholesky.451
  316.9 44.8 %all-gather.8.cloned.1.call-done = f32[2,4,64,1024]{3,2,1,0:T(8,128)} async-done(((f32[2,1,64,1024]{3,2,1,0:T(8,128)}), f32[2,4,64,1024]{3,2,1,0:T(8,128)}) %all-gather.8.cloned.1.call-update) | async-done | bytes 2097168 | tf_op jit(solution)/shard_map/all_gather | solution.py:69
  385.6 26.3 %all-gather.14.cloned.1.call-done = f32[2,128,1024]{2,1,0:T(8,128)} async-done(((f32[2,32,1024]{2,1,0:T(8,128)}), f32[2,128,1024]{2,1,0:T(8,128)}) %all-gather.14.cloned.1.call-update) | async-done | bytes 1048592 | tf_op jit(solution)/shard_map/all_gather | solution.py:69
  413.4 23.5 %collective-permute-done.4 = f32[2,4,32,1024]{3,2,1,0:T(8,128)S(1)} collective-permute-done((f32[2,4,32,1024]{3,2,1,0:T(8,128)}, f32[2,4,32,1024]{3,2,1,0:T(8,128)S(1)}, u32[]{:S(2)}, u32[]{:S(2)}) %collective-permute-start.4) | collective-permute-done | bytes 1048608 | tf_op jit(solution)/shard_map/ppermute | solution.py:13
  527.8 11.9 cholesky.495
  562.5 12.1 %cholesky.506 = f32[128,128]{1,0:T(8,128)S(1)} custom-call(f32[128,128]{1,0:T(8,128)S(1)} %fusion.248), custom_call_target="Cholesky" | custom-call | tf_op jit(solution)/shard_map/jit(cholesky)/cholesky | solution.py:23
  621.0 13.2 %cholesky.528 = f32[128,128]{1,0:T(8,128)} custom-call(f32[128,128]{1,0:T(8,128)} %fusion.244), custom_call_target="Cholesky" | custom-call | tf_op jit(solution)/shard_map/jit(cholesky)/cholesky | solution.py:23
  662.3 12.1 %cholesky.539 = f32[128,128]{1,0:T(8,128)S(1)} custom-call(f32[128,128]{1,0:T(8,128)S(1)} %fusion.242), custom_call_target="Cholesky" | custom-call | tf_op jit(solution)/shard_map/jit(cholesky)/cholesky | solution.py:23
  703.7 27.9 %all-gather.10.cloned.1.call-done = f32[2,4,32,1024]{3,2,1,0:T(8,128)} async-done(((f32[2,1,32,1024]{3,2,1,0:T(8,128)}), f32[2,4,32,1024]{3,2,1,0:T(8,128)}) %all-gather.10.cloned.1.call-update) | async-done | bytes 1048592 | tf_op jit(solution)/shard_map/all_gather | solution.py:69
  733.0 23.5 %collective-permute-done.6 = f32[2,4,32,1024]{3,2,1,0:T(8,128)S(1)} collective-permute-done((f32[2,4,32,1024]{3,2,1,0:T(8,128)}, f32[2,4,32,1024]{3,2,1,0:T(8,128)S(1)}, u32[]{:S(2)}, u32[]{:S(2)}) %collective-permute-start.6) | collective-permute-done | bytes 1048608 | tf_op jit(solution)/shard_map/ppermute | solution.py:13
  773.6 15.8 %all-gather.2 = f32[2,64,1024]{2,1,0:T(8,128)S(1)} all-gather(f32[2,16,1024]{2,1,0:T(8,128)S(1)} %fusion.199), channel_id=4, replica_groups=mesh['leaf'=8,'front'=4] {'front'}, dimensions={1}, use_global_device_ids=true | all-gather | bytes 655360 | tf_op jit(solution)/shard_map/all_gather | solution.py:69
  801.9 19.6 %collective-permute-done.10 = f32[2,4,32,1024]{3,2,1,0:T(8,128)S(1)} collective-permute-done((f32[2,4,32,1024]{3,2,1,0:T(8,128)S(1)}, f32[2,4,32,1024]{3,2,1,0:T(8,128)S(1)}, u32[]{:S(2)}, u32[]{:S(2)}) %collective-permute-start.10) | collective-permute-done | bytes 1048608 | tf_op jit(solution)/shard_map/ppermute | solution.py:13
  916.4 12.1 %cholesky.583 = f32[128,128]{1,0:T(8,128)S(1)} custom-call(f32[128,128]{1,0:T(8,128)S(1)} %fusion.234), custom_call_target="Cholesky" | custom-call | tf_op jit(solution)/shard_map/jit(cholesky)/cholesky | solution.py:23
  956.5 12.7 %cholesky.594 = f32[128,128]{1,0:T(8,128)S(1)} custom-call(f32[128,128]{1,0:T(8,128)} %fusion.232), custom_call_target="Cholesky" | custom-call | tf_op jit(solution)/shard_map/jit(cholesky)/cholesky | solution.py:23
  990.5 13.2 %cholesky.605 = f32[128,128]{1,0:T(8,128)} custom-call(f32[128,128]{1,0:T(8,128)} %fusion.230), custom_call_target="Cholesky" | custom-call | tf_op jit(solution)/shard_map/jit(cholesky)/cholesky | solution.py:23
  1031.9 13.2 %cholesky.616 = f32[128,128]{1,0:T(8,128)} custom-call(f32[128,128]{1,0:T(8,128)} %fusion.228), custom_call_target="Cholesky" | custom-call | tf_op jit(solution)/shard_map/jit(cholesky)/cholesky | solution.py:23
  1075.9 12.9 %cholesky.627 = f32[128,128]{1,0:T(8,128)S(1)} custom-call(f32[128,128]{1,0:T(8,128)} %fusion.226), custom_call_target="Cholesky" | custom-call | tf_op jit(solution)/shard_map/jit(cholesky)/cholesky | solution.py:23
  1119.3 16.8 %all_gather.23 = f32[2,4,16,1024]{3,2,1,0:T(8,128)} all-gather(f32[2,1,16,1024]{3,2,1,0:T(8,128)S(1)} %bitcast.496), channel_id=1, replica_groups=mesh['leaf'=8,'front'=4] {'front'}, dimensions={1}, use_global_device_ids=true | all-gather | bytes 655360 | tf_op jit(solution)/shard_map/all_gather | solution.py:69
  (696 shorter events, 761.6 us)
Async XLA Ops:
  7.2 61.9 %all-gather.12.cloned.1.call-start = ((), (), s32[]{:S(2)}) async-start(), calls=%async_computation.2 | async-start | bytes 2621440 | tf_op jit(solution)/shard_map/all_gather | solution.py:69
  8.5 7.0 collective-permute-start
  20.6 341.1 %all-gather.8.cloned.1.call-start = ((), (), s32[]{:S(2)}) async-start(), calls=%async_computation | async-start | bytes 2621440 | tf_op jit(solution)/shard_map/all_gather | solution.py:69
  69.1 4.4 collective-permute-start.1
  188.9 85.8 %copy-start.47 = (f32[128,256]{1,0:T(8,128)S(1)}, f32[128,256]{1,0:T(8,128)}, u32[]{:S(2)}) copy-start(f32[128,256]{1,0:T(8,128)} %copy-done.46) | copy-start | bytes 393220
  188.9 85.8 %copy-start.51 = (f32[256,256]{1,0:T(8,128)S(1)}, f32[256,256]{1,0:T(8,128)}, u32[]{:S(2)}) copy-start(f32[256,256]{1,0:T(8,128)} %copy-done.50) | copy-start | bytes 786436
  316.8 95.1 %all-gather.14.cloned.1.call-start = ((), (), s32[]{:S(2)}) async-start(), calls=%async_computation.3 | async-start | bytes 1310720 | tf_op jit(solution)/shard_map/all_gather | solution.py:69
  361.6 4.4 collective-permute-start.2
  374.3 8.7 collective-permute-start.3
  385.1 346.4 %all-gather.10.cloned.1.call-start = ((), (), s32[]{:S(2)}) async-start(), calls=%async_computation.1 | async-start | bytes 1310720 | tf_op jit(solution)/shard_map/all_gather | solution.py:69
  411.9 25.0 %collective-permute-start.4 = (f32[2,4,32,1024]{3,2,1,0:T(8,128)}, f32[2,4,32,1024]{3,2,1,0:T(8,128)S(1)}, u32[]{:S(2)}, u32[]{:S(2)}) collective-permute-start(f32[2,4,32,1024]{3,2,1,0:T(8,128)} %bitcast.497), channel_id=1, source_target_pairs={{0,8},{4,12},{8,0},{12,4},{16,24},{20,28},{24,16},{28,20},{1,9},{5... | collective-permute-start | bytes 3145736 | tf_op jit(solution)/shard_map/ppermute | solution.py:13
  438.7 4.2 collective-permute-start.5
  561.4 97.0 %copy-start.44 = (f32[128,256]{1,0:T(8,128)S(1)}, f32[128,256]{1,0:T(8,128)}, u32[]{:S(2)}) copy-start(f32[128,256]{1,0:T(8,128)} %copy-done.43) | copy-start | bytes 393220
  561.4 97.0 %copy-start.53 = (f32[256,256]{1,0:T(8,128)S(1)}, f32[256,256]{1,0:T(8,128)}, u32[]{:S(2)}) copy-start(f32[256,256]{1,0:T(8,128)} %copy-done.52) | copy-start | bytes 786436
  561.4 97.0 %copy-start.58 = (f32[256,256]{1,0:T(8,128)S(1)}, f32[256,256]{1,0:T(8,128)}, u32[]{:S(2)}) copy-start(f32[256,256]{1,0:T(8,128)} %copy-done.57) | copy-start | bytes 786436
  731.5 25.0 %collective-permute-start.6 = (f32[2,4,32,1024]{3,2,1,0:T(8,128)}, f32[2,4,32,1024]{3,2,1,0:T(8,128)S(1)}, u32[]{:S(2)}, u32[]{:S(2)}) collective-permute-start(f32[2,4,32,1024]{3,2,1,0:T(8,128)} %all-gather.10.cloned.1.call-done), channel_id=1, source_target_pairs={{0,8},{4,12},{8,0},{12,4},{16,24},{20,28},{24,16},{28,20},{1,9},{5... | collective-permute-start | bytes 3145736 | tf_op jit(solution)/shard_map/ppermute | solution.py:13
  758.4 4.2 collective-permute-start.7
  767.7 5.6 collective-permute-start.8
  789.4 10.6 collective-permute-start.9
  800.1 21.4 %collective-permute-start.10 = (f32[2,4,32,1024]{3,2,1,0:T(8,128)S(1)}, f32[2,4,32,1024]{3,2,1,0:T(8,128)S(1)}, u32[]{:S(2)}, u32[]{:S(2)}) collective-permute-start(f32[2,4,32,1024]{3,2,1,0:T(8,128)S(1)} %maximum_select_fusion.10), channel_id=1, source_target_pairs={{0,8},{4,12},{8,0},{12,4},{16,24},{20,28},{24,16},{28,20},{1,9},{5... | collective-permute-start | bytes 3145736 | tf_op jit(solution)/shard_map/ppermute | solution.py:13
  821.8 4.2 collective-permute-start.11
  1136.1 13.7 %collective-permute-start.12 = (f32[2,4,16,1024]{3,2,1,0:T(8,128)}, f32[2,4,16,1024]{3,2,1,0:T(8,128)}, u32[]{:S(2)}, u32[]{:S(2)}) collective-permute-start(f32[2,4,16,1024]{3,2,1,0:T(8,128)} %all_gather.23), channel_id=1, source_target_pairs={{0,16},{4,20},{8,24},{12,28},{16,0},{20,4},{24,8},{28,12},{1,17},{... | collective-permute-start | bytes 1572872 | tf_op jit(solution)/shard_map/ppermute | solution.py:13
  1152.5 22.0 %collective-permute-start.13 = (f32[2,4,32,1024]{3,2,1,0:T(8,128)}, f32[2,4,32,1024]{3,2,1,0:T(8,128)}, u32[]{:S(2)}, u32[]{:S(2)}) collective-permute-start(f32[2,4,32,1024]{3,2,1,0:T(8,128)} %maximum_select_fusion.11), channel_id=1, source_target_pairs={{0,8},{4,12},{8,0},{12,4},{16,24},{20,28},{24,16},{28,20},{1,9},{5... | collective-permute-start | bytes 3145736 | tf_op jit(solution)/shard_map/ppermute | solution.py:13
  1178.7 15.2 %collective-permute-start.14 = (f32[2,4,64,1024]{3,2,1,0:T(8,128)}, f32[2,4,64,1024]{3,2,1,0:T(8,128)}, u32[]{:S(2)}, u32[]{:S(2)}) collective-permute-start(f32[2,4,64,1024]{3,2,1,0:T(8,128)} %maximum_select_fusion.9), channel_id=1, source_target_pairs={{0,4},{4,0},{8,12},{12,8},{16,20},{20,16},{24,28},{28,24},{1,5},{5... | collective-permute-start | bytes 6291464 | tf_op jit(solution)/shard_map/ppermute | solution.py:13
  (106 other events, 1867.5 us)
Sparse Core Ops, SparseCore 0:
  20.7 48.3 all-gather.11
  316.9 44.6 all-gather.7
  385.2 26.6 all-gather.13
  703.8 27.7 all-gather.9
where the time goes:
time: 1220 us; the launch traced here: 1210 us
  other arithmetic  671 us (55%)
  waiting for transfers between devices  255 us (21%)
  matrix products  148 us (12%)
  local copies, waits for them, and re-layouts  73.1 us (6%)
  blocking collectives  32.6 us (3%)
  between operations  17.1 us (1%)
  starting transfers between devices  13.9 us (1%)
    another operation x72, other arithmetic, factor_inverse(): lower_factor = jnp.linalg.cholesky(matrix)  308 us
    another operation x48, other arithmetic, factor_inverse(): jax.scipy.linalg.solve_triangular(lower_factor, identity, lower=True)  277 us
    all_gather x4, waiting for transfers between devices, group_gather(): gathered = lax.all_gather(pieces[:, None], 'front', axis=1, tiled=True)  147 us
    dot_general x90, matrix products, product(): jnp.dot(left, right, precision=lax.Precision.HIGHEST, preferred_element_t...  136 us
    ppermute x15, waiting for transfers between devices, partner_2(): return lax.ppermute(value, axis, pairs)  107 us
    all_gather x2, blocking collectives, group_gather(): gathered = lax.all_gather(pieces[:, None], 'front', axis=1, tiled=True)  32.6 us
  transfers between devices with their start and end apart: 19, of which 16 were waited for; matrix products, arithmetic and copies ran while one was open for 4% of the time, Pallas kernels for 0%

commit v1 on v0

--- a/solution.py
+++ b/solution.py
@@ -1,10 +1,121 @@
 import jax
 import jax.numpy as jnp
 from jax import lax
+from jax.experimental import pallas as pl
+from jax.experimental.pallas import tpu as pltpu
 from jax.sharding import PartitionSpec as P
 
 BLK = 128
 PIVOT_BLOCKS = 8
+SUB = 8
+
+
+def split_parts(value):
+    high = value.astype(jnp.bfloat16)
+    low = (value - high.astype(jnp.float32)).astype(jnp.bfloat16)
+    return high, low
+
+
+def product_3(left, right, transposed=False):
+    dims = (((1,), (1 if transposed else 0,)), ((), ()))
+    left_high, left_low = split_parts(left)
+    right_high, right_low = split_parts(right)
+
+    def one(first, second):
+        return lax.dot_general(first, second, dims, preferred_element_type=jnp.float32)
+
+    return one(left_high, right_high) + (one(left_high, right_low) + one(left_low, right_high))
+
+
+def invert_block(block, inverse_ref):
+    count = BLK // SUB
+    shape = (SUB, BLK)
+    rows = [block[SUB * m : SUB * m + SUB] for m in range(count)]
+    lane = lax.broadcasted_iota(jnp.int32, shape, 1)
+    sublane = lax.broadcasted_iota(jnp.int32, shape, 0)
+    unit = [(lane == sublane + SUB * m).astype(jnp.float32) for m in range(count)]
+    for k in range(count):
+        base = SUB * k
+        cols = [jnp.broadcast_to(rows[k][:, base + j : base + j + 1], shape) for j in range(SUB)]
+        d = [[jnp.broadcast_to(cols[j][i : i + 1], shape) for j in range(i + 1)] for i in range(SUB)]
+        ya = [jnp.broadcast_to(rows[k][j : j + 1], shape) for j in range(SUB)]
+        ye = [jnp.broadcast_to(unit[k][j : j + 1], shape) for j in range(SUB)]
+        f = [[None] * SUB for _ in range(SUB)]
+        reciprocal = [None] * SUB
+        for c in range(SUB):
+            reciprocal[c] = 1.0 / d[c][c]
+            for i in range(c + 1, SUB):
+                f[i][c] = d[i][c] * reciprocal[c]
+            for i in range(c + 1, SUB):
+                for j in range(c + 1, i + 1):
+                    d[i][j] = d[i][j] - (d[i][c] * d[j][c]) * reciprocal[c]
+            for i in range(c + 1, SUB):
+                ya[i] = ya[i] - f[i][c] * ya[c]
+                ye[i] = ye[i] - f[i][c] * ye[c]
+            inverse_ref[base + c : base + c + 1, :] = (lax.rsqrt(d[c][c]) * ye[c])[0:1]
+        if k == count - 1:
+            break
+        za = [y * r for y, r in zip(ya, reciprocal)]
+        ze = [y * r for y, r in zip(ye, reciprocal)]
+        for i in reversed(range(SUB)):
+            for c in range(i):
+                za[c] = za[c] - f[i][c] * za[i]
+                ze[c] = ze[c] - f[i][c] * ze[i]
+        for m in range(k + 1, count):
+            col = [jnp.broadcast_to(rows[m][:, base + j : base + j + 1], shape) for j in range(SUB)]
+            pa = [c * z for c, z in zip(col, za)]
+            pe = [c * z for c, z in zip(col, ze)]
+            while len(pa) > 1:
+                pa = [x + y for x, y in zip(pa[::2], pa[1::2])]
+                pe = [x + y for x, y in zip(pe[::2], pe[1::2])]
+            rows[m] = rows[m] - pa[0]
+            unit[m] = unit[m] - pe[0]
+
+
+def factor_kernel(matrix_ref, factor_ref, inverse_ref, work_ref, block_ref):
+    size = matrix_ref.shape[0]
+    work_ref[:, :size] = matrix_ref[...]
+    row = lax.broadcasted_iota(jnp.int32, (size, size), 0)
+    column = lax.broadcasted_iota(jnp.int32, (size, size), 1)
+    work_ref[:, size:] = (row == column).astype(jnp.float32)
+    row = lax.broadcasted_iota(jnp.int32, (size, BLK), 0)
+    column = lax.broadcasted_iota(jnp.int32, (size, BLK), 1)
+
+    def step(index, carry):
+        base = pl.multiple_of(index * BLK, BLK)
+        invert_block(work_ref[pl.ds(base, BLK), pl.ds(base, BLK)], block_ref)
+        block = block_ref[...]
+        below = product_3(work_ref[:, pl.ds(base, BLK)], block, transposed=True)
+        right = product_3(block, work_ref[pl.ds(base, BLK), :])
+        below = jnp.where(row >= column + base, below, 0.0)
+        factor_ref[:, pl.ds(base, BLK)] = below
+        inverse_ref[pl.ds(base, BLK), :] = right[:, size:]
+        below = jnp.where(row >= base + BLK, below, 0.0)
+        work_ref[...] = work_ref[...] - product_3(below, right)
+        return carry
+
+    lax.fori_loop(0, size // BLK, step, 0)
+
+
+def factor_inverse(matrix):
+    size = matrix.shape[0]
+    vmem = pl.BlockSpec(memory_space=pltpu.VMEM)
+    whole = jax.ShapeDtypeStruct((size, size), jnp.float32)
+    return pl.pallas_call(
+        factor_kernel,
+        out_shape=[whole, whole],
+        in_specs=[vmem],
+        out_specs=[vmem, vmem],
+        scratch_shapes=[
+            pltpu.VMEM((size, 2 * size), jnp.float32),
+            pltpu.VMEM((BLK, BLK), jnp.float32),
+        ],
+        compiler_params=pltpu.CompilerParams(vmem_limit_bytes=48 * 2**20),
+        cost_estimate=pl.CostEstimate(
+            flops=60_000_000_000 * size // 1024, bytes_accessed=12 * size * size, transcendentals=0
+        ),
+        name="factor_inverse",
+    )(matrix)
 
 
 def partner_2(value, axis, stride):
@@ -14,39 +125,7 @@
 
 
 def product(left, right):
-    return jnp.dot(left, right, precision=lax.Precision.HIGHEST, preferred_element_type=jnp.float32)
-
-
-def factor_inverse(matrix):
-    order_size = matrix.shape[0]
-    if order_size <= 128 or order_size % 2 != 0:
-        lower_factor = jnp.linalg.cholesky(matrix)
-        identity = jnp.eye(order_size, dtype=jnp.float32)
-        inverse = jax.scipy.linalg.solve_triangular(lower_factor, identity, lower=True)
-        return (lower_factor, inverse)
-    half = order_size // 2
-    first_factor, first_inverse = factor_inverse(matrix[:half, :half])
-    coupling = product(matrix[half:, :half], first_inverse.T)
-    second_factor, second_inverse = factor_inverse(
-        matrix[half:, half:] - product(coupling, coupling.T)
-    )
-    corner = -product(second_inverse, product(coupling, first_inverse))
-    zeros_block = jnp.zeros((half, half), jnp.float32)
-    lower_factor = jnp.concatenate(
-        [
-            jnp.concatenate([first_factor, zeros_block], 1),
-            jnp.concatenate([coupling, second_factor], 1),
-        ],
-        0,
-    )
-    inverse = jnp.concatenate(
-        [
-            jnp.concatenate([first_inverse, zeros_block], 1),
-            jnp.concatenate([corner, second_inverse], 1),
-        ],
-        0,
-    )
-    return (lower_factor, inverse)
+    return jnp.dot(left, right, precision=lax.Precision.HIGH, preferred_element_type=jnp.float32)
 
 
 def reversed_bits(number, bit_count):
@@ -56,21 +135,21 @@
     return result
 
 
-def join_pieces(mine, theirs, bit_index, axis_index):
+def join_pieces(mine, theirs, bit_index):
     upper_bit = lax.axis_index("leaf") >> bit_index & 1
     return jnp.where(
         upper_bit == 0,
-        jnp.concatenate([mine, theirs], axis_index),
-        jnp.concatenate([theirs, mine], axis_index),
+        jnp.concatenate([mine, theirs], 1),
+        jnp.concatenate([theirs, mine], 1),
     )
 
 
 def group_gather(pieces, height):
-    gathered = lax.all_gather(pieces[:, None], "front", axis=1, tiled=True)
+    gathered = lax.all_gather(pieces, "front", axis=0, tiled=False)
     for bit_index in reversed(range(height)):
         partner = partner_2(gathered, "leaf", bit_index)
-        gathered = join_pieces(gathered, partner, bit_index, 2)
-    return gathered
+        gathered = join_pieces(gathered, partner, bit_index)
+    return gathered.reshape(-1, pieces.shape[-1])
 
 
 def spread_columns(rows_in, upper_mask):
@@ -85,6 +164,16 @@
 def own_rows(whole, front_index, piece_index, piece_rows):
     chosen = lax.dynamic_index_in_dim(whole, front_index, 1, keepdims=False)
     return lax.dynamic_slice_in_dim(chosen, piece_index * piece_rows, piece_rows, 1)
+
+
+def solve_panel(rows, chunk, factors, inverses):
+    panels = []
+    for index, inverse in enumerate(inverses):
+        part = rows[:, index * chunk : (index + 1) * chunk]
+        for previous in range(index):
+            part = part - product(panels[previous], factors[index][previous].T)
+        panels.append(product(part, inverse.T))
+    return jnp.concatenate(panels, axis=1)
 
 
 def local(
@@ -98,6 +187,7 @@
 ):
     front_count = lax.axis_size("front")
     local_count = PIVOT_BLOCKS // front_count
+    chunk = front_count * BLK
     leaf_index = lax.axis_index("leaf")
     front_index = lax.axis_index("front")
     pivot_size = leaf_contrib.shape[1]
@@ -136,12 +226,35 @@
             update_slab = update_slab + row_upper[:, None, None] * spread
         piece_index = reversed_bits(leaf_index & 2**height - 1, height)
         update_pivot = update_slab[:, :, :pivot_size]
-        whole_pivot = group_gather(pivot_slab, height).reshape(pivot_size, pivot_size)
-        lower_factor, factor_inv = factor_inverse(whole_pivot)
-        own_panel = product(update_pivot.reshape(-1, pivot_size), factor_inv.T)
-        all_panel = group_gather(
-            own_panel.reshape(local_count, piece_rows, pivot_size), height
-        ).reshape(pivot_size, pivot_size)
+        pivot_rows = [
+            group_gather(pivot_slab[t, :, : (t + 1) * chunk], height) for t in range(local_count)
+        ]
+        update_rows = [group_gather(update_pivot[t], height) for t in range(local_count)]
+        factors, inverses = [], []
+        for t in range(local_count):
+            row = []
+            for s in range(t):
+                part = pivot_rows[t][:, s * chunk : (s + 1) * chunk]
+                for r in range(s):
+                    part = part - product(row[r], factors[s][r].T)
+                row.append(product(part, inverses[s].T))
+            part = pivot_rows[t][:, t * chunk :]
+            for s in range(t):
+                part = part - product(row[s], row[s].T)
+            factor, inverse = factor_inverse(part)
+            row.append(factor)
+            factors.append(row)
+            inverses.append(inverse)
+        own_panel = solve_panel(update_pivot.reshape(-1, pivot_size), chunk, factors, inverses)
+        all_panel = solve_panel(jnp.concatenate(update_rows, 0), chunk, factors, inverses)
+        lower_factor = jnp.stack(
+            [
+                jnp.concatenate(
+                    row + [jnp.zeros((chunk, chunk), jnp.float32)] * (local_count - 1 - t), axis=1
+                )
+                for t, row in enumerate(factors)
+            ]
+        )
         own_factor = own_rows(
             lower_factor.reshape(local_count, front_count, BLK, pivot_size),
             front_index,
@@ -157,19 +270,11 @@
 
 
 def solution(mesh):
-    in_specs = (
-        P(("leaf", "front"), None),
-        P(("leaf", "front"), None),
-        P(("leaf", "front"), None),
-        P(("leaf", "front"), None),
-        P(),
-        P(),
-        P(),
-    )
-    out_specs = (
-        P(("leaf", "front"), None),
-        P(("leaf", "front"), None),
-        P(("leaf", "front"), None),
-        P(("leaf", "front"), None),
-    )
-    return jax.shard_map(local, mesh=mesh, in_specs=in_specs, out_specs=out_specs, check_vma=False)
+    spec = P(("leaf", "front"), None)
+    return jax.shard_map(
+        local,
+        mesh=mesh,
+        in_specs=(spec, spec, spec, spec, P(), P(), P()),
+        out_specs=(spec, spec, spec, spec),
+        check_vma=False,
+    )

time: 1220 us -> 517 us (0.42)
  other arithmetic: 671 us -> 36.1 us
  waiting for transfers between devices: 255 us -> 75.5 us
  Pallas kernels: 0 us -> 175 us
  matrix products: 148 us -> 33.1 us
  blocking collectives: 32.6 us -> 138 us
  local copies, waits for them, and re-layouts: 73.1 us -> 26.5 us
    another operation x120 -> x3, other arithmetic: 585 us -> 0.1 us  [local(): jnp.stack([jnp.concatenate(row + [jnp.zeros((chunk, chunk), jnp.float32)]...]
    pallas_call x0 -> x6, Pallas kernels: none -> 175 us  [factor_inverse(): pl.pallas_call(factor_kernel, out_shape=[whole, whole], in_specs=[vmem],...]
    all_gather x4 -> x3, waiting for transfers between devices: 147 us -> 36.9 us  [group_gather(): gathered = lax.all_gather(pieces, 'front', axis=0, tiled=False)]
    all_gather x2 -> x9, blocking collectives: 32.6 us -> 138 us  [group_gather(): gathered = lax.all_gather(pieces, 'front', axis=0, tiled=False)]
    dot_general x90 -> x27, matrix products: 136 us -> 33.1 us  [product(): jnp.dot(left, right, precision=lax.Precision.HIGH, preferred_element_type...]
    ppermute x15 -> x27, waiting for transfers between devices: 107 us -> 38.5 us  [partner_2(): return lax.ppermute(value, axis, pairs)]
    concatenate x21 -> x3, other arithmetic: 29.7 us -> 0.41 us  [local(): jnp.concatenate(row + [jnp.zeros((chunk, chunk), jnp.float32)] * (local_c...]
    slice x30 -> x12, local copies, waits for them, and re-layouts: 20 us -> 4.25 us  [the longest x3 2.63 us: local(): entries[slab_rows:].reshape(local_count, piece_rows, pivot_size)]
  transfers between devices with their start and end apart: 19 -> 30, of which waited for: 16 -> 10; matrix products, arithmetic and copies ran while one was open for 4% -> 9% of each run, Pallas kernels for 0% -> 34%
where the time goes in v1:
time: 517 us; the launch traced here: 514 us
  Pallas kernels  175 us (34%)
  blocking collectives  138 us (27%)
  waiting for transfers between devices  75.5 us (15%)
  other arithmetic  36.1 us (7%)
  matrix products  33.1 us (6%)
  local copies, waits for them, and re-layouts  26.5 us (5%)
  between operations  15.2 us (3%)
  starting transfers between devices  14.4 us (3%)
    pallas_call x6, Pallas kernels, factor_inverse(): pl.pallas_call(factor_kernel, out_shape=[whole, whole], in_specs=[vmem],...  175 us
    all_gather x9, blocking collectives, group_gather(): gathered = lax.all_gather(pieces, 'front', axis=0, tiled=False)  138 us
    ppermute x27, waiting for transfers between devices, partner_2(): return lax.ppermute(value, axis, pairs)  38.5 us
    all_gather x3, waiting for transfers between devices, group_gather(): gathered = lax.all_gather(pieces, 'front', axis=0, tiled=False)  36.9 us
    dot_general x27, matrix products, product(): jnp.dot(left, right, precision=lax.Precision.HIGH, preferred_element_type...  33.1 us
    select_n x24, other arithmetic, join_pieces(): jnp.where(upper_bit == 0, jnp.concatenate([mine, theirs], 1), jnp.concate...  23.2 us
    ppermute x27, starting transfers between devices, partner_2(): return lax.ppermute(value, axis, pairs)  14.3 us
  transfers between devices with their start and end apart: 30, of which 10 were waited for; matrix products, arithmetic and copies ran while one was open for 9% of the time, Pallas kernels for 34%

profile of v1, /device:TPU:0, one launch (start us, length us, event | category | flops | bytes accessed | tf_op | source)
XLA Modules:
  0.0 513.9 jit_solution(17011075769415509732)
XLA Ops:
  19.2 22.6 %all_gather.36 = f32[4,64,512]{2,1,0:T(8,128)S(1)} all-gather(f32[1,64,512]{2,1,0:T(8,128)S(1)} %slice.328), channel_id=1, replica_groups=mesh['leaf'=8,'front'=4] {'front'}, dimensions={0}, use_global_device_ids=true | all-gather | bytes 655360 | tf_op jit(solution)/shard_map/all_gather | solution.py:148
  44.3 7.9 %all-gather.4.cloned.1.call-done = f32[4,64,1024]{2,1,0:T(8,128)} async-done(((f32[1,64,1024]{2,1,0:T(8,128)}), f32[4,64,1024]{2,1,0:T(8,128)}) %all-gather.4.cloned.1.call-update) | async-done | bytes 1048592 | tf_op jit(solution)/shard_map/all_gather | solution.py:148
  52.2 27.5 %factor_inverse.6 = (f32[512,512]{1,0:T(8,128)S(1)}, f32[512,512]{1,0:T(8,128)S(1)}) custom-call(f32[512,512]{1,0:T(8,128)S(1)} %bitcast.143), custom_call_target="tpu_custom_call" | custom-call | flops 30000001024 | bytes 3145728 | tf_op jit(solution)/shard_map/factor_inverse/pallas_call | solution.py:104
  82.5 29.0 %all-gather.8.cloned.1.call-done = f32[4,64,1024]{2,1,0:T(8,128)} async-done(((f32[1,64,1024]{2,1,0:T(8,128)}), f32[4,64,1024]{2,1,0:T(8,128)}) %all-gather.8.cloned.1.call-update) | async-done | bytes 1048592 | tf_op jit(solution)/shard_map/all_gather | solution.py:148
  115.6 27.7 %factor_inverse.7 = (f32[512,512]{1,0:T(8,128)S(1)}, f32[512,512]{1,0:T(8,128)S(1)}) custom-call(f32[512,512]{1,0:T(8,128)S(1)} %slice_subtract_fusion.2.matrix_ref), custom_call_target="tpu_custom_call" | custom-call | flops 30000001024 | bytes 3145728 | tf_op jit(solution)/shard_map/factor_inverse/pallas_call | solution.py:104
  145.9 3.0 maximum_select_fusion.1
  170.3 14.0 %all_gather.40 = f32[4,32,512]{2,1,0:T(8,128)S(1)} all-gather(f32[1,32,512]{2,1,0:T(8,128)S(1)} %slice.344), channel_id=1, replica_groups=mesh['leaf'=8,'front'=4] {'front'}, dimensions={0}, use_global_device_ids=true | all-gather | bytes 327680 | tf_op jit(solution)/shard_map/all_gather | solution.py:148
  185.9 15.7 %all_gather.41 = f32[4,32,1024]{2,1,0:T(8,128)S(1)} all-gather(f32[1,32,1024]{2,1,0:T(8,128)S(1)} %slice.345), channel_id=1, replica_groups=mesh['leaf'=8,'front'=4] {'front'}, dimensions={0}, use_global_device_ids=true | all-gather | bytes 655360 | tf_op jit(solution)/shard_map/all_gather | solution.py:148
  201.6 15.2 %all_gather.42 = f32[4,32,1024]{2,1,0:T(8,128)S(1)} all-gather(f32[1,32,1024]{2,1,0:T(8,128)S(1)} %get-tuple-element.91), channel_id=1, replica_groups=mesh['leaf'=8,'front'=4] {'front'}, dimensions={0}, use_global_device_ids=true | all-gather | bytes 655360 | tf_op jit(solution)/shard_map/all_gather | solution.py:148
  218.7 14.9 %all_gather.43 = f32[4,32,1024]{2,1,0:T(8,128)S(1)} all-gather(f32[1,32,1024]{2,1,0:T(8,128)S(1)} %get-tuple-element.90), channel_id=1, replica_groups=mesh['leaf'=8,'front'=4] {'front'}, dimensions={0}, use_global_device_ids=true | all-gather | bytes 655360 | tf_op jit(solution)/shard_map/all_gather | solution.py:148
  236.3 6.5 %collective-permute-done.12 = f32[4,32,1024]{2,1,0:T(8,128)S(1)} collective-permute-done((f32[4,32,1024]{2,1,0:T(8,128)S(1)}, f32[4,32,1024]{2,1,0:T(8,128)S(1)}, u32[]{:S(2)}, u32[]{:S(2)}) %collective-permute-start.12) | collective-permute-done | bytes 524320 | tf_op jit(solution)/shard_map/ppermute | solution.py:124
  244.0 36.8 %factor_inverse.8 = (f32[512,512]{1,0:T(8,128)S(1)}, f32[512,512]{1,0:T(8,128)S(1)}) custom-call(f32[512,512]{1,0:T(8,128)S(1)} %bitcast.144), custom_call_target="tpu_custom_call" | custom-call | flops 30000001024 | bytes 3145728 | tf_op jit(solution)/shard_map/factor_inverse/pallas_call | solution.py:104
  285.4 27.9 %factor_inverse.9 = (f32[512,512]{1,0:T(8,128)S(1)}, f32[512,512]{1,0:T(8,128)S(1)}) custom-call(f32[512,512]{1,0:T(8,128)S(1)} %slice_subtract_fusion.1.matrix_ref), custom_call_target="tpu_custom_call" | custom-call | flops 30000001024 | bytes 3145728 | tf_op jit(solution)/shard_map/factor_inverse/pallas_call | solution.py:104
  335.9 13.4 %all_gather.44 = f32[4,16,512]{2,1,0:T(8,128)S(1)} all-gather(f32[1,16,512]{2,1,0:T(8,128)S(1)} %slice.360), channel_id=1, replica_groups=mesh['leaf'=8,'front'=4] {'front'}, dimensions={0}, use_global_device_ids=true | all-gather | bytes 163840 | tf_op jit(solution)/shard_map/all_gather | solution.py:148
  350.3 14.6 %all_gather.45 = f32[4,16,1024]{2,1,0:T(8,128)S(1)} all-gather(f32[1,16,1024]{2,1,0:T(8,128)S(1)} %slice.361), channel_id=1, replica_groups=mesh['leaf'=8,'front'=4] {'front'}, dimensions={0}, use_global_device_ids=true | all-gather | bytes 327680 | tf_op jit(solution)/shard_map/all_gather | solution.py:148
  365.3 13.8 %all_gather.46 = f32[4,16,1024]{2,1,0:T(8,128)S(1)} all-gather(f32[1,16,1024]{2,1,0:T(8,128)S(1)} %get-tuple-element.103), channel_id=1, replica_groups=mesh['leaf'=8,'front'=4] {'front'}, dimensions={0}, use_global_device_ids=true | all-gather | bytes 327680 | tf_op jit(solution)/shard_map/all_gather | solution.py:148
  381.0 13.9 %all_gather.47 = f32[4,16,1024]{2,1,0:T(8,128)S(1)} all-gather(f32[1,16,1024]{2,1,0:T(8,128)S(1)} %get-tuple-element.102), channel_id=1, replica_groups=mesh['leaf'=8,'front'=4] {'front'}, dimensions={0}, use_global_device_ids=true | all-gather | bytes 327680 | tf_op jit(solution)/shard_map/all_gather | solution.py:148
  397.8 3.5 collective-permute-done.24
  404.4 11.1 %collective-permute-done.19 = f32[4,32,1024]{2,1,0:T(8,128)S(1)} collective-permute-done((f32[4,32,1024]{2,1,0:T(8,128)S(1)}, f32[4,32,1024]{2,1,0:T(8,128)S(1)}, u32[]{:S(2)}, u32[]{:S(2)}) %collective-permute-start.19) | collective-permute-done | bytes 524320 | tf_op jit(solution)/shard_map/ppermute | solution.py:124
  415.7 5.6 %collective-permute-done.22 = f32[4,32,1024]{2,1,0:T(8,128)S(1)} collective-permute-done((f32[4,32,1024]{2,1,0:T(8,128)S(1)}, f32[4,32,1024]{2,1,0:T(8,128)S(1)}, u32[]{:S(2)}, u32[]{:S(2)}) %collective-permute-start.22) | collective-permute-done | bytes 524320 | tf_op jit(solution)/shard_map/ppermute | solution.py:124
  422.4 4.5 collective-permute-done.25
  428.1 27.6 %factor_inverse.10 = (f32[512,512]{1,0:T(8,128)S(1)}, f32[512,512]{1,0:T(8,128)S(1)}) custom-call(f32[512,512]{1,0:T(8,128)S(1)} %bitcast.145), custom_call_target="tpu_custom_call" | custom-call | flops 30000001024 | bytes 3145728 | tf_op jit(solution)/shard_map/factor_inverse/pallas_call | solution.py:104
  460.3 27.7 %factor_inverse.11 = (f32[512,512]{1,0:T(8,128)S(1)}, f32[512,512]{1,0:T(8,128)S(1)}) custom-call(f32[512,512]{1,0:T(8,128)S(1)} %slice_subtract_fusion.matrix_ref), custom_call_target="tpu_custom_call" | custom-call | flops 30000001024 | bytes 3145728 | tf_op jit(solution)/shard_map/factor_inverse/pallas_call | solution.py:104
  493.7 2.8 maximum_select_fusion.8
  (268 shorter events, 111.6 us)
Async XLA Ops:
  7.2 45.0 %all-gather.4.cloned.1.call-start = ((), (), s32[]{:S(2)}) async-start(), calls=%async_computation | async-start | bytes 1310720 | tf_op jit(solution)/shard_map/all_gather | solution.py:148
  16.9 65.1 %all-gather.6.cloned.1.call-start = ((), (), s32[]{:S(2)}) async-start(), calls=%async_computation.1 | async-start | bytes 1310720 | tf_op jit(solution)/shard_map/all_gather | solution.py:148
  18.4 93.2 %all-gather.8.cloned.1.call-start = ((), (), s32[]{:S(2)}) async-start(), calls=%async_computation.2 | async-start | bytes 1310720 | tf_op jit(solution)/shard_map/all_gather | solution.py:148
  52.2 59.4 %collective-permute-start.2 = (f32[4,64,1024]{2,1,0:T(8,128)}, f32[4,64,1024]{2,1,0:T(8,128)}, u32[]{:S(2)}, u32[]{:S(2)}) collective-permute-start(f32[4,64,1024]{2,1,0:T(8,128)} %all-gather.4.cloned.1.call-done), channel_id=1, source_target_pairs={{0,4},{4,0},{8,12},{12,8},{16,20},{20,16},{24,28},{28,24},{1,5},{5... | collective-permute-start | bytes 3145736 | tf_op jit(solution)/shard_map/ppermute | solution.py:124
  82.0 63.9 %collective-permute-start.3 = (f32[4,64,1024]{2,1,0:T(8,128)}, f32[4,64,1024]{2,1,0:T(8,128)}, u32[]{:S(2)}, u32[]{:S(2)}) collective-permute-start(f32[4,64,1024]{2,1,0:T(8,128)} %all-gather.6.cloned.1.call-done), channel_id=1, source_target_pairs={{0,4},{4,0},{8,12},{12,8},{16,20},{20,16},{24,28},{28,24},{1,5},{5... | collective-permute-start | bytes 3145736 | tf_op jit(solution)/shard_map/ppermute | solution.py:124
  111.5 37.8 %collective-permute-start.4 = (f32[4,64,1024]{2,1,0:T(8,128)}, f32[4,64,1024]{2,1,0:T(8,128)}, u32[]{:S(2)}, u32[]{:S(2)}) collective-permute-start(f32[4,64,1024]{2,1,0:T(8,128)} %all-gather.8.cloned.1.call-done), channel_id=1, source_target_pairs={{0,4},{4,0},{8,12},{12,8},{16,20},{20,16},{24,28},{28,24},{1,5},{5... | collective-permute-start | bytes 3145736 | tf_op jit(solution)/shard_map/ppermute | solution.py:124
  184.3 49.4 %collective-permute-start.6 = (f32[4,32,512]{2,1,0:T(8,128)S(1)}, f32[4,32,512]{2,1,0:T(8,128)S(1)}, u32[]{:S(2)}, u32[]{:S(2)}) collective-permute-start(f32[4,32,512]{2,1,0:T(8,128)S(1)} %all_gather.40), channel_id=1, source_target_pairs={{0,8},{4,12},{8,0},{12,4},{16,24},{20,28},{24,16},{28,20},{1,9},{5... | collective-permute-start | bytes 786440 | tf_op jit(solution)/shard_map/ppermute | solution.py:124
  201.5 33.0 %collective-permute-start.8 = (f32[4,32,1024]{2,1,0:T(8,128)S(1)}, f32[4,32,1024]{2,1,0:T(8,128)S(1)}, u32[]{:S(2)}, u32[]{:S(2)}) collective-permute-start(f32[4,32,1024]{2,1,0:T(8,128)S(1)} %all_gather.41), channel_id=1, source_target_pairs={{0,8},{4,12},{8,0},{12,4},{16,24},{20,28},{24,16},{28,20},{1,9},{5... | collective-permute-start | bytes 1572872 | tf_op jit(solution)/shard_map/ppermute | solution.py:124
  216.7 18.5 %collective-permute-start.10 = (f32[4,32,1024]{2,1,0:T(8,128)S(1)}, f32[4,32,1024]{2,1,0:T(8,128)S(1)}, u32[]{:S(2)}, u32[]{:S(2)}) collective-permute-start(f32[4,32,1024]{2,1,0:T(8,128)S(1)} %all_gather.42), channel_id=1, source_target_pairs={{0,8},{4,12},{8,0},{12,4},{16,24},{20,28},{24,16},{28,20},{1,9},{5... | collective-permute-start | bytes 1572872 | tf_op jit(solution)/shard_map/ppermute | solution.py:124
  233.7 10.2 %collective-permute-start.7 = (f32[4,64,512]{2,1,0:T(8,128)S(1)}, f32[4,64,512]{2,1,0:T(8,128)S(1)}, u32[]{:S(2)}, u32[]{:S(2)}) collective-permute-start(f32[4,64,512]{2,1,0:T(8,128)S(1)} %maximum_select_fusion.18), channel_id=1, source_target_pairs={{0,4},{4,0},{8,12},{12,8},{16,20},{20,16},{24,28},{28,24},{1,5},{5... | collective-permute-start | bytes 1572872 | tf_op jit(solution)/shard_map/ppermute | solution.py:124
  234.6 48.5 %collective-permute-start.9 = (f32[4,64,1024]{2,1,0:T(8,128)S(1)}, f32[4,64,1024]{2,1,0:T(8,128)S(1)}, u32[]{:S(2)}, u32[]{:S(2)}) collective-permute-start(f32[4,64,1024]{2,1,0:T(8,128)S(1)} %maximum_select_fusion.11), channel_id=1, source_target_pairs={{0,4},{4,0},{8,12},{12,8},{16,20},{20,16},{24,28},{28,24},{1,5},{5... | collective-permute-start | bytes 3145736 | tf_op jit(solution)/shard_map/ppermute | solution.py:124
  236.3 79.6 %collective-permute-start.11 = (f32[4,64,1024]{2,1,0:T(8,128)}, f32[4,64,1024]{2,1,0:T(8,128)}, u32[]{:S(2)}, u32[]{:S(2)}) collective-permute-start(f32[4,64,1024]{2,1,0:T(8,128)} %maximum_select_fusion.12), channel_id=1, source_target_pairs={{0,4},{4,0},{8,12},{12,8},{16,20},{20,16},{24,28},{28,24},{1,5},{5... | collective-permute-start | bytes 3145736 | tf_op jit(solution)/shard_map/ppermute | solution.py:124
  243.9 75.1 %collective-permute-start.13 = (f32[4,64,1024]{2,1,0:T(8,128)}, f32[4,64,1024]{2,1,0:T(8,128)}, u32[]{:S(2)}, u32[]{:S(2)}) collective-permute-start(f32[4,64,1024]{2,1,0:T(8,128)} %maximum_select_fusion.13), channel_id=1, source_target_pairs={{0,4},{4,0},{8,12},{12,8},{16,20},{20,16},{24,28},{28,24},{1,5},{5... | collective-permute-start | bytes 3145736 | tf_op jit(solution)/shard_map/ppermute | solution.py:124
  349.2 45.7 %collective-permute-start.15 = (f32[4,16,512]{2,1,0:T(8,128)S(1)}, f32[4,16,512]{2,1,0:T(8,128)S(1)}, u32[]{:S(2)}, u32[]{:S(2)}) collective-permute-start(f32[4,16,512]{2,1,0:T(8,128)S(1)} %all_gather.44), channel_id=1, source_target_pairs={{0,16},{4,20},{8,24},{12,28},{16,0},{20,4},{24,8},{28,12},{1,17},{... | collective-permute-start | bytes 393224 | tf_op jit(solution)/shard_map/ppermute | solution.py:124
  365.0 30.6 %collective-permute-start.18 = (f32[4,16,1024]{2,1,0:T(8,128)S(1)}, f32[4,16,1024]{2,1,0:T(8,128)S(1)}, u32[]{:S(2)}, u32[]{:S(2)}) collective-permute-start(f32[4,16,1024]{2,1,0:T(8,128)S(1)} %all_gather.45), channel_id=1, source_target_pairs={{0,16},{4,20},{8,24},{12,28},{16,0},{20,4},{24,8},{28,12},{1,17},{... | collective-permute-start | bytes 786440 | tf_op jit(solution)/shard_map/ppermute | solution.py:124
  379.1 18.1 %collective-permute-start.21 = (f32[4,16,1024]{2,1,0:T(8,128)S(1)}, f32[4,16,1024]{2,1,0:T(8,128)S(1)}, u32[]{:S(2)}, u32[]{:S(2)}) collective-permute-start(f32[4,16,1024]{2,1,0:T(8,128)S(1)} %all_gather.46), channel_id=1, source_target_pairs={{0,16},{4,20},{8,24},{12,28},{16,0},{20,4},{24,8},{28,12},{1,17},{... | collective-permute-start | bytes 786440 | tf_op jit(solution)/shard_map/ppermute | solution.py:124
  395.0 9.3 %collective-permute-start.16 = (f32[4,32,512]{2,1,0:T(8,128)S(1)}, f32[4,32,512]{2,1,0:T(8,128)S(1)}, u32[]{:S(2)}, u32[]{:S(2)}) collective-permute-start(f32[4,32,512]{2,1,0:T(8,128)S(1)} %maximum_select_fusion.23), channel_id=1, source_target_pairs={{0,8},{4,12},{8,0},{12,4},{16,24},{20,28},{24,16},{28,20},{1,9},{5... | collective-permute-start | bytes 786440 | tf_op jit(solution)/shard_map/ppermute | solution.py:124
  395.6 19.9 %collective-permute-start.19 = (f32[4,32,1024]{2,1,0:T(8,128)S(1)}, f32[4,32,1024]{2,1,0:T(8,128)S(1)}, u32[]{:S(2)}, u32[]{:S(2)}) collective-permute-start(f32[4,32,1024]{2,1,0:T(8,128)S(1)} %maximum_select_fusion.20), channel_id=1, source_target_pairs={{0,8},{4,12},{8,0},{12,4},{16,24},{20,28},{24,16},{28,20},{1,9},{5... | collective-permute-start | bytes 1572872 | tf_op jit(solution)/shard_map/ppermute | solution.py:124
  397.2 24.1 %collective-permute-start.22 = (f32[4,32,1024]{2,1,0:T(8,128)S(1)}, f32[4,32,1024]{2,1,0:T(8,128)S(1)}, u32[]{:S(2)}, u32[]{:S(2)}) collective-permute-start(f32[4,32,1024]{2,1,0:T(8,128)S(1)} %maximum_select_fusion.21), channel_id=1, source_target_pairs={{0,8},{4,12},{8,0},{12,4},{16,24},{20,28},{24,16},{28,20},{1,9},{5... | collective-permute-start | bytes 1572872 | tf_op jit(solution)/shard_map/ppermute | solution.py:124
  401.3 25.6 %collective-permute-start.25 = (f32[4,32,1024]{2,1,0:T(8,128)S(1)}, f32[4,32,1024]{2,1,0:T(8,128)S(1)}, u32[]{:S(2)}, u32[]{:S(2)}) collective-permute-start(f32[4,32,1024]{2,1,0:T(8,128)S(1)} %maximum_select_fusion.22), channel_id=1, source_target_pairs={{0,8},{4,12},{8,0},{12,4},{16,24},{20,28},{24,16},{28,20},{1,9},{5... | collective-permute-start | bytes 1572872 | tf_op jit(solution)/shard_map/ppermute | solution.py:124
  404.3 23.7 %collective-permute-start.17 = (f32[4,64,512]{2,1,0:T(8,128)S(1)}, f32[4,64,512]{2,1,0:T(8,128)S(1)}, u32[]{:S(2)}, u32[]{:S(2)}) collective-permute-start(f32[4,64,512]{2,1,0:T(8,128)S(1)} %maximum_select_fusion.19), channel_id=1, source_target_pairs={{0,4},{4,0},{8,12},{12,8},{16,20},{20,16},{24,28},{28,24},{1,5},{5... | collective-permute-start | bytes 1572872 | tf_op jit(solution)/shard_map/ppermute | solution.py:124
  415.6 42.3 %collective-permute-start.20 = (f32[4,64,1024]{2,1,0:T(8,128)S(1)}, f32[4,64,1024]{2,1,0:T(8,128)S(1)}, u32[]{:S(2)}, u32[]{:S(2)}) collective-permute-start(f32[4,64,1024]{2,1,0:T(8,128)S(1)} %maximum_select_fusion.15), channel_id=1, source_target_pairs={{0,4},{4,0},{8,12},{12,8},{16,20},{20,16},{24,28},{28,24},{1,5},{5... | collective-permute-start | bytes 3145736 | tf_op jit(solution)/shard_map/ppermute | solution.py:124
  422.4 68.2 %collective-permute-start.23 = (f32[4,64,1024]{2,1,0:T(8,128)}, f32[4,64,1024]{2,1,0:T(8,128)}, u32[]{:S(2)}, u32[]{:S(2)}) collective-permute-start(f32[4,64,1024]{2,1,0:T(8,128)} %maximum_select_fusion.16), channel_id=1, source_target_pairs={{0,4},{4,0},{8,12},{12,8},{16,20},{20,16},{24,28},{28,24},{1,5},{5... | collective-permute-start | bytes 3145736 | tf_op jit(solution)/shard_map/ppermute | solution.py:124
  428.0 65.7 %collective-permute-start.26 = (f32[4,64,1024]{2,1,0:T(8,128)}, f32[4,64,1024]{2,1,0:T(8,128)}, u32[]{:S(2)}, u32[]{:S(2)}) collective-permute-start(f32[4,64,1024]{2,1,0:T(8,128)} %maximum_select_fusion.17), channel_id=1, source_target_pairs={{0,4},{4,0},{8,12},{12,8},{16,20},{20,16},{24,28},{28,24},{1,5},{5... | collective-permute-start | bytes 3145736 | tf_op jit(solution)/shard_map/ppermute | solution.py:124
  (48 other events, 288.9 us)
Sparse Core Ops, SparseCore 0:
  17.0 35.1 all-gather.3
  53.7 28.1 all-gather.5
  84.1 27.4 all-gather.7

commit v2 on v1

v2 whole, which is shorter than its diff:
```python
import jax
import jax.numpy as jnp
from jax import lax
from jax.experimental import pallas as pl
from jax.experimental.pallas import tpu as pltpu
from jax.sharding import PartitionSpec as P

BLK = 128
PIVOT_BLOCKS = 8
SUB = 8
STRIP = 256


def split_parts(value):
    high = value.astype(jnp.bfloat16)
    low = (value - high.astype(jnp.float32)).astype(jnp.bfloat16)
    return high, low


def product_3(left, right, transposed=False):
    dims = (((1,), (1 if transposed else 0,)), ((), ()))
    left_high, left_low = split_parts(left)
    right_high, right_low = split_parts(right)

    def one(first, second):
        return lax.dot_general(first, second, dims, preferred_element_type=jnp.float32)

    return one(left_high, right_high) + (one(left_high, right_low) + one(left_low, right_high))


def invert_block(block, inverse_ref):
    count = BLK // SUB
    shape = (SUB, BLK)
    rows = [block[SUB * m : SUB * m + SUB] for m in range(count)]
    lane = lax.broadcasted_iota(jnp.int32, shape, 1)
    sublane = lax.broadcasted_iota(jnp.int32, shape, 0)
    unit = [(lane == sublane + SUB * m).astype(jnp.float32) for m in range(count)]
    for k in range(count):
        base = SUB * k
        cols = [jnp.broadcast_to(rows[k][:, base + j : base + j + 1], shape) for j in range(SUB)]
        d = [[jnp.broadcast_to(cols[j][i : i + 1], shape) for j in range(i + 1)] for i in range(SUB)]
        ya = [jnp.broadcast_to(rows[k][j : j + 1], shape) for j in range(SUB)]
        ye = [jnp.broadcast_to(unit[k][j : j + 1], shape) for j in range(SUB)]
        f = [[None] * SUB for _ in range(SUB)]
        reciprocal = [None] * SUB
        for c in range(SUB):
            reciprocal[c] = 1.0 / d[c][c]
            for i in range(c + 1, SUB):
                f[i][c] = d[i][c] * reciprocal[c]
            for i in range(c + 1, SUB):
                for j in range(c + 1, i + 1):
                    d[i][j] = d[i][j] - (d[i][c] * d[j][c]) * reciprocal[c]
            for i in range(c + 1, SUB):
                ya[i] = ya[i] - f[i][c] * ya[c]
                ye[i] = ye[i] - f[i][c] * ye[c]
            inverse_ref[base + c : base + c + 1, :] = (lax.rsqrt(d[c][c]) * ye[c])[0:1]
        if k == count - 1:
            break
        za = [y * r for y, r in zip(ya, reciprocal)]
        ze = [y * r for y, r in zip(ye, reciprocal)]
        for i in reversed(range(SUB)):
            for c in range(i):
                za[c] = za[c] - f[i][c] * za[i]
                ze[c] = ze[c] - f[i][c] * ze[i]
        for m in range(k + 1, count):
            col = [jnp.broadcast_to(rows[m][:, base + j : base + j + 1], shape) for j in range(SUB)]
            pa = [c * z for c, z in zip(col, za)]
            pe = [c * z for c, z in zip(col, ze)]
            while len(pa) > 1:
                pa = [x + y for x, y in zip(pa[::2], pa[1::2])]
                pe = [x + y for x, y in zip(pe[::2], pe[1::2])]
            rows[m] = rows[m] - pa[0]
            unit[m] = unit[m] - pe[0]


def factor_in_place(work_ref, block_ref, factor_ref, first_column, inverse_ref):
    size = work_ref.shape[0]
    row = lax.broadcasted_iota(jnp.int32, (size, size), 0)
    column = lax.broadcasted_iota(jnp.int32, (size, size), 1)
    work_ref[:, size:] = (row == column).astype(jnp.float32)
    row = lax.broadcasted_iota(jnp.int32, (size, BLK), 0)
    column = lax.broadcasted_iota(jnp.int32, (size, BLK), 1)

    def step(index, carry):
        base = pl.multiple_of(index * BLK, BLK)
        invert_block(work_ref[pl.ds(base, BLK), pl.ds(base, BLK)], block_ref)
        block = block_ref[...]
        below = product_3(work_ref[:, pl.ds(base, BLK)], block, transposed=True)
        right = product_3(block, work_ref[pl.ds(base, BLK), :])
        below = jnp.where(row >= column + base, below, 0.0)
        factor_ref[:, pl.ds(pl.multiple_of(first_column + base, BLK), BLK)] = below
        inverse_ref[pl.ds(base, BLK), :] = right[:, size:]
        below = jnp.where(row >= base + BLK, below, 0.0)
        work_ref[...] = work_ref[...] - product_3(below, right)
        return carry

    lax.fori_loop(0, size // BLK, step, 0)


def start_copies(plan, position_ref, source, blocks, portion, width, first, target_ref, sems):
    copies = []
    rows = plan["piece_rows"]
    members = 2 ** plan["height"]
    for order, block in enumerate(blocks):
        slot = position_ref[block % plan["front_count"]]
        for member in range(members):
            place = position_ref[plan["front_count"] + member]
            start = pl.multiple_of(order * BLK + place * rows, rows)
            copy = pltpu.make_async_copy(
                source(member, portion, block, slot).at[:, pl.ds(first, width)],
                target_ref.at[pl.ds(start, rows), pl.ds(0, width)],
                sems.at[order * members + member],
            )
            copy.start()
            copies.append(copy)
    return copies


class Child:
    def __init__(self, strips, halves, core):
        self.strips, self.halves, self.core = strips, halves, core

    def block(self, i, j):
        strip, part = i // 2, i % 2
        columns = pl.ds(j * BLK, BLK)
        if self.halves is None:
            return self.strips[strip][pl.ds(part * BLK, BLK), columns]
        mine, theirs = self.halves[strip]
        return jnp.where(self.core == part, mine[:, columns], theirs[:, columns])


def child_sum(children, i, j, weights):
    flip = i // 2 < j // 2
    total = None
    for child, weight in zip(children, weights):
        term = child.block(*((j, i) if flip else (i, j))) * weight
        total = term if total is None else total + term
    return total.T if flip else total


def make_source(plan, refs):
    if plan["height"] == 1:
        return lambda member, portion, block, slot: refs[
            (portion, block // plan["front_count"], member)
        ].at[slot]
    return lambda member, portion, block, slot: refs[member].at[
        slot, portion, block // plan["front_count"]
    ]


def unpack(plan, refs, portions, blocks, strips):
    refs = list(refs)
    position_ref, mask_ref = refs.pop(0), refs.pop(0)
    names = piece_names(plan, portions, blocks)
    pieces = {name: refs.pop(0) for name in names}
    children = []
    if plan["height"] > 1:
        own = {strip: refs.pop(0) for strip in strips}
        other = {strip: (refs.pop(0), refs.pop(0)) for strip in strips}
        core = position_ref[plan["front_count"] + 2 ** plan["height"]]
        children = [Child(own, None, core), Child(None, other, core)]
    return position_ref, mask_ref, make_source(plan, pieces), children, refs


def piece_names(plan, portions, blocks):
    members = range(2 ** plan["height"])
    if plan["height"] > 1:
        return list(members)
    slabs = sorted({block // plan["front_count"] for block in blocks})
    return [(p, t, m) for p in portions for t in slabs for m in members]


def leading(plan, state, portions, blocks, strips):
    smem = pl.BlockSpec(memory_space=pltpu.SMEM)
    anywhere = pl.BlockSpec(memory_space=pl.ANY)
    vmem = pl.BlockSpec(memory_space=pltpu.VMEM)
    operands = [state["position"], state["masks"]]
    specs = [smem, smem]
    for name in piece_names(plan, portions, blocks):
        operands.append(state["pieces"][name])
        specs.append(anywhere)
    if plan["height"] > 1:
        for strip in strips:
            operands.append(state["own"][strip])
            specs.append(vmem)
        for strip in strips:
            operands.extend(state["other"][strip])
            specs.extend([vmem, vmem])
    return operands, specs


def factor_chunk(plan, state, chunk, factors, inverses):
    low, high = plan["chunks"][chunk]
    size, width = high - low, high
    blocks = range(low // BLK, high // BLK)
    strips = range(low // STRIP, high // STRIP)
    earlier = plan["chunks"][:chunk]

    def kernel(*refs):
        position_ref, mask_ref, source, children, refs = unpack(plan, refs, (0,), blocks, strips)
        old_factors, old_inverses = refs[:chunk], refs[chunk : 2 * chunk]
        factor_ref, inverse_ref, rows_ref, work_ref, block_ref, sems = refs[2 * chunk :]
        copies = start_copies(plan, position_ref, source, blocks, 0, width, 0, rows_ref, sems)
        for copy in copies:
            copy.wait()
        if children:
            for order, i in enumerate(blocks):
                for j in range(width // BLK):
                    weights = [
                        mask_ref[c * PIVOT_BLOCKS + i] * mask_ref[c * PIVOT_BLOCKS + j] for c in (0, 1)
                    ]
                    if i // 2 < j // 2 and (i // 2) * STRIP + STRIP <= low:
                        continue
                    rows_ref[pl.ds(order * BLK, BLK), pl.ds(j * BLK, BLK)] += child_sum(
                        children, i, j, weights
                    )
        corner = rows_ref[:, pl.ds(low, size)]
        for index, (first, last) in enumerate(earlier):
            part = rows_ref[:, pl.ds(first, last - first)]
            if index:
                part = part - product_3(
                    factor_ref[:, pl.ds(0, first)], old_factors[index][:, pl.ds(0, first)], True
                )
            part = product_3(part, old_inverses[index][...], True)
            factor_ref[:, pl.ds(first, last - first)] = part
        if chunk:
            done = factor_ref[:, pl.ds(0, low)]
            corner = corner - product_3(done, done, True)
        work_ref[:, pl.ds(0, size)] = corner
        if width < plan["pivot_size"]:
            factor_ref[:, width:] = jnp.zeros((size, plan["pivot_size"] - width), jnp.float32)
        factor_in_place(work_ref, block_ref, factor_ref, low, inverse_ref)

    operands, specs = leading(plan, state, (0,), blocks, strips)
    vmem = pl.BlockSpec(memory_space=pltpu.VMEM)
    operands += factors[:chunk] + inverses[:chunk]
    specs += [vmem] * (2 * chunk)
    return pl.pallas_call(
        kernel,
        out_shape=[
            jax.ShapeDtypeStruct((size, plan["pivot_size"]), jnp.float32),
            jax.ShapeDtypeStruct((size, size), jnp.float32),
        ],
        in_specs=specs,
        out_specs=[vmem, vmem],
        scratch_shapes=[
            pltpu.VMEM((size, width), jnp.float32),
            pltpu.VMEM((size, 2 * size), jnp.float32),
            pltpu.VMEM((BLK, BLK), jnp.float32),
            pltpu.SemaphoreType.DMA((len(blocks) * 2 ** plan["height"],)),
        ],
        compiler_params=pltpu.CompilerParams(vmem_limit_bytes=48 * 2**20),
        cost_estimate=pl.CostEstimate(
            flops=60_000_000_000 * size // 1024, bytes_accessed=8 * size * width, transcendentals=0
        ),
        name=f"factor_chunk_{chunk}",
    )(*operands)


def panel_and_schur(plan, state, strips, factors, inverses, panel_before, last):
    pivot_size = plan["pivot_size"]
    blocks = range(strips[0] * STRIP // BLK, (strips[-1] + 1) * STRIP // BLK)
    size = len(blocks) * BLK
    start = strips[0] * STRIP
    chunks = plan["chunks"]
    count = len(chunks)
    everything = range(pivot_size // STRIP)
    final = strips[-1] == everything[-1]
    before = [] if panel_before is None else [panel_before]
    first_level = plan["height"] == 1
    rows = plan["piece_rows"]
    slabs = PIVOT_BLOCKS // plan["front_count"]

    def kernel(*refs):
        position_ref, mask_ref, source, children, refs = unpack(plan, refs, (1,), blocks, everything)
        factor_refs, inverse_refs = refs[:count], refs[count : 2 * count]
        refs = refs[2 * count :]
        before_refs, refs = refs[: len(before)], refs[len(before) :]
        panel_ref, refs = refs[0], refs[1:]
        if last:
            schur_refs, refs = refs[:1], refs[1:]
        else:
            schur_refs, refs = refs[: len(strips)], refs[len(strips) :]
        if final:
            own_ref, refs = refs[0], refs[1:]
        rows_ref, corner_ref, sems, corner_sems = refs
        copies = start_copies(plan, position_ref, source, blocks, 1, pivot_size, 0, rows_ref, sems)
        corner_copies = []
        if first_level:
            members = 2 ** plan["height"]
            for order, block in enumerate(blocks):
                limit = (block // plan["front_count"] + 1) * plan["front_count"] * BLK
                corner_copies += start_copies(
                    plan,
                    position_ref,
                    source,
                    [block],
                    1,
                    limit,
                    pivot_size,
                    corner_ref.at[pl.ds(order * BLK, BLK)],
                    corner_sems.at[pl.ds(order * members, members)],
                )
        for copy in copies:
            copy.wait()
        if children:
            for order, i in enumerate(blocks):
                for j in range(PIVOT_BLOCKS):
                    weights = [
                        (1.0 - mask_ref[c * PIVOT_BLOCKS + i]) * mask_ref[c * PIVOT_BLOCKS + j]
                        for c in (0, 1)
                    ]
                    rows_ref[pl.ds(order * BLK, BLK), pl.ds(j * BLK, BLK)] += child_sum(
                        children, i, j, weights
                    )
                    if last or j // 2 <= i // 2:
                        weights = [
                            (1.0 - mask_ref[c * PIVOT_BLOCKS + i])
                            * (1.0 - mask_ref[c * PIVOT_BLOCKS + j])
                            for c in (0, 1)
                        ]
                        corner_ref[pl.ds(order * BLK, BLK), pl.ds(j * BLK, BLK)] = child_sum(
                            children, i, j, weights
                        )
        for index, (low, high) in enumerate(chunks):
            part = rows_ref[:, pl.ds(low, high - low)]
            if index:
                part = part - product_3(
                    panel_ref[:, pl.ds(0, low)], factor_refs[index][:, pl.ds(0, low)], True
                )
            panel_ref[:, pl.ds(low, high - low)] = product_3(part, inverse_refs[index][...], True)
        for copy in corner_copies:
            copy.wait()
        if not last:
            for order, strip in enumerate(strips):
                mine = panel_ref[pl.ds(order * STRIP, STRIP), :]
                for column in range(strip + 1):
                    if column * STRIP < start:
                        other = before_refs[0][pl.ds(column * STRIP, STRIP), :]
                    else:
                        other = panel_ref[pl.ds(column * STRIP - start, STRIP), :]
                    schur_refs[order][:, pl.ds(column * STRIP, STRIP)] = corner_ref[
                        pl.ds(order * STRIP, STRIP), pl.ds(column * STRIP, STRIP)
                    ] - product_3(mine, other, True)
        if not final:
            return
        base = plan["front_count"] + 2 ** plan["height"] + 1
        piece = pl.multiple_of(position_ref[base + 1] * rows, rows)
        for slab in range(slabs):
            block = position_ref[base] + plan["front_count"] * slab
            line = pl.multiple_of(block * BLK + piece, rows)
            for index, (low, high) in enumerate(chunks):

                @pl.when((line >= low) & (line < high))
                def _():
                    own_ref[pl.ds(slab * rows, rows), :] = factor_refs[index][
                        pl.ds(pl.multiple_of(line - low, rows), rows), :
                    ]

            target = pl.ds((slabs + slab) * rows, rows)
            if before:

                @pl.when(line < start)
                def _():
                    own_ref[target, :] = before_refs[0][pl.ds(pl.multiple_of(line, rows), rows), :]

            @pl.when(line >= start)
            def _():
                own_ref[target, :] = panel_ref[pl.ds(pl.multiple_of(line - start, rows), rows), :]

            if last:
                schur_refs[0][pl.ds(slab * rows, rows), :] = corner_ref[pl.ds(line, rows), :]
        if last:
            mine = own_ref[pl.ds(slabs * rows, slabs * rows), :]
            schur_refs[0][...] -= product_3(mine, panel_ref[...], True)

    operands, specs = leading(plan, state, (1,), blocks, everything)
    vmem = pl.BlockSpec(memory_space=pltpu.VMEM)
    operands += factors + inverses + before
    specs += [vmem] * (2 * count + len(before))
    shapes = [(size, pivot_size)]
    if last:
        shapes.append((slabs * rows, pivot_size))
    else:
        shapes += [(STRIP, (strip + 1) * STRIP) for strip in strips]
    if final:
        shapes.append((2 * slabs * rows, pivot_size))
    copy_count = len(blocks) * 2 ** plan["height"]
    return pl.pallas_call(
        kernel,
        out_shape=[jax.ShapeDtypeStruct(shape, jnp.float32) for shape in shapes],
        in_specs=specs,
        out_specs=[vmem] * len(shapes),
        scratch_shapes=[
            pltpu.VMEM((size, pivot_size), jnp.float32),
            pltpu.VMEM((size, pivot_size), jnp.float32),
            pltpu.SemaphoreType.DMA((copy_count,)),
            pltpu.SemaphoreType.DMA((copy_count,)),
        ],
        compiler_params=pltpu.CompilerParams(vmem_limit_bytes=56 * 2**20),
        cost_estimate=pl.CostEstimate(
            flops=8_000_000_000 * size // 1024, bytes_accessed=8 * size * pivot_size, transcendentals=0
        ),
        name=f"panel_{strips[0]}",
    )(*operands)


def partner_2(value, axis, stride):
    mask = 2**stride
    pairs = [(source, source ^ mask) for source in range(lax.axis_size(axis))]
    return lax.ppermute(value, axis, pairs)


def reversed_bits(number, bit_count):
    result = jnp.zeros((), jnp.int32)
    for bit_index in range(bit_count):
        result = result + (number >> bit_index & 1) * (1 << bit_count - 1 - bit_index)
    return result


def ring_front(value):
    count = lax.axis_size("front")
    pairs = [(source, (source + 1) % count) for source in range(count)]
    slots = [value]
    for _ in range(count - 1):
        slots.append(lax.ppermute(slots[-1], "front", pairs))
    return jnp.stack(slots)


def gather_pieces(value, height):
    arrays = {0: ring_front(value)}
    for bit in reversed(range(height)):
        arrays.update({m | 1 << bit: partner_2(a, "leaf", bit) for m, a in list(arrays.items())})
    return [arrays[m] for m in range(2**height)]


def local(
    leaf_contrib,
    entries_lower,
    entries_middle,
    entries_upper,
    assembly_lower,
    assembly_middle,
    assembly_upper,
):
    front_count = lax.axis_size("front")
    slabs = PIVOT_BLOCKS // front_count
    leaf_index = lax.axis_index("leaf")
    front_index = lax.axis_index("front")
    pivot_size = leaf_contrib.shape[1]
    core = leaf_index & 1
    my_blocks = front_index + front_count * jnp.arange(slabs, dtype=jnp.int32)
    chunks = [(0, STRIP), (STRIP, 2 * STRIP), (2 * STRIP, pivot_size)]
    results = []
    schur = None
    for height, entries, routes in (
        (1, entries_lower, assembly_lower),
        (2, entries_middle, assembly_middle),
        (3, entries_upper, assembly_upper),
    ):
        piece_rows = BLK // 2**height
        plan = dict(
            height=height,
            piece_rows=piece_rows,
            front_count=front_count,
            pivot_size=pivot_size,
            chunks=chunks,
        )
        child_bit = leaf_index >> height - 1 & 1
        route_pair = lax.dynamic_index_in_dim(routes, leaf_index >> height, 0, keepdims=False)
        pivot_masks = (route_pair < PIVOT_BLOCKS).astype(jnp.float32)
        masks = jnp.where(child_bit == 0, pivot_masks, pivot_masks[::-1])
        position = jnp.concatenate(
            [
                (front_index - jnp.arange(front_count, dtype=jnp.int32)) % front_count,
                jnp.stack(
                    [
                        reversed_bits((leaf_index ^ m) & 2**height - 1, height)
                        for m in range(2**height)
                    ]
                    + [core, front_index, reversed_bits(leaf_index & 2**height - 1, height)]
                ),
            ]
        ).astype(jnp.int32)
        state = dict(position=position, masks=masks.reshape(-1))
        local_entries = entries.reshape(2, slabs, piece_rows, pivot_size)
        if height == 1:
            update = leaf_contrib.reshape(slabs, BLK, pivot_size)
            low_rows, high_rows = update[:, :piece_rows], update[:, piece_rows:]
            kept = jnp.where(child_bit == 0, low_rows, high_rows)
            outgoing = jnp.where(child_bit == 0, high_rows, low_rows)
            received = partner_2(outgoing, "leaf", 0)
            row_masks = masks[:, my_blocks]
            spread = jnp.repeat(masks, BLK, axis=1)

            def term(slab, width, row_pivot, column_pivot):
                total = 0.0
                for child, rows in enumerate((kept, received)):
                    row = row_masks[child, slab] if row_pivot else 1.0 - row_masks[child, slab]
                    column = spread[child] if column_pivot else 1.0 - spread[child]
                    total = total + rows[slab, :, :width] * (row * column[:width])[None]
                return total

            state["pieces"] = {}
            for slab in range(slabs):
                width = (slab + 1) * front_count * BLK
                value = local_entries[0, slab, :, :width] + term(slab, width, True, True)
                for m, array in enumerate(gather_pieces(value, height)):
                    state["pieces"][(0, slab, m)] = array
            for slab in range(slabs):
                width = (slab + 1) * front_count * BLK
                value = jnp.concatenate(
                    [
                        local_entries[1, slab] + term(slab, pivot_size, False, True),
                        term(slab, width, False, False),
                    ],
                    axis=1,
                )
                for m, array in enumerate(gather_pieces(value, height)):
                    state["pieces"][(1, slab, m)] = array
        else:
            state["pieces"] = dict(enumerate(gather_pieces(local_entries, height)))
            state["own"] = schur
            state["other"] = []
            for strip in schur:
                half = lax.dynamic_slice_in_dim(strip, core * BLK, BLK, 0)
                mine = partner_2(half, "leaf", height - 1)
                state["other"].append((mine, partner_2(mine, "leaf", 0)))
        factors, inverses = [], []
        for chunk in range(len(chunks)):
            factor, inverse = factor_chunk(plan, state, chunk, factors, inverses)
            factors.append(factor)
            inverses.append(inverse)
        strips = list(range(pivot_size // STRIP))
        if height < 3:
            panel, first_strip = panel_and_schur(
                plan, state, strips[:1], factors, inverses, None, False
            )
            _, *others, own = panel_and_schur(
                plan, state, strips[1:], factors, inverses, panel, False
            )
            schur = [first_strip] + others
        else:
            _, top, own = panel_and_schur(plan, state, strips, factors, inverses, None, True)
        results.append(own)
    return (results[0], results[1], results[2], top)


def solution(mesh):
    spec = P(("leaf", "front"), None)
    return jax.shard_map(
        local,
        mesh=mesh,
        in_specs=(spec, spec, spec, spec, P(), P(), P()),
        out_specs=(spec, spec, spec, spec),
        check_vma=False,
    )
```

time: 517 us -> 478 us (0.925)
  blocking collectives: 138 us -> 0 us
  Pallas kernels: 175 us -> 261 us
  waiting for transfers between devices: 75.5 us -> 132 us
  matrix products: 33.1 us -> 0 us
  starting transfers between devices: 14.4 us -> 37.3 us
  other arithmetic: 36.1 us -> 17.3 us
  between operations: 15.2 us -> 4.59 us
  local copies, waits for them, and re-layouts: 26.5 us -> 19.7 us
    all_gather x9 -> x0, blocking collectives: 138 us -> none  [group_gather(): gathered = lax.all_gather(pieces, 'front', axis=0, tiled=False)]
    pallas_call x6 -> x14, Pallas kernels: 175 us -> 261 us  [the longest x9 184 us: factor_chunk(): pl.pallas_call(kernel, out_shape=[jax.ShapeDtypeStruct((size, plan['pivot...]
    ppermute x0 -> x18, waiting for transfers between devices: none -> 71.9 us  [ring_front(): slots.append(lax.ppermute(slots[-1], 'front', pairs))]
    all_gather x3 -> x0, waiting for transfers between devices: 36.9 us -> none  [group_gather(): gathered = lax.all_gather(pieces, 'front', axis=0, tiled=False)]
    dot_general x27 -> x0, matrix products: 33.1 us -> none  [product(): jnp.dot(left, right, precision=lax.Precision.HIGH, preferred_element_type...]
    select_n x24 -> x5, other arithmetic: 23.2 us -> 0.61 us  [the longest x3 0.59 us: local(): masks = jnp.where(child_bit == 0, pivot_masks, pivot_masks[::-1])]
    ppermute x27 -> x31, waiting for transfers between devices: 38.5 us -> 59.7 us  [partner_2(): return lax.ppermute(value, axis, pairs)]
    ppermute x0 -> x18, starting transfers between devices: none -> 20.4 us  [ring_front(): slots.append(lax.ppermute(slots[-1], 'front', pairs))]
  transfers between devices with their start and end apart: 30 -> 49, of which waited for: 10 -> 14; matrix products, arithmetic and copies ran while one was open for 9% -> 6% of each run, Pallas kernels for 34% -> 44%
where the time goes in v2:
time: 478 us; the launch traced here: 471 us
  Pallas kernels  261 us (55%)
  waiting for transfers between devices  132 us (28%)
  starting transfers between devices  37.3 us (8%)
  local copies, waits for them, and re-layouts  19.7 us (4%)
  other arithmetic  17.3 us (4%)
    pallas_call x9, Pallas kernels, factor_chunk(): pl.pallas_call(kernel, out_shape=[jax.ShapeDtypeStruct((size, plan['pivot...  184 us
    pallas_call x5, Pallas kernels, panel_and_schur(): pl.pallas_call(kernel, out_shape=[jax.ShapeDtypeStruct(shape, jnp.float32...  76.5 us
    ppermute x18, waiting for transfers between devices, ring_front(): slots.append(lax.ppermute(slots[-1], 'front', pairs))  71.9 us
    ppermute x31, waiting for transfers between devices, partner_2(): return lax.ppermute(value, axis, pairs)  59.7 us
    ppermute x18, starting transfers between devices, ring_front(): slots.append(lax.ppermute(slots[-1], 'front', pairs))  20.4 us
    ppermute x31, starting transfers between devices, partner_2(): return lax.ppermute(value, axis, pairs)  16.9 us
  transfers between devices with their start and end apart: 49, of which 14 were waited for; matrix products, arithmetic and copies ran while one was open for 6% of the time, Pallas kernels for 44%

profile of v2, /device:TPU:0, one launch (start us, length us, event | category | flops | bytes accessed | tf_op | source)
XLA Modules:
  0.0 471.2 jit_solution(10573007556820395660)
XLA Ops:
  29.0 8.0 %collective-permute-done.9 = f32[64,512]{1,0:T(8,128)} collective-permute-done((f32[64,512]{1,0:T(8,128)}, f32[64,512]{1,0:T(8,128)}, u32[]{:S(2)}, u32[]{:S(2)}) %collective-permute-start.9) | collective-permute-done | bytes 131104 | tf_op jit(solution)/shard_map/ppermute | solution.py:426
  37.0 5.6 %collective-permute-done.13 = f32[64,1024]{1,0:T(8,128)} collective-permute-done((f32[64,1024]{1,0:T(8,128)}, f32[64,1024]{1,0:T(8,128)}, u32[]{:S(2)}, u32[]{:S(2)}) %collective-permute-start.13) | collective-permute-done | bytes 262176 | tf_op jit(solution)/shard_map/ppermute | solution.py:426
  42.7 19.4 %collective-permute-done.10 = f32[64,512]{1,0:T(8,128)S(1)} collective-permute-done((f32[64,512]{1,0:T(8,128)}, f32[64,512]{1,0:T(8,128)S(1)}, u32[]{:S(2)}, u32[]{:S(2)}) %collective-permute-start.10) | collective-permute-done | bytes 131104 | tf_op jit(solution)/shard_map/ppermute | solution.py:426
  66.0 15.9 %collective-permute-done.11 = f32[64,512]{1,0:T(8,128)S(1)} collective-permute-done((f32[64,512]{1,0:T(8,128)S(1)}, f32[64,512]{1,0:T(8,128)S(1)}, u32[]{:S(2)}, u32[]{:S(2)}) %collective-permute-start.11) | collective-permute-done | bytes 131104 | tf_op jit(solution)/shard_map/ppermute | solution.py:426
  86.1 21.0 %collective-permute-done.15 = f32[64,1024]{1,0:T(8,128)S(1)} collective-permute-done((f32[64,1024]{1,0:T(8,128)S(1)}, f32[64,1024]{1,0:T(8,128)S(1)}, u32[]{:S(2)}, u32[]{:S(2)}) %collective-permute-start.15) | collective-permute-done | bytes 262176 | tf_op jit(solution)/shard_map/ppermute | solution.py:426
  112.8 12.6 %factor_chunk_0.3 = (f32[256,1024]{1,0:T(8,128)S(1)}, f32[256,256]{1,0:T(8,128)S(1)}) custom-call(s32[9]{0:T(128)S(1)} %concatenate.15.refs_0_, f32[16]{0:T(128)S(1)} %reshape.223.refs_1_, f32[4,64,512]{2,1,0:T(8,128)S(1)} %pad_maximum_fusion.6.refs_2_, f32[4,64,512]{2,1,0:T(8,128)S(1)} %collective-permute-done.12.refs_3_), custom_call_target="tpu_custom_call" | custom-call | flops 15000000512 | bytes 524288 | tf_op jit(solution)/shard_map/factor_chunk_0/pallas_call | solution.py:238
  127.3 13.9 %factor_chunk_1.3 = (f32[256,1024]{1,0:T(8,128)S(1)}, f32[256,256]{1,0:T(8,128)S(1)}) custom-call(s32[9]{0:T(128)S(1)} %concatenate.15.refs_0_, f32[16]{0:T(128)S(1)} %reshape.223.refs_1_, f32[4,64,512]{2,1,0:T(8,128)S(1)} %pad_maximum_fusion.6.refs_2_, f32[4,64,512]{2,1,0:T(8,128)S(1)} %collective-permute-done.12.refs_3_, ...), custom_call_target="tpu_custom_call" | custom-call | flops 15000000512 | bytes 1048576 | tf_op jit(solution)/shard_map/factor_chunk_1/pallas_call | solution.py:238
  145.5 13.6 %collective-permute-done.21.refs_4_ = f32[4,2,2,32,1024]{4,3,2,1,0:T(8,128)} collective-permute-done((f32[4,2,2,32,1024]{4,3,2,1,0:T(8,128)S(1)}, f32[4,2,2,32,1024]{4,3,2,1,0:T(8,128)}, u32[]{:S(2)}, u32[]{:S(2)}) %collective-permute-start.21) | collective-permute-done | bytes 2097184 | tf_op jit(solution)/shard_map/ppermute | solution.py:411
  159.2 31.5 %factor_chunk_2.3 = (f32[512,1024]{1,0:T(8,128)}, f32[512,512]{1,0:T(8,128)S(1)}) custom-call(s32[9]{0:T(128)S(1)} %concatenate.15.refs_0_, f32[16]{0:T(128)S(1)} %reshape.223.refs_1_, f32[4,64,1024]{2,1,0:T(8,128)S(1)} %pad_maximum_fusion.3.refs_2_, f32[4,64,1024]{2,1,0:T(8,128)S(1)} %collective-permute-done.16.refs_3_, ...), custom_call_target="tpu_custom_call" | custom-call | flops 30000001024 | bytes 4194304 | tf_op jit(solution)/shard_map/factor_chunk_2/pallas_call | solution.py:238
  192.9 8.2 %panel_0.3 = (f32[256,1024]{1,0:T(8,128)}, f32[256,256]{1,0:T(8,128)}) custom-call(s32[9]{0:T(128)} %copy-done.29, f32[16]{0:T(128)} %copy-done.31, f32[4,64,1536]{2,1,0:T(8,128)} %copy-done.48, f32[4,64,1536]{2,1,0:T(8,128)} %copy-done.50, f32[256,1024]{1,0:T(8,128)} %copy-done.6, f32[256,1024]{1,0:T(8,128)} %copy-done.7, ...), custom_call_target="tpu_custom_call" | custom-call | flops 2000000000 | bytes 2097152 | tf_op jit(solution)/shard_map/panel_0/pallas_call | solution.py:389
  203.6 19.1 %panel_1.2 = (f32[768,1024]{1,0:T(8,128)}, f32[256,512]{1,0:T(8,128)}, f32[256,768]{1,0:T(8,128)}, f32[256,1024]{1,0:T(8,128)}, f32[256,1024]{1,0:T(8,128)}) custom-call(s32[9]{0:T(128)} %copy-done.29, f32[16]{0:T(128)} %copy-done.31, f32[4,64,1536]{2,1,0:T(8,128)} %copy-done.48, f32[4,64,1536]{2,1,0:T(8,128)} %copy-done.50, ...), custom_call_target="tpu_custom_call" | custom-call | flops 6000000000 | bytes 6291456 | tf_op jit(solution)/shard_map/panel_1/pallas_call | solution.py:389
  233.8 13.7 %factor_chunk_0.4 = (f32[256,1024]{1,0:T(8,128)S(1)}, f32[256,256]{1,0:T(8,128)S(1)}) custom-call(s32[11]{0:T(128)S(1)} %concatenate.18.refs_0_, f32[16]{0:T(128)S(1)} %reshape.226.refs_1_, f32[4,2,2,32,1024]{4,3,2,1,0:T(8,128)S(1)} %pad_maximum_fusion.1.refs_2_, f32[4,2,2,32,1024]{4,3,2,1,0:T(8,128)S(1)} %collective-permute-done.20.refs_3_, ...), custom_call_target="tpu_custom_call" | custom-call | flops 15000000512 | bytes 524288 | tf_op jit(solution)/shard_map/factor_chunk_0/pallas_call | solution.py:238
  247.5 7.4 %collective-permute-done.37.refs_6_ = f32[4,2,2,16,1024]{4,3,2,1,0:T(8,128)S(1)} collective-permute-done((f32[4,2,2,16,1024]{4,3,2,1,0:T(8,128)}, f32[4,2,2,16,1024]{4,3,2,1,0:T(8,128)S(1)}, u32[]{:S(2)}, u32[]{:S(2)}) %collective-permute-start.37) | collective-permute-done | bytes 1048608 | tf_op jit(solution)/shard_map/ppermute | solution.py:411
  257.4 14.3 %factor_chunk_1.4 = (f32[256,1024]{1,0:T(8,128)S(1)}, f32[256,256]{1,0:T(8,128)S(1)}) custom-call(s32[11]{0:T(128)S(1)} %concatenate.18.refs_0_, f32[16]{0:T(128)S(1)} %reshape.226.refs_1_, f32[4,2,2,32,1024]{4,3,2,1,0:T(8,128)S(1)} %pad_maximum_fusion.1.refs_2_, f32[4,2,2,32,1024]{4,3,2,1,0:T(8,128)} %copy-done.2, ...), custom_call_target="tpu_custom_call" | custom-call | flops 15000000512 | bytes 1048576 | tf_op jit(solution)/shard_map/factor_chunk_1/pallas_call | solution.py:238
  272.7 8.5 %collective-permute-done.35.refs_4_ = f32[4,2,2,16,1024]{4,3,2,1,0:T(8,128)} collective-permute-done((f32[4,2,2,16,1024]{4,3,2,1,0:T(8,128)}, f32[4,2,2,16,1024]{4,3,2,1,0:T(8,128)}, u32[]{:S(2)}, u32[]{:S(2)}) %collective-permute-start.35) | collective-permute-done | bytes 1048608 | tf_op jit(solution)/shard_map/ppermute | solution.py:411
  281.3 21.0 %collective-permute-done.39.refs_8_ = f32[4,2,2,16,1024]{4,3,2,1,0:T(8,128)} collective-permute-done((f32[4,2,2,16,1024]{4,3,2,1,0:T(8,128)S(1)}, f32[4,2,2,16,1024]{4,3,2,1,0:T(8,128)}, u32[]{:S(2)}, u32[]{:S(2)}) %collective-permute-start.39) | collective-permute-done | bytes 1048608 | tf_op jit(solution)/shard_map/ppermute | solution.py:411
  302.8 34.2 %factor_chunk_2.4 = (f32[512,1024]{1,0:T(8,128)}, f32[512,512]{1,0:T(8,128)S(1)}) custom-call(s32[11]{0:T(128)S(1)} %concatenate.18.refs_0_, f32[16]{0:T(128)S(1)} %reshape.226.refs_1_, f32[4,2,2,32,1024]{4,3,2,1,0:T(8,128)} %copy-done, f32[4,2,2,32,1024]{4,3,2,1,0:T(8,128)} %copy-done.2, f32[4,2,2,32,1024]{4,3,2,1,0:T(8,128)} %collective-permute-done.21.refs_4_, ...), custom_call_target="tpu_custom_call" | custom-call | flops 30000001024 | bytes 4194304 | tf_op jit(solution)/shard_map/factor_chunk_2/pallas_call | solution.py:238
  338.1 9.6 %panel_0.4 = (f32[256,1024]{1,0:T(8,128)}, f32[256,256]{1,0:T(8,128)}) custom-call(s32[11]{0:T(128)} %copy-done.28, f32[16]{0:T(128)} %copy-done.30, f32[4,2,2,32,1024]{4,3,2,1,0:T(8,128)} %copy-done, f32[4,2,2,32,1024]{4,3,2,1,0:T(8,128)} %copy-done.2, f32[4,2,2,32,1024]{4,3,2,1,0:T(8,128)} %collective-permute-done.21.refs_4_, ...), custom_call_target="tpu_custom_call" | custom-call | flops 2000000000 | bytes 2097152 | tf_op jit(solution)/shard_map/panel_0/pallas_call | solution.py:389
  350.2 19.7 %panel_1.3 = (f32[768,1024]{1,0:T(8,128)}, f32[256,512]{1,0:T(8,128)}, f32[256,768]{1,0:T(8,128)}, f32[256,1024]{1,0:T(8,128)}, f32[128,1024]{1,0:T(8,128)}) custom-call(s32[11]{0:T(128)} %copy-done.28, f32[16]{0:T(128)} %copy-done.30, f32[4,2,2,32,1024]{4,3,2,1,0:T(8,128)} %copy-done, f32[4,2,2,32,1024]{4,3,2,1,0:T(8,128)} %copy-done.2, ...), custom_call_target="tpu_custom_call" | custom-call | flops 6000000000 | bytes 6291456 | tf_op jit(solution)/shard_map/panel_1/pallas_call | solution.py:389
  376.1 4.1 collective-permute-done.43.refs_11_.refs_16_
  380.2 13.8 %factor_chunk_0.5 = (f32[256,1024]{1,0:T(8,128)S(1)}, f32[256,256]{1,0:T(8,128)S(1)}) custom-call(s32[15]{0:T(128)S(1)} %concatenate.19.refs_0_, f32[16]{0:T(128)S(1)} %reshape.228.refs_1_, f32[4,2,2,16,1024]{4,3,2,1,0:T(8,128)} %pad_maximum_fusion.4.refs_2_, f32[4,2,2,16,1024]{4,3,2,1,0:T(8,128)} %collective-permute-done.34.refs_3_, ...), custom_call_target="tpu_custom_call" | custom-call | flops 15000000512 | bytes 524288 | tf_op jit(solution)/shard_map/factor_chunk_0/pallas_call | solution.py:238
  398.7 15.3 %factor_chunk_1.5 = (f32[256,1024]{1,0:T(8,128)S(1)}, f32[256,256]{1,0:T(8,128)S(1)}) custom-call(s32[15]{0:T(128)S(1)} %concatenate.19.refs_0_, f32[16]{0:T(128)S(1)} %reshape.228.refs_1_, f32[4,2,2,16,1024]{4,3,2,1,0:T(8,128)} %pad_maximum_fusion.4.refs_2_, f32[4,2,2,16,1024]{4,3,2,1,0:T(8,128)} %collective-permute-done.34.refs_3_, ...), custom_call_target="tpu_custom_call" | custom-call | flops 15000000512 | bytes 1048576 | tf_op jit(solution)/shard_map/factor_chunk_1/pallas_call | solution.py:238
  415.1 34.8 %factor_chunk_2.5 = (f32[512,1024]{1,0:T(8,128)}, f32[512,512]{1,0:T(8,128)S(1)}) custom-call(s32[15]{0:T(128)S(1)} %concatenate.19.refs_0_, f32[16]{0:T(128)S(1)} %reshape.228.refs_1_, f32[4,2,2,16,1024]{4,3,2,1,0:T(8,128)} %pad_maximum_fusion.4.refs_2_, f32[4,2,2,16,1024]{4,3,2,1,0:T(8,128)} %collective-permute-done.34.refs_3_, ...), custom_call_target="tpu_custom_call" | custom-call | flops 30000001024 | bytes 4194304 | tf_op jit(solution)/shard_map/factor_chunk_2/pallas_call | solution.py:238
  451.0 20.0 %panel_0.5 = (f32[1024,1024]{1,0:T(8,128)}, f32[32,1024]{1,0:T(8,128)}, f32[64,1024]{1,0:T(8,128)}) custom-call(s32[15]{0:T(128)} %copy-done.32, f32[16]{0:T(128)} %copy-done.42, f32[4,2,2,16,1024]{4,3,2,1,0:T(8,128)} %pad_maximum_fusion.4.refs_2_, f32[4,2,2,16,1024]{4,3,2,1,0:T(8,128)} %collective-permute-done.34.refs_3_, ...), custom_call_target="tpu_custom_call" | custom-call | flops 8000000000 | bytes 8388608 | tf_op jit(solution)/shard_map/panel_0/pallas_call | solution.py:389
  (283 shorter events, 81.4 us)
Async XLA Ops:
  18.9 43.2 %collective-permute-start.1 = (f32[64,1536]{1,0:T(8,128)}, f32[64,1536]{1,0:T(8,128)S(1)}, u32[]{:S(2)}, u32[]{:S(2)}) collective-permute-start(f32[64,1536]{1,0:T(8,128)} %get-tuple-element.89), channel_id=1, source_target_pairs={{0,1},{1,2},{2,3},{3,0},{4,5},{5,6},{6,7},{7,4},{8,9},{9,10},{10,1... | collective-permute-start | bytes 1179656 | tf_op jit(solution)/shard_map/ppermute | solution.py:426
  22.3 41.4 %collective-permute-start.18 = (f32[2,2,32,1024]{3,2,1,0:T(8,128)}, f32[2,2,32,1024]{3,2,1,0:T(8,128)}, u32[]{:S(2)}, u32[]{:S(2)}) collective-permute-start(f32[2,2,32,1024]{3,2,1,0:T(8,128)} %collective-permute-done.17), channel_id=1, source_target_pairs={{0,1},{1,2},{2,3},{3,0},{4,5},{5,6},{6,7},{7,4},{8,9},{9,10},{10,1... | collective-permute-start | bytes 1572872 | tf_op jit(solution)/shard_map/ppermute | solution.py:426
  27.4 56.9 %collective-permute-start.32 = (f32[2,2,16,1024]{3,2,1,0:T(8,128)}, f32[2,2,16,1024]{3,2,1,0:T(8,128)}, u32[]{:S(2)}, u32[]{:S(2)}) collective-permute-start(f32[2,2,16,1024]{3,2,1,0:T(8,128)} %collective-permute-done.31), channel_id=1, source_target_pairs={{0,1},{1,2},{2,3},{3,0},{4,5},{5,6},{6,7},{7,4},{8,9},{9,10},{10,1... | collective-permute-start | bytes 786440 | tf_op jit(solution)/shard_map/ppermute | solution.py:426
  42.6 39.2 %collective-permute-start.14 = (f32[64,1024]{1,0:T(8,128)}, f32[64,1024]{1,0:T(8,128)S(1)}, u32[]{:S(2)}, u32[]{:S(2)}) collective-permute-start(f32[64,1024]{1,0:T(8,128)} %collective-permute-done.13), channel_id=1, source_target_pairs={{0,1},{1,2},{2,3},{3,0},{4,5},{5,6},{6,7},{7,4},{8,9},{9,10},{10,1... | collective-permute-start | bytes 786440 | tf_op jit(solution)/shard_map/ppermute | solution.py:426
  63.7 44.6 %collective-permute-start.19 = (f32[2,2,32,1024]{3,2,1,0:T(8,128)}, f32[2,2,32,1024]{3,2,1,0:T(8,128)S(1)}, u32[]{:S(2)}, u32[]{:S(2)}) collective-permute-start(f32[2,2,32,1024]{3,2,1,0:T(8,128)} %collective-permute-done.18), channel_id=1, source_target_pairs={{0,1},{1,2},{2,3},{3,0},{4,5},{5,6},{6,7},{7,4},{8,9},{9,10},{10,1... | collective-permute-start | bytes 1572872 | tf_op jit(solution)/shard_map/ppermute | solution.py:426
  81.8 26.3 %collective-permute-start.2 = (f32[64,1536]{1,0:T(8,128)S(1)}, f32[64,1536]{1,0:T(8,128)S(1)}, u32[]{:S(2)}, u32[]{:S(2)}) collective-permute-start(f32[64,1536]{1,0:T(8,128)S(1)} %collective-permute-done.1), channel_id=1, source_target_pairs={{0,1},{1,2},{2,3},{3,0},{4,5},{5,6},{6,7},{7,4},{8,9},{9,10},{10,1... | collective-permute-start | bytes 1179656 | tf_op jit(solution)/shard_map/ppermute | solution.py:426
  84.3 27.0 %collective-permute-start.12 = (f32[4,64,512]{2,1,0:T(8,128)S(1)}, f32[4,64,512]{2,1,0:T(8,128)S(1)}, u32[]{:S(2)}, u32[]{:S(2)}) collective-permute-start(f32[4,64,512]{2,1,0:T(8,128)S(1)} %pad_maximum_fusion.6.refs_2_), channel_id=1, source_target_pairs={{0,4},{4,0},{8,12},{12,8},{16,20},{20,16},{24,28},{28,24},{1,5},{5... | collective-permute-start | bytes 1572872 | tf_op jit(solution)/shard_map/ppermute | solution.py:411
  84.5 140.0 %collective-permute-start.33 = (f32[2,2,16,1024]{3,2,1,0:T(8,128)}, f32[2,2,16,1024]{3,2,1,0:T(8,128)}, u32[]{:S(2)}, u32[]{:S(2)}) collective-permute-start(f32[2,2,16,1024]{3,2,1,0:T(8,128)} %collective-permute-done.32), channel_id=1, source_target_pairs={{0,1},{1,2},{2,3},{3,0},{4,5},{5,6},{6,7},{7,4},{8,9},{9,10},{10,1... | collective-permute-start | bytes 786440 | tf_op jit(solution)/shard_map/ppermute | solution.py:426
  108.2 36.8 %collective-permute-start.16 = (f32[4,64,1024]{2,1,0:T(8,128)S(1)}, f32[4,64,1024]{2,1,0:T(8,128)S(1)}, u32[]{:S(2)}, u32[]{:S(2)}) collective-permute-start(f32[4,64,1024]{2,1,0:T(8,128)S(1)} %pad_maximum_fusion.3.refs_2_), channel_id=1, source_target_pairs={{0,4},{4,0},{8,12},{12,8},{16,20},{20,16},{24,28},{28,24},{1,5},{5... | collective-permute-start | bytes 3145736 | tf_op jit(solution)/shard_map/ppermute | solution.py:411
  108.3 32.9 %collective-permute-start.3 = (f32[64,1536]{1,0:T(8,128)S(1)}, f32[64,1536]{1,0:T(8,128)S(1)}, u32[]{:S(2)}, u32[]{:S(2)}) collective-permute-start(f32[64,1536]{1,0:T(8,128)S(1)} %collective-permute-done.2), channel_id=1, source_target_pairs={{0,1},{1,2},{2,3},{3,0},{4,5},{5,6},{6,7},{7,4},{8,9},{9,10},{10,1... | collective-permute-start | bytes 1179656 | tf_op jit(solution)/shard_map/ppermute | solution.py:426
  111.3 47.9 %collective-permute-start.21 = (f32[4,2,2,32,1024]{4,3,2,1,0:T(8,128)S(1)}, f32[4,2,2,32,1024]{4,3,2,1,0:T(8,128)}, u32[]{:S(2)}, u32[]{:S(2)}) collective-permute-start(f32[4,2,2,32,1024]{4,3,2,1,0:T(8,128)S(1)} %pad_maximum_fusion.1.refs_2_), channel_id=1, source_target_pairs={{0,8},{4,12},{8,0},{12,4},{16,24},{20,28},{24,16},{28,20},{1,9},{5... | collective-permute-start | bytes 6291464 | tf_op jit(solution)/shard_map/ppermute | solution.py:411
  141.2 89.5 %collective-permute-start.20 = (f32[4,2,2,32,1024]{4,3,2,1,0:T(8,128)S(1)}, f32[4,2,2,32,1024]{4,3,2,1,0:T(8,128)S(1)}, u32[]{:S(2)}, u32[]{:S(2)}) collective-permute-start(f32[4,2,2,32,1024]{4,3,2,1,0:T(8,128)S(1)} %pad_maximum_fusion.1.refs_2_), channel_id=1, source_target_pairs={{0,4},{4,0},{8,12},{12,8},{16,20},{20,16},{24,28},{28,24},{1,5},{5... | collective-permute-start | bytes 6291464 | tf_op jit(solution)/shard_map/ppermute | solution.py:411
  143.4 48.3 %collective-permute-start.4 = (f32[4,64,1536]{2,1,0:T(8,128)S(1)}, f32[4,64,1536]{2,1,0:T(8,128)S(1)}, u32[]{:S(2)}, u32[]{:S(2)}) collective-permute-start(f32[4,64,1536]{2,1,0:T(8,128)S(1)} %pad_maximum_fusion.2.refs_2_), channel_id=1, source_target_pairs={{0,4},{4,0},{8,12},{12,8},{16,20},{20,16},{24,28},{28,24},{1,5},{5... | collective-permute-start | bytes 4718600 | tf_op jit(solution)/shard_map/ppermute | solution.py:411
  145.0 58.6 %collective-permute-start.8 = (f32[4,64,2048]{2,1,0:T(8,128)}, f32[4,64,2048]{2,1,0:T(8,128)}, u32[]{:S(2)}, u32[]{:S(2)}) collective-permute-start(f32[4,64,2048]{2,1,0:T(8,128)} %pad_maximum_fusion.refs_4_), channel_id=1, source_target_pairs={{0,4},{4,0},{8,12},{12,8},{16,20},{20,16},{24,28},{28,24},{1,5},{5... | collective-permute-start | bytes 6291464 | tf_op jit(solution)/shard_map/ppermute | solution.py:411
  159.1 73.7 %collective-permute-start.22 = (f32[4,2,2,32,1024]{4,3,2,1,0:T(8,128)}, f32[4,2,2,32,1024]{4,3,2,1,0:T(8,128)}, u32[]{:S(2)}, u32[]{:S(2)}) collective-permute-start(f32[4,2,2,32,1024]{4,3,2,1,0:T(8,128)} %collective-permute-done.21.refs_4_), channel_id=1, source_target_pairs={{0,4},{4,0},{8,12},{12,8},{16,20},{20,16},{24,28},{28,24},{1,5},{5... | collective-permute-start | bytes 6291464 | tf_op jit(solution)/shard_map/ppermute | solution.py:411
  226.7 144.1 %collective-permute-start.34 = (f32[4,2,2,16,1024]{4,3,2,1,0:T(8,128)}, f32[4,2,2,16,1024]{4,3,2,1,0:T(8,128)}, u32[]{:S(2)}, u32[]{:S(2)}) collective-permute-start(f32[4,2,2,16,1024]{4,3,2,1,0:T(8,128)} %pad_maximum_fusion.4.refs_2_), channel_id=1, source_target_pairs={{0,4},{4,0},{8,12},{12,8},{16,20},{20,16},{24,28},{28,24},{1,5},{5... | collective-permute-start | bytes 3145736 | tf_op jit(solution)/shard_map/ppermute | solution.py:411
  229.2 25.6 %collective-permute-start.37 = (f32[4,2,2,16,1024]{4,3,2,1,0:T(8,128)}, f32[4,2,2,16,1024]{4,3,2,1,0:T(8,128)S(1)}, u32[]{:S(2)}, u32[]{:S(2)}) collective-permute-start(f32[4,2,2,16,1024]{4,3,2,1,0:T(8,128)} %pad_maximum_fusion.4.refs_2_), channel_id=1, source_target_pairs={{0,16},{4,20},{8,24},{12,28},{16,0},{20,4},{24,8},{28,12},{1,17},{... | collective-permute-start | bytes 3145736 | tf_op jit(solution)/shard_map/ppermute | solution.py:411
  254.9 26.4 %collective-permute-start.35 = (f32[4,2,2,16,1024]{4,3,2,1,0:T(8,128)}, f32[4,2,2,16,1024]{4,3,2,1,0:T(8,128)}, u32[]{:S(2)}, u32[]{:S(2)}) collective-permute-start(f32[4,2,2,16,1024]{4,3,2,1,0:T(8,128)} %pad_maximum_fusion.4.refs_2_), channel_id=1, source_target_pairs={{0,8},{4,12},{8,0},{12,4},{16,24},{20,28},{24,16},{28,20},{1,9},{5... | collective-permute-start | bytes 3145736 | tf_op jit(solution)/shard_map/ppermute | solution.py:411
  256.4 45.9 %collective-permute-start.39 = (f32[4,2,2,16,1024]{4,3,2,1,0:T(8,128)S(1)}, f32[4,2,2,16,1024]{4,3,2,1,0:T(8,128)}, u32[]{:S(2)}, u32[]{:S(2)}) collective-permute-start(f32[4,2,2,16,1024]{4,3,2,1,0:T(8,128)S(1)} %collective-permute-done.37.refs_6_), channel_id=1, source_target_pairs={{0,8},{4,12},{8,0},{12,4},{16,24},{20,28},{24,16},{28,20},{1,9},{5... | collective-permute-start | bytes 3145736 | tf_op jit(solution)/shard_map/ppermute | solution.py:411
  256.9 45.4 %collective-permute-start.28 = (f32[128,768]{1,0:T(8,128)S(1)}, f32[128,768]{1,0:T(8,128)S(1)}, u32[]{:S(2)}, u32[]{:S(2)}) collective-permute-start(f32[128,768]{1,0:T(8,128)S(1)} %collective-permute-done.27.refs_8_.refs_14_), channel_id=1, source_target_pairs={{0,4},{4,0},{8,12},{12,8},{16,20},{20,16},{24,28},{28,24},{1,5},{5... | collective-permute-start | bytes 1179656 | tf_op jit(solution)/shard_map/ppermute | solution.py:411
  256.9 45.9 %collective-permute-start.30 = (f32[128,1024]{1,0:T(8,128)S(1)}, f32[128,1024]{1,0:T(8,128)S(1)}, u32[]{:S(2)}, u32[]{:S(2)}) collective-permute-start(f32[128,1024]{1,0:T(8,128)S(1)} %collective-permute-done.29.refs_10_.refs_16_), channel_id=1, source_target_pairs={{0,4},{4,0},{8,12},{12,8},{16,20},{20,16},{24,28},{28,24},{1,5},{5... | collective-permute-start | bytes 1572872 | tf_op jit(solution)/shard_map/ppermute | solution.py:411
  281.3 94.3 %collective-permute-start.38 = (f32[4,2,2,16,1024]{4,3,2,1,0:T(8,128)S(1)}, f32[4,2,2,16,1024]{4,3,2,1,0:T(8,128)}, u32[]{:S(2)}, u32[]{:S(2)}) collective-permute-start(f32[4,2,2,16,1024]{4,3,2,1,0:T(8,128)S(1)} %collective-permute-done.37.refs_6_), channel_id=1, source_target_pairs={{0,4},{4,0},{8,12},{12,8},{16,20},{20,16},{24,28},{28,24},{1,5},{5... | collective-permute-start | bytes 3145736 | tf_op jit(solution)/shard_map/ppermute | solution.py:411
  302.3 71.7 %collective-permute-start.36 = (f32[4,2,2,16,1024]{4,3,2,1,0:T(8,128)}, f32[4,2,2,16,1024]{4,3,2,1,0:T(8,128)S(1)}, u32[]{:S(2)}, u32[]{:S(2)}) collective-permute-start(f32[4,2,2,16,1024]{4,3,2,1,0:T(8,128)} %collective-permute-done.35.refs_4_), channel_id=1, source_target_pairs={{0,4},{4,0},{8,12},{12,8},{16,20},{20,16},{24,28},{28,24},{1,5},{5... | collective-permute-start | bytes 3145736 | tf_op jit(solution)/shard_map/ppermute | solution.py:411
  302.3 77.8 %collective-permute-start.40 = (f32[4,2,2,16,1024]{4,3,2,1,0:T(8,128)}, f32[4,2,2,16,1024]{4,3,2,1,0:T(8,128)}, u32[]{:S(2)}, u32[]{:S(2)}) collective-permute-start(f32[4,2,2,16,1024]{4,3,2,1,0:T(8,128)} %collective-permute-done.39.refs_8_), channel_id=1, source_target_pairs={{0,4},{4,0},{8,12},{12,8},{16,20},{20,16},{24,28},{28,24},{1,5},{5... | collective-permute-start | bytes 3145736 | tf_op jit(solution)/shard_map/ppermute | solution.py:411
  (96 other events, 2693.6 us)

commit v3 on v2

--- a/solution.py
+++ b/solution.py
@@ -28,73 +28,131 @@
     return one(left_high, right_high) + (one(left_high, right_low) + one(left_low, right_high))
 
 
-def invert_block(block, inverse_ref):
+def invert_block(block, inverse_ref, spare_ref):
     count = BLK // SUB
     shape = (SUB, BLK)
     rows = [block[SUB * m : SUB * m + SUB] for m in range(count)]
     lane = lax.broadcasted_iota(jnp.int32, shape, 1)
     sublane = lax.broadcasted_iota(jnp.int32, shape, 0)
-    unit = [(lane == sublane + SUB * m).astype(jnp.float32) for m in range(count)]
+
+    def columns(m, base):
+        return [jnp.broadcast_to(rows[m][:, base + j : base + j + 1], shape) for j in range(SUB)]
+
+    def put(slot, value):
+        spare_ref[SUB * slot : SUB * slot + SUB, :] = value
+
+    def get(slot, i):
+        return spare_ref[pl.ds(SUB * slot + i, SUB, stride=0), :]
+
+    pivot_slot, next_slot, row_slot = 0, 2 * SUB, 4 * SUB
+    for j, value in enumerate(columns(0, 0)):
+        put(pivot_slot + j, value)
     for k in range(count):
         base = SUB * k
-        cols = [jnp.broadcast_to(rows[k][:, base + j : base + j + 1], shape) for j in range(SUB)]
-        d = [[jnp.broadcast_to(cols[j][i : i + 1], shape) for j in range(i + 1)] for i in range(SUB)]
-        ya = [jnp.broadcast_to(rows[k][j : j + 1], shape) for j in range(SUB)]
-        ye = [jnp.broadcast_to(unit[k][j : j + 1], shape) for j in range(SUB)]
+        turn = k % 2 * SUB
+        last = k == count - 1
+        d = [[get(pivot_slot + turn + j, i) for j in range(i + 1)] for i in range(SUB)]
+        inside = (lane >= base) & (lane < base + SUB)
+        unit = (lane == sublane + base).astype(jnp.float32)
+        put(row_slot + k % 2, jnp.where(inside, unit, rows[k]))
+        y = [get(row_slot + k % 2, j) for j in range(SUB)]
+        if not last:
+            g = columns(k + 1, base)
+            ahead = columns(k + 1, base + SUB)
         f = [[None] * SUB for _ in range(SUB)]
-        reciprocal = [None] * SUB
+        inverse = [None] * SUB
+        for c in range(0, SUB, 2):
+            e = c + 1
+            p, q, r = d[c][c], d[e][c], d[e][e]
+            inverse[c] = 1.0 / p
+            both = 1.0 / (p * r - q * q)
+            inverse[e] = p * both
+            f[e][c] = q * inverse[c]
+            h = {}
+            for i in range(e + 1, SUB):
+                f[i][c] = d[i][c] * inverse[c]
+                h[i] = p * d[i][e] - q * d[i][c]
+                f[i][e] = h[i] * both
+            for i in range(e + 1, SUB):
+                w = r * d[i][c] - q * d[i][e]
+                for j in range(e + 1, i + 1):
+                    d[i][j] = d[i][j] - (w * d[j][c] + h[i] * d[j][e]) * both
+            for x in (c, e):
+                if not last:
+                    put(next_slot + turn + x, g[x])
+                    scaled = g[x] * inverse[x]
+                    for j in range(SUB):
+                        ahead[j] = ahead[j] - scaled * get(next_slot + turn + x, j)
+                for i in range(x + 1, SUB):
+                    if not last:
+                        g[i] = g[i] - f[i][x] * g[x]
+                    y[i] = y[i] - f[i][x] * y[x]
+        keep = lane[0:1] < base + SUB
         for c in range(SUB):
-            reciprocal[c] = 1.0 / d[c][c]
-            for i in range(c + 1, SUB):
-                f[i][c] = d[i][c] * reciprocal[c]
-            for i in range(c + 1, SUB):
-                for j in range(c + 1, i + 1):
-                    d[i][j] = d[i][j] - (d[i][c] * d[j][c]) * reciprocal[c]
-            for i in range(c + 1, SUB):
-                ya[i] = ya[i] - f[i][c] * ya[c]
-                ye[i] = ye[i] - f[i][c] * ye[c]
-            inverse_ref[base + c : base + c + 1, :] = (lax.rsqrt(d[c][c]) * ye[c])[0:1]
-        if k == count - 1:
+            row = (lax.rsqrt(inverse[c]) * inverse[c] * y[c])[0:1]
+            inverse_ref[base + c : base + c + 1, :] = jnp.where(keep, row, 0.0)
+        if last:
             break
-        za = [y * r for y, r in zip(ya, reciprocal)]
-        ze = [y * r for y, r in zip(ye, reciprocal)]
-        for i in reversed(range(SUB)):
-            for c in range(i):
-                za[c] = za[c] - f[i][c] * za[i]
-                ze[c] = ze[c] - f[i][c] * ze[i]
+        for j in range(SUB):
+            put(pivot_slot + SUB - turn + j, ahead[j])
+        if k + 2 < count:
+            z = [a * b for a, b in zip(y, inverse)]
+            for i in reversed(range(SUB)):
+                for c in range(i):
+                    z[c] = z[c] - f[i][c] * z[i]
         for m in range(k + 1, count):
-            col = [jnp.broadcast_to(rows[m][:, base + j : base + j + 1], shape) for j in range(SUB)]
-            pa = [c * z for c, z in zip(col, za)]
-            pe = [c * z for c, z in zip(col, ze)]
-            while len(pa) > 1:
-                pa = [x + y for x, y in zip(pa[::2], pa[1::2])]
-                pe = [x + y for x, y in zip(pe[::2], pe[1::2])]
-            rows[m] = rows[m] - pa[0]
-            unit[m] = unit[m] - pe[0]
-
-
-def factor_in_place(work_ref, block_ref, factor_ref, first_column, inverse_ref):
+            cleared = jnp.where(inside, 0.0, rows[m])
+            if m == k + 1:
+                for c in range(SUB):
+                    cleared = cleared - (g[c] * y[c]) * inverse[c]
+            else:
+                terms = [a * b for a, b in zip(columns(m, base), z)]
+                while len(terms) > 1:
+                    terms = [a + b for a, b in zip(terms[::2], terms[1::2])]
+                cleared = cleared - terms[0]
+            rows[m] = cleared
+
+
+def factor_in_place(work_ref, block_ref, spare_ref, factor_ref, first_column, inverse_ref):
     size = work_ref.shape[0]
-    row = lax.broadcasted_iota(jnp.int32, (size, size), 0)
-    column = lax.broadcasted_iota(jnp.int32, (size, size), 1)
-    work_ref[:, size:] = (row == column).astype(jnp.float32)
-    row = lax.broadcasted_iota(jnp.int32, (size, BLK), 0)
-    column = lax.broadcasted_iota(jnp.int32, (size, BLK), 1)
+    steps = size // BLK
+    row = lax.broadcasted_iota(jnp.int32, (BLK, BLK), 0)
+    column = lax.broadcasted_iota(jnp.int32, (BLK, BLK), 1)
 
     def step(index, carry):
         base = pl.multiple_of(index * BLK, BLK)
-        invert_block(work_ref[pl.ds(base, BLK), pl.ds(base, BLK)], block_ref)
-        block = block_ref[...]
-        below = product_3(work_ref[:, pl.ds(base, BLK)], block, transposed=True)
-        right = product_3(block, work_ref[pl.ds(base, BLK), :])
-        below = jnp.where(row >= column + base, below, 0.0)
-        factor_ref[:, pl.ds(pl.multiple_of(first_column + base, BLK), BLK)] = below
-        inverse_ref[pl.ds(base, BLK), :] = right[:, size:]
-        below = jnp.where(row >= base + BLK, below, 0.0)
-        work_ref[...] = work_ref[...] - product_3(below, right)
+        invert_block(work_ref[pl.ds(base, BLK), pl.ds(base, BLK)], block_ref, spare_ref)
+        for now in range(steps):
+
+            @pl.when(index == now)
+            def _():
+                low, high = now * BLK, now * BLK + BLK
+                block = block_ref[...]
+                below = product_3(work_ref[low:, low:high], block, True)
+                if now:
+                    factor_ref[0:low, first_column + low : first_column + high] = jnp.zeros(
+                        (low, BLK), jnp.float32
+                    )
+                factor_ref[low:high, first_column + low : first_column + high] = jnp.where(
+                    row >= column, below[:BLK], 0.0
+                )
+                inverse_ref[low:high, low:high] = block
+                if high < size:
+                    inverse_ref[low:high, high:] = jnp.zeros((BLK, size - high), jnp.float32)
+                    below = below[BLK:]
+                    factor_ref[high:, first_column + low : first_column + high] = below
+                    right = product_3(block, work_ref[low:high, high:])
+                    work_ref[high:, high:] = work_ref[high:, high:] - product_3(below, right)
+                    work_ref[high:, low:high] = -product_3(below, block)
+                if now:
+                    left = product_3(block, work_ref[low:high, :low])
+                    inverse_ref[low:high, :low] = left
+                    if high < size:
+                        work_ref[high:, :low] = work_ref[high:, :low] - product_3(below, left)
+
         return carry
 
-    lax.fori_loop(0, size // BLK, step, 0)
+    lax.fori_loop(0, steps, step, 0)
 
 
 def start_copies(plan, position_ref, source, blocks, portion, width, first, target_ref, sems):
@@ -102,7 +160,9 @@
     rows = plan["piece_rows"]
     members = 2 ** plan["height"]
     for order, block in enumerate(blocks):
-        slot = position_ref[block % plan["front_count"]]
+        slot = block % plan["front_count"]
+        if plan["where"][(portion, block // plan["front_count"])][0] in plan["direct"]:
+            slot = position_ref[slot]
         for member in range(members):
             place = position_ref[plan["front_count"] + member]
             start = pl.multiple_of(order * BLK + place * rows, rows)
@@ -138,14 +198,19 @@
     return total.T if flip else total
 
 
+def stack_index(member, height):
+    return sum((member >> bit & 1) << height - 1 - bit for bit in range(1, height))
+
+
 def make_source(plan, refs):
-    if plan["height"] == 1:
-        return lambda member, portion, block, slot: refs[
-            (portion, block // plan["front_count"], member)
-        ].at[slot]
-    return lambda member, portion, block, slot: refs[member].at[
-        slot, portion, block // plan["front_count"]
-    ]
+    height = plan["height"]
+
+    def source(member, portion, block, slot):
+        group, index = plan["where"][(portion, block // plan["front_count"])]
+        ref = refs[(group, member & 1)].at[stack_index(member, height), slot]
+        return ref if index is None else ref.at[index]
+
+    return source
 
 
 def unpack(plan, refs, portions, blocks, strips):
@@ -163,11 +228,9 @@
 
 
 def piece_names(plan, portions, blocks):
-    members = range(2 ** plan["height"])
-    if plan["height"] > 1:
-        return list(members)
     slabs = sorted({block // plan["front_count"] for block in blocks})
-    return [(p, t, m) for p in portions for t in slabs for m in members]
+    groups = sorted({plan["where"][(p, t)][0] for p in portions for t in slabs})
+    return [(group, c) for group in groups for c in (0, 1)]
 
 
 def leading(plan, state, portions, blocks, strips):
@@ -199,7 +262,7 @@
     def kernel(*refs):
         position_ref, mask_ref, source, children, refs = unpack(plan, refs, (0,), blocks, strips)
         old_factors, old_inverses = refs[:chunk], refs[chunk : 2 * chunk]
-        factor_ref, inverse_ref, rows_ref, work_ref, block_ref, sems = refs[2 * chunk :]
+        factor_ref, inverse_ref, rows_ref, work_ref, block_ref, spare_ref, sems = refs[2 * chunk :]
         copies = start_copies(plan, position_ref, source, blocks, 0, width, 0, rows_ref, sems)
         for copy in copies:
             copy.wait()
@@ -209,8 +272,6 @@
                     weights = [
                         mask_ref[c * PIVOT_BLOCKS + i] * mask_ref[c * PIVOT_BLOCKS + j] for c in (0, 1)
                     ]
-                    if i // 2 < j // 2 and (i // 2) * STRIP + STRIP <= low:
-                        continue
                     rows_ref[pl.ds(order * BLK, BLK), pl.ds(j * BLK, BLK)] += child_sum(
                         children, i, j, weights
                     )
@@ -226,10 +287,10 @@
         if chunk:
             done = factor_ref[:, pl.ds(0, low)]
             corner = corner - product_3(done, done, True)
-        work_ref[:, pl.ds(0, size)] = corner
+        work_ref[...] = corner
         if width < plan["pivot_size"]:
             factor_ref[:, width:] = jnp.zeros((size, plan["pivot_size"] - width), jnp.float32)
-        factor_in_place(work_ref, block_ref, factor_ref, low, inverse_ref)
+        factor_in_place(work_ref, block_ref, spare_ref, factor_ref, low, inverse_ref)
 
     operands, specs = leading(plan, state, (0,), blocks, strips)
     vmem = pl.BlockSpec(memory_space=pltpu.VMEM)
@@ -245,8 +306,9 @@
         out_specs=[vmem, vmem],
         scratch_shapes=[
             pltpu.VMEM((size, width), jnp.float32),
-            pltpu.VMEM((size, 2 * size), jnp.float32),
+            pltpu.VMEM((size, size), jnp.float32),
             pltpu.VMEM((BLK, BLK), jnp.float32),
+            pltpu.VMEM((SUB * (4 * SUB + 2), BLK), jnp.float32),
             pltpu.SemaphoreType.DMA((len(blocks) * 2 ** plan["height"],)),
         ],
         compiler_params=pltpu.CompilerParams(vmem_limit_bytes=48 * 2**20),
@@ -399,7 +461,7 @@
         ],
         compiler_params=pltpu.CompilerParams(vmem_limit_bytes=56 * 2**20),
         cost_estimate=pl.CostEstimate(
-            flops=8_000_000_000 * size // 1024, bytes_accessed=8 * size * pivot_size, transcendentals=0
+            flops=20_000_000_000 * size // 1024, bytes_accessed=8 * size * pivot_size, transcendentals=0
         ),
         name=f"panel_{strips[0]}",
     )(*operands)
@@ -418,20 +480,18 @@
     return result
 
 
-def ring_front(value):
+def all_front(value):
     count = lax.axis_size("front")
-    pairs = [(source, (source + 1) % count) for source in range(count)]
     slots = [value]
-    for _ in range(count - 1):
-        slots.append(lax.ppermute(slots[-1], "front", pairs))
+    for mask in range(1, count):
+        pairs = [(source, source ^ mask) for source in range(count)]
+        slots.append(lax.ppermute(value, "front", pairs))
     return jnp.stack(slots)
 
 
-def gather_pieces(value, height):
-    arrays = {0: ring_front(value)}
-    for bit in reversed(range(height)):
-        arrays.update({m | 1 << bit: partner_2(a, "leaf", bit) for m, a in list(arrays.items())})
-    return [arrays[m] for m in range(2**height)]
+def after(value, done):
+    corner = done.reshape(-1)[:1]
+    return value + jnp.where(corner > jnp.inf, 1.0, 0.0).reshape((1,) * value.ndim)
 
 
 def local(
@@ -451,20 +511,28 @@
     core = leaf_index & 1
     my_blocks = front_index + front_count * jnp.arange(slabs, dtype=jnp.int32)
     chunks = [(0, STRIP), (STRIP, 2 * STRIP), (2 * STRIP, pivot_size)]
-    results = []
-    schur = None
+    plans, states, entry_slabs = {}, {}, {}
+    names = [(p, t) for p in (0, 1) for t in range(slabs)]
+    where = {
+        1: {name: (order, None) for order, name in enumerate(names)},
+        2: {(p, t): (slabs, t) if p else (t, None) for p, t in names},
+        3: {(p, t): (p * slabs + t, None) for p, t in names},
+    }
+    direct = {1: (0,), 2: range(slabs), 3: range(2 * slabs)}
     for height, entries, routes in (
         (1, entries_lower, assembly_lower),
         (2, entries_middle, assembly_middle),
         (3, entries_upper, assembly_upper),
     ):
         piece_rows = BLK // 2**height
-        plan = dict(
+        plans[height] = dict(
             height=height,
             piece_rows=piece_rows,
             front_count=front_count,
             pivot_size=pivot_size,
             chunks=chunks,
+            where=where[height],
+            direct=direct[height],
         )
         child_bit = leaf_index >> height - 1 & 1
         route_pair = lax.dynamic_index_in_dim(routes, leaf_index >> height, 0, keepdims=False)
@@ -472,7 +540,7 @@
         masks = jnp.where(child_bit == 0, pivot_masks, pivot_masks[::-1])
         position = jnp.concatenate(
             [
-                (front_index - jnp.arange(front_count, dtype=jnp.int32)) % front_count,
+                front_index ^ jnp.arange(front_count, dtype=jnp.int32),
                 jnp.stack(
                     [
                         reversed_bits((leaf_index ^ m) & 2**height - 1, height)
@@ -482,68 +550,199 @@
                 ),
             ]
         ).astype(jnp.int32)
-        state = dict(position=position, masks=masks.reshape(-1))
-        local_entries = entries.reshape(2, slabs, piece_rows, pivot_size)
-        if height == 1:
-            update = leaf_contrib.reshape(slabs, BLK, pivot_size)
-            low_rows, high_rows = update[:, :piece_rows], update[:, piece_rows:]
-            kept = jnp.where(child_bit == 0, low_rows, high_rows)
-            outgoing = jnp.where(child_bit == 0, high_rows, low_rows)
-            received = partner_2(outgoing, "leaf", 0)
-            row_masks = masks[:, my_blocks]
-            spread = jnp.repeat(masks, BLK, axis=1)
-
-            def term(slab, width, row_pivot, column_pivot):
-                total = 0.0
-                for child, rows in enumerate((kept, received)):
-                    row = row_masks[child, slab] if row_pivot else 1.0 - row_masks[child, slab]
-                    column = spread[child] if column_pivot else 1.0 - spread[child]
-                    total = total + rows[slab, :, :width] * (row * column[:width])[None]
-                return total
-
-            state["pieces"] = {}
-            for slab in range(slabs):
-                width = (slab + 1) * front_count * BLK
-                value = local_entries[0, slab, :, :width] + term(slab, width, True, True)
-                for m, array in enumerate(gather_pieces(value, height)):
-                    state["pieces"][(0, slab, m)] = array
-            for slab in range(slabs):
-                width = (slab + 1) * front_count * BLK
-                value = jnp.concatenate(
-                    [
-                        local_entries[1, slab] + term(slab, pivot_size, False, True),
-                        term(slab, width, False, False),
-                    ],
-                    axis=1,
-                )
-                for m, array in enumerate(gather_pieces(value, height)):
-                    state["pieces"][(1, slab, m)] = array
-        else:
-            state["pieces"] = dict(enumerate(gather_pieces(local_entries, height)))
-            state["own"] = schur
-            state["other"] = []
-            for strip in schur:
-                half = lax.dynamic_slice_in_dim(strip, core * BLK, BLK, 0)
-                mine = partner_2(half, "leaf", height - 1)
-                state["other"].append((mine, partner_2(mine, "leaf", 0)))
-        factors, inverses = [], []
-        for chunk in range(len(chunks)):
-            factor, inverse = factor_chunk(plan, state, chunk, factors, inverses)
-            factors.append(factor)
-            inverses.append(inverse)
-        strips = list(range(pivot_size // STRIP))
-        if height < 3:
-            panel, first_strip = panel_and_schur(
-                plan, state, strips[:1], factors, inverses, None, False
-            )
-            _, *others, own = panel_and_schur(
-                plan, state, strips[1:], factors, inverses, panel, False
-            )
-            schur = [first_strip] + others
-        else:
-            _, top, own = panel_and_schur(plan, state, strips, factors, inverses, None, True)
-        results.append(own)
-    return (results[0], results[1], results[2], top)
+        states[height] = dict(position=position, masks=masks.reshape(-1), pieces={})
+        entry_slabs[height] = entries.reshape(2, slabs, piece_rows, pivot_size)
+
+    piece_rows = BLK // 2
+    update = leaf_contrib.reshape(slabs, BLK, pivot_size)
+    low_rows, high_rows = update[:, :piece_rows], update[:, piece_rows:]
+    kept = jnp.where(core == 0, low_rows, high_rows)
+    received = partner_2(jnp.where(core == 0, high_rows, low_rows), "leaf", 0)
+    masks = states[1]["masks"].reshape(2, PIVOT_BLOCKS)
+    row_masks = masks[:, my_blocks]
+    spread = jnp.repeat(masks, BLK, axis=1)
+
+    def term(slab, width, row_pivot, column_pivot):
+        total = 0.0
+        for child, rows in enumerate((kept, received)):
+            row = row_masks[child, slab] if row_pivot else 1.0 - row_masks[child, slab]
+            column = spread[child] if column_pivot else 1.0 - spread[child]
+            total = total + rows[slab, :, :width] * (row * column[:width])[None]
+        return total
+
+    def slab_width(slab):
+        return (slab + 1) * front_count * BLK
+
+    lower_values = {}
+    for slab in range(slabs):
+        width = slab_width(slab)
+        lower_values[(0, slab)] = entry_slabs[1][0, slab, :, :width] + term(slab, width, True, True)
+        lower_values[(1, slab)] = jnp.concatenate(
+            [
+                entry_slabs[1][1, slab] + term(slab, pivot_size, False, True),
+                term(slab, width, False, False),
+            ],
+            axis=1,
+        )
+
+    for height in (2, 3):
+        states[height]["own"], states[height]["other"] = {}, {}
+    factors = {1: [], 2: [], 3: []}
+    inverses = {1: [], 2: [], 3: []}
+    now = [leaf_contrib]
+
+    def ready(value):
+        return lax.optimization_barrier((value, now[0]))[0]
+
+    def end_step(*results):
+        now[0] = results
+
+    def gather(value):
+        return lax.all_gather(ready(value), "front")
+
+    def across(value, bit):
+        value = ready(value)
+        return value, partner_2(value, "leaf", bit)
+
+    def joined(pair):
+        return jnp.concatenate(pair, axis=0)
+
+    def place(height, group, stack):
+        stack = ready(stack)
+        pieces = (stack, partner_2(stack, "leaf", 0))
+        for index, piece in enumerate(pieces):
+            states[height]["pieces"][(group, index)] = piece
+        return pieces[1]
+
+    def offer(height, strip):
+        half = lax.dynamic_slice_in_dim(states[height]["own"][strip], core * BLK, BLK, 0)
+        return partner_2(ready(half), "leaf", height - 1)
+
+    def swap(height, strip, mine):
+        theirs = partner_2(ready(mine), "leaf", 0)
+        states[height]["other"][strip] = (mine, theirs)
+        return theirs
+
+    def factor(height, chunk):
+        states[height]["position"] = ready(states[height]["position"])
+        one, other = factor_chunk(
+            plans[height], states[height], chunk, factors[height], inverses[height]
+        )
+        factors[height].append(one)
+        inverses[height].append(other)
+        return other
+
+    def panel(height, strips, before, last=False):
+        states[height]["position"] = ready(states[height]["position"])
+        outputs = panel_and_schur(
+            plans[height], states[height], strips, factors[height], inverses[height], before, last
+        )
+        if not last:
+            for strip, value in zip(strips, outputs[1:]):
+                states[height + 1]["own"][strip] = value
+        return outputs
+
+    strips = list(range(pivot_size // STRIP))
+    later = range(1, slabs)
+    middle = all_front(entry_slabs[2][0, 0, :, : slab_width(0)])[None]
+    first = all_front(lower_values[(0, 0)])
+    end_step(middle, first)
+    end_step(place(1, 0, first[None]))
+
+    pair = across(middle, 1)
+    pivots = [gather(after(lower_values[(0, t)], first)) for t in later]
+    end_step(factor(1, 0), pair)
+
+    taken = place(2, 0, joined(pair))
+    updates = [gather(lower_values[(1, 0)])]
+    end_step(factor(1, 1), taken)
+
+    end_step(*[place(1, t, ready(value)[None]) for t, value in zip(later, pivots)])
+
+    updates += [gather(lower_values[(1, t)]) for t in later]
+    end_step(factor(1, 2))
+
+    middle_update = gather(entry_slabs[2][1])
+    end_step(place(1, slabs, ready(updates[0])[None]))
+
+    panel_0, _ = panel(1, [0], None)
+    end_step(panel_0)
+
+    mine_0 = offer(2, 0)
+    panel_1, _ = panel(1, [1], panel_0)
+    end_step(panel_1, mine_0)
+
+    end_step(swap(2, 0, mine_0))
+
+    mine_1 = offer(2, 1)
+    middle = [all_front(ready(entry_slabs[2][0, t]))[None] for t in later]
+    end_step(factor(2, 0), mine_1, middle)
+
+    taken = swap(2, 1, mine_1)
+    end_step(taken)
+
+    pairs = [across(value, 1) for value in middle]
+    taken = [place(1, slabs + t, ready(updates[t])[None]) for t in later]
+    end_step(factor(2, 1), pairs, taken)
+
+    taken = [place(2, t, joined(pair)) for t, pair in zip(later, pairs)]
+    upper = [all_front(ready(entry_slabs[3][0, t]))[None] for t in range(slabs)]
+    before = jnp.concatenate([panel_0, panel_1], axis=0)
+    panel_2, _ = panel(1, [2], before)
+    end_step(panel_2, taken, upper)
+
+    mine_2 = offer(2, 2)
+    upper_update = [all_front(ready(entry_slabs[3][1, t]))[None] for t in range(slabs)]
+    before = jnp.concatenate([before, panel_2], axis=0)
+    panel_3, _, lower_own = panel(1, [3], before)
+    end_step(panel_3, mine_2, upper_update)
+
+    mine_3 = offer(2, 3)
+    taken = swap(2, 2, mine_2)
+    end_step(mine_3, taken)
+    end_step(swap(2, 3, mine_3))
+
+    pair = across(middle_update[None], 1)
+    pairs = [across(value, 2) for value in upper + upper_update]
+    end_step(factor(2, 2), pair, pairs)
+
+    taken = place(2, slabs, joined(pair))
+    upper = [joined(pair) for pair in pairs]
+    end_step(taken, upper)
+
+    panel_0, _ = panel(2, [0], None)
+    end_step(panel_0)
+
+    mine_0 = offer(3, 0)
+    panel_1, _ = panel(2, [1], panel_0)
+    end_step(panel_1, mine_0)
+
+    mine_1 = offer(3, 1)
+    taken = swap(3, 0, mine_0)
+    pair = across(upper[0], 1)
+    before = jnp.concatenate([panel_0, panel_1], axis=0)
+    _, _, _, middle_own = panel(2, [2, 3], before)
+    end_step(middle_own, mine_1, taken, pair)
+
+    taken = place(3, 0, joined(pair)), swap(3, 1, mine_1)
+    end_step(taken)
+
+    mine_2, mine_3 = offer(3, 2), offer(3, 3)
+    pairs = [across(upper[t], 1) for t in later]
+    end_step(factor(3, 0), mine_2, mine_3, pairs)
+
+    taken = swap(3, 2, mine_2), swap(3, 3, mine_3)
+    taken += tuple(place(3, t, joined(pair)) for t, pair in zip(later, pairs))
+    pair = across(upper[slabs], 1)
+    end_step(factor(3, 1), taken, pair)
+
+    taken = place(3, slabs, joined(pair))
+    pairs = [across(upper[slabs + t], 1) for t in later]
+    end_step(factor(3, 2), taken, pairs)
+
+    end_step(*[place(3, slabs + t, joined(pair)) for t, pair in zip(later, pairs)])
+    _, top, upper_own = panel(3, strips, None, True)
+    return (lower_own, middle_own, upper_own, top)
 
 
 def solution(mesh):

time: 478 us -> 445 us (0.931)
  Pallas kernels: 261 us -> 203 us
  waiting for transfers between devices: 132 us -> 91.5 us
  local copies, waits for them, and re-layouts: 19.7 us -> 39.5 us
  starting transfers between devices: 37.3 us -> 55.7 us
  between operations: 4.59 us -> 18.6 us
  other arithmetic: 17.3 us -> 28.3 us
    pallas_call x9, Pallas kernels: 184 us -> 109 us  [factor_chunk(): pl.pallas_call(kernel, out_shape=[jax.ShapeDtypeStruct((size, plan['pivot...]
    ppermute x18 -> x21, waiting for transfers between devices: 71.9 us -> 23.2 us  [all_front(): slots.append(lax.ppermute(value, 'front', pairs))]
    all_gather x0 -> x4, waiting for transfers between devices: none -> 34.3 us  [gather(): return lax.all_gather(ready(value), 'front')]
    ppermute x31 -> x39, waiting for transfers between devices: 59.7 us -> 33.9 us  [partner_2(): return lax.ppermute(value, axis, pairs)]
    pallas_call x5 -> x8, Pallas kernels: 76.5 us -> 94.4 us  [panel_and_schur(): pl.pallas_call(kernel, out_shape=[jax.ShapeDtypeStruct(shape, jnp.float32...]
    unnamed x142 -> x159, local copies, waits for them, and re-layouts: 8.6 us -> 22 us
    concatenate x0 -> x12, other arithmetic: none -> 13 us  [the longest x2 4.52 us: local(): before = jnp.concatenate([panel_0, panel_1], axis=0)]
    ppermute x18 -> x21, starting transfers between devices: 20.4 us -> 32.2 us  [all_front(): slots.append(lax.ppermute(value, 'front', pairs))]
  transfers between devices with their start and end apart: 49 -> 64, of which waited for: 14 -> 23; matrix products, arithmetic and copies ran while one was open for 6% -> 11% of each run, Pallas kernels for 44% -> 40%
where the time goes in v3:
time: 445 us; the launch traced here: 437 us
  Pallas kernels  203 us (46%)
  waiting for transfers between devices  91.5 us (21%)
  starting transfers between devices  55.7 us (13%)
  local copies, waits for them, and re-layouts  39.5 us (9%)
  other arithmetic  28.3 us (6%)
  between operations  18.6 us (4%)
    pallas_call x9, Pallas kernels, factor_chunk(): pl.pallas_call(kernel, out_shape=[jax.ShapeDtypeStruct((size, plan['pivot...  109 us
    pallas_call x8, Pallas kernels, panel_and_schur(): pl.pallas_call(kernel, out_shape=[jax.ShapeDtypeStruct(shape, jnp.float32...  94.4 us
    all_gather x4, waiting for transfers between devices, gather(): return lax.all_gather(ready(value), 'front')  34.3 us
    ppermute x39, waiting for transfers between devices, partner_2(): return lax.ppermute(value, axis, pairs)  33.9 us
    ppermute x21, starting transfers between devices, all_front(): slots.append(lax.ppermute(value, 'front', pairs))  32.2 us
    ppermute x21, waiting for transfers between devices, all_front(): slots.append(lax.ppermute(value, 'front', pairs))  23.2 us
    ppermute x39, starting transfers between devices, partner_2(): return lax.ppermute(value, axis, pairs)  22.8 us
    unnamed x159, local copies, waits for them, and re-layouts  22 us
  transfers between devices with their start and end apart: 64, of which 23 were waited for; matrix products, arithmetic and copies ran while one was open for 11% of the time, Pallas kernels for 40%

profile of v3, /device:TPU:0, one launch (start us, length us, event | category | flops | bytes accessed | tf_op | source)
XLA Modules:
  0.0 437.0 jit_solution(10100373543952594289)
XLA Ops:
  34.1 6.0 %collective-permute-done.2 = f32[64,512]{1,0:T(8,128)S(1)} collective-permute-done((f32[64,512]{1,0:T(8,128)S(1)}, f32[64,512]{1,0:T(8,128)S(1)}, u32[]{:S(2)}, u32[]{:S(2)}) %collective-permute-start.2) | collective-permute-done | bytes 131104 | tf_op jit(solution)/shard_map/ppermute | solution.py:488
  45.6 6.7 %factor_chunk_0.3 = (f32[256,1024]{1,0:T(8,128)S(1)}, f32[256,256]{1,0:T(8,128)S(1)}) custom-call(s32[9]{0:T(128)S(1)} %concatenate.58.refs_0_, f32[16]{0:T(128)S(1)} %reshape.220.refs_1_, f32[1,4,64,512]{3,2,1,0:T(8,128)S(1)} %get-tuple-element.107.refs_2_, f32[1,4,64,512]{3,2,1,0:T(8,128)S(1)} %collective-permute-done.7.refs_3_), custom_call_target="tpu_custom_call" | custom-call | flops 15000000512 | bytes 524288 | tf_op jit(solution)/shard_map/factor_chunk_0/pallas_call | solution.py:299
  54.0 8.0 %factor_chunk_1.3 = (f32[256,1024]{1,0:T(8,128)S(1)}, f32[256,256]{1,0:T(8,128)S(1)}) custom-call(s32[9]{0:T(128)S(1)} %concatenate.58.refs_0_, f32[16]{0:T(128)S(1)} %reshape.220.refs_1_, f32[1,4,64,512]{3,2,1,0:T(8,128)S(1)} %get-tuple-element.107.refs_2_, f32[1,4,64,512]{3,2,1,0:T(8,128)S(1)} %collective-permute-done.7.refs_3_, ...), custom_call_target="tpu_custom_call" | custom-call | flops 15000000512 | bytes 1048576 | tf_op jit(solution)/shard_map/factor_chunk_1/pallas_call | solution.py:299
  63.7 10.6 %all-gather.9.cloned.1.call-done = f32[256,1024]{1,0:T(8,128)} async-done(((f32[64,1024]{1,0:T(8,128)}), f32[256,1024]{1,0:T(8,128)}) %all-gather.9.cloned.1.call-update) | async-done | bytes 1048592 | tf_op jit(solution)/shard_map/all_gather | solution.py:601
  81.7 18.2 %factor_chunk_2.3 = (f32[512,1024]{1,0:T(8,128)}, f32[512,512]{1,0:T(8,128)S(1)}) custom-call(s32[9]{0:T(128)S(1)} %concatenate.58.refs_0_, f32[16]{0:T(128)S(1)} %reshape.220.refs_1_, f32[1,4,64,1024]{3,2,1,0:T(8,128)S(1)} %bitcast.191, f32[1,4,64,1024]{3,2,1,0:T(8,128)S(1)} %collective-permute-done.10.refs_3_, f32[256,1024]{1,0:T(8,128)S(1)} %copy-done.39, ...), custom_call_target="tpu_custom_call" | custom-call | flops 30000001024 | bytes 4194304 | tf_op jit(solution)/shard_map/factor_chunk_2/pallas_call | solution.py:299
  100.9 12.0 %all-gather.11.cloned.1.call-done = f32[256,1536]{1,0:T(8,128)} async-done(((f32[64,1536]{1,0:T(8,128)}), f32[256,1536]{1,0:T(8,128)}) %all-gather.11.cloned.1.call-update) | async-done | bytes 1572880 | tf_op jit(solution)/shard_map/all_gather | solution.py:601
  116.6 8.2 %panel_0.3 = (f32[256,1024]{1,0:T(8,128)}, f32[256,256]{1,0:T(8,128)}) custom-call(s32[9]{0:T(128)} %copy-done.6, f32[16]{0:T(128)} %copy-done.27, f32[1,4,64,1536]{3,2,1,0:T(8,128)} %bitcast.233, f32[1,4,64,1536]{3,2,1,0:T(8,128)} %collective-permute-done.11.refs_3_, f32[256,1024]{1,0:T(8,128)} %copy-done.38, f32[256,1024]{1,0:T(8,128)} %copy-done.40, ...), custom_call_target="tpu_custom_call" | custom-call | flops 5000000000 | bytes 2097152 | tf_op jit(solution)/shard_map/panel_0/pallas_call | solution.py:451
  127.4 8.7 %panel_1.2 = (f32[256,1024]{1,0:T(8,128)}, f32[256,512]{1,0:T(8,128)}) custom-call(s32[9]{0:T(128)} %copy-done.6, f32[16]{0:T(128)} %copy-done.27, f32[1,4,64,1536]{3,2,1,0:T(8,128)} %bitcast.234, f32[1,4,64,1536]{3,2,1,0:T(8,128)} %collective-permute-done.11.refs_3_, f32[256,1024]{1,0:T(8,128)} %copy-done.38, f32[256,1024]{1,0:T(8,128)} %copy-done.40, ...), custom_call_target="tpu_custom_call" | custom-call | flops 5000000000 | bytes 2097152 | tf_op jit(solution)/shard_map/panel_1/pallas_call | solution.py:451
  142.5 7.0 %factor_chunk_0.4 = (f32[256,1024]{1,0:T(8,128)S(1)}, f32[256,256]{1,0:T(8,128)S(1)}) custom-call(s32[11]{0:T(128)S(1)} %concatenate.61.refs_0_, f32[16]{0:T(128)S(1)} %reshape.222.refs_1_, f32[2,4,32,512]{3,2,1,0:T(8,128)S(1)} %pad_maximum_fusion.10.refs_2_, f32[2,4,32,512]{3,2,1,0:T(8,128)S(1)} %collective-permute-done.9.refs_3_, ...), custom_call_target="tpu_custom_call" | custom-call | flops 15000000512 | bytes 524288 | tf_op jit(solution)/shard_map/factor_chunk_0/pallas_call | solution.py:299
  152.6 3.5 collective-permute-done.16
  160.1 11.8 %all-gather.13.cloned.1.call-done = f32[256,2048]{1,0:T(8,128)} async-done(((f32[64,2048]{1,0:T(8,128)}), f32[256,2048]{1,0:T(8,128)}) %all-gather.13.cloned.1.call-update) | async-done | bytes 2097168 | tf_op jit(solution)/shard_map/all_gather | solution.py:601
  178.0 8.3 %factor_chunk_1.4 = (f32[256,1024]{1,0:T(8,128)S(1)}, f32[256,256]{1,0:T(8,128)S(1)}) custom-call(s32[11]{0:T(128)S(1)} %concatenate.61.refs_0_, f32[16]{0:T(128)S(1)} %reshape.222.refs_1_, f32[2,4,32,512]{3,2,1,0:T(8,128)S(1)} %pad_maximum_fusion.10.refs_2_, f32[2,4,32,512]{3,2,1,0:T(8,128)S(1)} %collective-permute-done.9.refs_3_, ...), custom_call_target="tpu_custom_call" | custom-call | flops 15000000512 | bytes 1048576 | tf_op jit(solution)/shard_map/factor_chunk_1/pallas_call | solution.py:299
  195.8 10.1 %panel_2.2 = (f32[256,1024]{1,0:T(8,128)}, f32[256,768]{1,0:T(8,128)}) custom-call(s32[9]{0:T(128)} %copy-done.6, f32[16]{0:T(128)} %copy-done.27, f32[1,4,64,2048]{3,2,1,0:T(8,128)} %bitcast.230, f32[1,4,64,2048]{3,2,1,0:T(8,128)} %collective-permute-done.20.refs_3_, f32[256,1024]{1,0:T(8,128)} %copy-done.38, f32[256,1024]{1,0:T(8,128)} %copy-done.40, ...), custom_call_target="tpu_custom_call" | custom-call | flops 5000000000 | bytes 2097152 | tf_op jit(solution)/shard_map/panel_2/pallas_call | solution.py:451
  224.4 11.2 %panel_3.1 = (f32[256,1024]{1,0:T(8,128)}, f32[256,1024]{1,0:T(8,128)}, f32[256,1024]{1,0:T(8,128)}) custom-call(s32[9]{0:T(128)} %copy-done.6, f32[16]{0:T(128)} %copy-done.27, f32[1,4,64,2048]{3,2,1,0:T(8,128)} %bitcast.231, f32[1,4,64,2048]{3,2,1,0:T(8,128)} %collective-permute-done.20.refs_3_, f32[256,1024]{1,0:T(8,128)} %copy-done.38, ...), custom_call_target="tpu_custom_call" | custom-call | flops 5000000000 | bytes 2097152 | tf_op jit(solution)/shard_map/panel_3/pallas_call | solution.py:451
  250.4 6.2 %collective-permute-done.35.refs_8_.refs_14_ = f32[128,1024]{1,0:T(8,128)S(1)} collective-permute-done((f32[128,1024]{1,0:T(8,128)S(1)}, f32[128,1024]{1,0:T(8,128)S(1)}, u32[]{:S(2)}, u32[]{:S(2)}) %collective-permute-start.35) | collective-permute-done | bytes 524320 | tf_op jit(solution)/shard_map/ppermute | solution.py:473
  265.0 22.6 %factor_chunk_2.4 = (f32[512,1024]{1,0:T(8,128)}, f32[512,512]{1,0:T(8,128)S(1)}) custom-call(s32[11]{0:T(128)S(1)} %concatenate.61.refs_0_, f32[16]{0:T(128)S(1)} %reshape.222.refs_1_, f32[2,4,32,1024]{3,2,1,0:T(8,128)S(1)} %pad_maximum_fusion.4.refs_2_, f32[2,4,32,1024]{3,2,1,0:T(8,128)} %copy-done.73, f32[256,768]{1,0:T(8,128)S(1)} %copy-done.1, ...), custom_call_target="tpu_custom_call" | custom-call | flops 30000001024 | bytes 4194304 | tf_op jit(solution)/shard_map/factor_chunk_2/pallas_call | solution.py:299
  298.7 9.6 %panel_0.4 = (f32[256,1024]{1,0:T(8,128)}, f32[256,256]{1,0:T(8,128)}) custom-call(s32[11]{0:T(128)} %copy-done.7, f32[16]{0:T(128)} %copy-done.28, f32[2,4,2,32,1024]{4,3,2,1,0:T(8,128)} %copy-done.55, f32[2,4,2,32,1024]{4,3,2,1,0:T(8,128)} %copy-done.72, f32[256,256]{1,0:T(8,128)} %get-tuple-element.128.refs_4_, ...), custom_call_target="tpu_custom_call" | custom-call | flops 5000000000 | bytes 2097152 | tf_op jit(solution)/shard_map/panel_0/pallas_call | solution.py:451
  310.8 10.1 %panel_1.3 = (f32[256,1024]{1,0:T(8,128)}, f32[256,512]{1,0:T(8,128)}) custom-call(s32[11]{0:T(128)} %copy-done.7, f32[16]{0:T(128)} %copy-done.28, f32[2,4,2,32,1024]{4,3,2,1,0:T(8,128)} %copy-done.55, f32[2,4,2,32,1024]{4,3,2,1,0:T(8,128)} %copy-done.72, f32[256,256]{1,0:T(8,128)} %get-tuple-element.128.refs_4_, ...), custom_call_target="tpu_custom_call" | custom-call | flops 5000000000 | bytes 2097152 | tf_op jit(solution)/shard_map/panel_1/pallas_call | solution.py:451
  326.1 16.5 %panel_2.3 = (f32[512,1024]{1,0:T(8,128)}, f32[256,768]{1,0:T(8,128)}, f32[256,1024]{1,0:T(8,128)}, f32[128,1024]{1,0:T(8,128)}) custom-call(s32[11]{0:T(128)} %copy-done.7, f32[16]{0:T(128)} %copy-done.28, f32[2,4,2,32,1024]{4,3,2,1,0:T(8,128)} %copy-done.55, f32[2,4,2,32,1024]{4,3,2,1,0:T(8,128)} %copy-done.72, f32[256,256]{1,0:T(8,128)} %get-tuple-element.128.refs_4_, ...), custom_call_target="tpu_custom_call" | custom-call | flops 10000000000 | bytes 4194304 | tf_op jit(solution)/shard_map/panel_2/pallas_call | solution.py:451
  348.4 7.7 %factor_chunk_0.5 = (f32[256,1024]{1,0:T(8,128)S(1)}, f32[256,256]{1,0:T(8,128)S(1)}) custom-call(s32[15]{0:T(128)S(1)} %concatenate.72.refs_0_, f32[16]{0:T(128)S(1)} %reshape.224.refs_1_, f32[4,4,16,1024]{3,2,1,0:T(8,128)S(1)} %pad_maximum_fusion.5.refs_2_, f32[4,4,16,1024]{3,2,1,0:T(8,128)} %collective-permute-done.48.refs_3_, f32[256,256]{1,0:T(8,128)S(1)} %copy-done.5, ...), custom_call_target="tpu_custom_call" | custom-call | flops 15000000512 | bytes 524288 | tf_op jit(solution)/shard_map/factor_chunk_0/pallas_call | solution.py:299
  356.1 12.4 %collective-permute-done.50.refs_6_.refs_14_ = f32[128,768]{1,0:T(8,128)S(1)} collective-permute-done((f32[128,768]{1,0:T(8,128)S(1)}, f32[128,768]{1,0:T(8,128)S(1)}, u32[]{:S(2)}, u32[]{:S(2)}) %collective-permute-start.50) | collective-permute-done | bytes 393248 | tf_op jit(solution)/shard_map/ppermute | solution.py:473
  370.9 8.4 %factor_chunk_1.5 = (f32[256,1024]{1,0:T(8,128)S(1)}, f32[256,256]{1,0:T(8,128)S(1)}) custom-call(s32[15]{0:T(128)S(1)} %concatenate.72.refs_0_, f32[16]{0:T(128)S(1)} %reshape.224.refs_1_, f32[4,4,16,1024]{3,2,1,0:T(8,128)S(1)} %pad_maximum_fusion.5.refs_2_, f32[4,4,16,1024]{3,2,1,0:T(8,128)} %collective-permute-done.48.refs_3_, f32[256,512]{1,0:T(8,128)S(1)} %copy-done.3, ...), custom_call_target="tpu_custom_call" | custom-call | flops 15000000512 | bytes 1048576 | tf_op jit(solution)/shard_map/factor_chunk_1/pallas_call | solution.py:299
  383.3 22.1 %factor_chunk_2.5 = (f32[512,1024]{1,0:T(8,128)}, f32[512,512]{1,0:T(8,128)S(1)}) custom-call(s32[15]{0:T(128)S(1)} %concatenate.72.refs_0_, f32[16]{0:T(128)S(1)} %reshape.224.refs_1_, f32[4,4,16,1024]{3,2,1,0:T(8,128)S(1)} %pad_maximum_fusion.6.refs_2_, f32[4,4,16,1024]{3,2,1,0:T(8,128)} %copy-done.75, f32[256,768]{1,0:T(8,128)S(1)} %copy-done, ...), custom_call_target="tpu_custom_call" | custom-call | flops 30000001024 | bytes 4194304 | tf_op jit(solution)/shard_map/factor_chunk_2/pallas_call | solution.py:299
  410.3 19.9 %panel_0.5 = (f32[1024,1024]{1,0:T(8,128)}, f32[32,1024]{1,0:T(8,128)}, f32[64,1024]{1,0:T(8,128)}) custom-call(s32[15]{0:T(128)} %copy-done.8, f32[16]{0:T(128)} %copy-done.29, f32[4,4,16,1024]{3,2,1,0:T(8,128)} %copy-done.64, f32[4,4,16,1024]{3,2,1,0:T(8,128)} %copy-done.74, f32[4,4,16,1024]{3,2,1,0:T(8,128)} %copy-done.65, f32[4,4,16,1024]{3,2,1,0:T(8,128)} %copy-done.76, ...), custom_call_target="tpu_custom_call" | custom-call | flops 20000000000 | bytes 8388608 | tf_op jit(solution)/shard_map/panel_0/pallas_call | solution.py:451
  (357 shorter events, 152.5 us)
Async XLA Ops:
  7.2 67.1 %all-gather.9.cloned.1.call-start = ((), (), s32[]{:S(2)}) async-start(), calls=%async_computation | async-start | bytes 1310720 | tf_op jit(solution)/shard_map/all_gather | solution.py:601
  45.5 67.4 %all-gather.11.cloned.1.call-start = ((), (), s32[]{:S(2)}) async-start(), calls=%async_computation.1 | async-start | bytes 1966080 | tf_op jit(solution)/shard_map/all_gather | solution.py:601
  76.0 96.0 %all-gather.13.cloned.1.call-start = ((), (), s32[]{:S(2)}) async-start(), calls=%async_computation.2 | async-start | bytes 2621440 | tf_op jit(solution)/shard_map/all_gather | solution.py:601
  115.8 146.8 %all-gather.15.cloned.1.call-start = ((), (), s32[]{:S(2)}) async-start(), calls=%async_computation.3 | async-start | bytes 1310720 | tf_op jit(solution)/shard_map/all_gather | solution.py:601
  139.4 19.1 %collective-permute-start.17 = (f32[32,1024]{1,0:T(8,128)S(1)}, f32[32,1024]{1,0:T(8,128)S(1)}, u32[]{:S(2)}, u32[]{:S(2)}) collective-permute-start(f32[32,1024]{1,0:T(8,128)S(1)} %slice_bitcast_fusion.7), channel_id=1, source_target_pairs={{0,3},{1,2},{2,1},{3,0},{4,7},{5,6},{6,5},{7,4},{8,11},{9,10},{10,... | collective-permute-start | bytes 393224 | tf_op jit(solution)/shard_map/ppermute | solution.py:488
  189.7 28.4 %collective-permute-start.21 = (f32[2,4,32,1024]{3,2,1,0:T(8,128)S(1)}, f32[2,4,32,1024]{3,2,1,0:T(8,128)S(1)}, u32[]{:S(2)}, u32[]{:S(2)}) collective-permute-start(f32[2,4,32,1024]{3,2,1,0:T(8,128)S(1)} %pad_maximum_fusion.4.refs_2_), channel_id=1, source_target_pairs={{0,4},{4,0},{8,12},{12,8},{16,20},{20,16},{24,28},{28,24},{1,5},{5... | collective-permute-start | bytes 3145736 | tf_op jit(solution)/shard_map/ppermute | solution.py:473
  191.4 19.5 %collective-permute-start.26 = (f32[16,1024]{1,0:T(8,128)S(1)}, f32[16,1024]{1,0:T(8,128)S(1)}, u32[]{:S(2)}, u32[]{:S(2)}) collective-permute-start(f32[16,1024]{1,0:T(8,128)S(1)} %get-tuple-element.149), channel_id=1, source_target_pairs={{0,2},{1,3},{2,0},{3,1},{4,6},{5,7},{6,4},{7,5},{8,10},{9,11},{10,... | collective-permute-start | bytes 196616 | tf_op jit(solution)/shard_map/ppermute | solution.py:488
  193.1 20.7 %collective-permute-start.27 = (f32[16,1024]{1,0:T(8,128)S(1)}, f32[16,1024]{1,0:T(8,128)S(1)}, u32[]{:S(2)}, u32[]{:S(2)}) collective-permute-start(f32[16,1024]{1,0:T(8,128)S(1)} %get-tuple-element.149), channel_id=1, source_target_pairs={{0,3},{1,2},{2,1},{3,0},{4,7},{5,6},{6,5},{7,4},{8,11},{9,10},{10,... | collective-permute-start | bytes 196616 | tf_op jit(solution)/shard_map/ppermute | solution.py:488
  219.4 20.1 %collective-permute-start.33 = (f32[16,1024]{1,0:T(8,128)}, f32[16,1024]{1,0:T(8,128)S(1)}, u32[]{:S(2)}, u32[]{:S(2)}) collective-permute-start(f32[16,1024]{1,0:T(8,128)} %get-tuple-element.157), channel_id=1, source_target_pairs={{0,2},{1,3},{2,0},{3,1},{4,6},{5,7},{6,4},{7,5},{8,10},{9,11},{10,... | collective-permute-start | bytes 196616 | tf_op jit(solution)/shard_map/ppermute | solution.py:488
  221.2 19.8 %collective-permute-start.34 = (f32[16,1024]{1,0:T(8,128)}, f32[16,1024]{1,0:T(8,128)S(1)}, u32[]{:S(2)}, u32[]{:S(2)}) collective-permute-start(f32[16,1024]{1,0:T(8,128)} %get-tuple-element.157), channel_id=1, source_target_pairs={{0,3},{1,2},{2,1},{3,0},{4,7},{5,6},{6,5},{7,4},{8,11},{9,10},{10,... | collective-permute-start | bytes 196616 | tf_op jit(solution)/shard_map/ppermute | solution.py:488
  222.6 20.0 %collective-permute-start.29 = (f32[16,1024]{1,0:T(8,128)}, f32[16,1024]{1,0:T(8,128)S(1)}, u32[]{:S(2)}, u32[]{:S(2)}) collective-permute-start(f32[16,1024]{1,0:T(8,128)} %get-tuple-element.156), channel_id=1, source_target_pairs={{0,1},{1,0},{2,3},{3,2},{4,5},{5,4},{6,7},{7,6},{8,9},{9,8},{10,11... | collective-permute-start | bytes 196616 | tf_op jit(solution)/shard_map/ppermute | solution.py:488
  222.9 24.5 %collective-permute-start.28 = (f32[128,768]{1,0:T(8,128)S(1)}, f32[128,768]{1,0:T(8,128)S(1)}, u32[]{:S(2)}, u32[]{:S(2)}) collective-permute-start(f32[128,768]{1,0:T(8,128)S(1)} %constant_dynamic-slice_fusion.4), channel_id=1, source_target_pairs={{0,8},{4,12},{8,0},{12,4},{16,24},{20,28},{24,16},{28,20},{1,9},{5... | collective-permute-start | bytes 1179656 | tf_op jit(solution)/shard_map/ppermute | solution.py:473
  258.5 30.1 %collective-permute-start.42 = (f32[1,4,16,1024]{3,2,1,0:T(8,128)}, f32[1,4,16,1024]{3,2,1,0:T(8,128)}, u32[]{:S(2)}, u32[]{:S(2)}) collective-permute-start(f32[1,4,16,1024]{3,2,1,0:T(8,128)} %maximum_bitcast_fusion.5), channel_id=1, source_target_pairs={{0,16},{4,20},{8,24},{12,28},{16,0},{20,4},{24,8},{28,12},{1,17},{... | collective-permute-start | bytes 786440 | tf_op jit(solution)/shard_map/ppermute | solution.py:473
  260.0 28.7 %collective-permute-start.41 = (f32[1,4,16,1024]{3,2,1,0:T(8,128)}, f32[1,4,16,1024]{3,2,1,0:T(8,128)}, u32[]{:S(2)}, u32[]{:S(2)}) collective-permute-start(f32[1,4,16,1024]{3,2,1,0:T(8,128)} %maximum_bitcast_fusion.4), channel_id=1, source_target_pairs={{0,16},{4,20},{8,24},{12,28},{16,0},{20,4},{24,8},{28,12},{1,17},{... | collective-permute-start | bytes 786440 | tf_op jit(solution)/shard_map/ppermute | solution.py:473
  260.5 28.1 %collective-permute-start.40 = (f32[1,4,16,1024]{3,2,1,0:T(8,128)}, f32[1,4,16,1024]{3,2,1,0:T(8,128)}, u32[]{:S(2)}, u32[]{:S(2)}) collective-permute-start(f32[1,4,16,1024]{3,2,1,0:T(8,128)} %maximum_bitcast_fusion.3), channel_id=1, source_target_pairs={{0,16},{4,20},{8,24},{12,28},{16,0},{20,4},{24,8},{28,12},{1,17},{... | collective-permute-start | bytes 786440 | tf_op jit(solution)/shard_map/ppermute | solution.py:473
  262.0 26.7 %collective-permute-start.39 = (f32[1,4,16,1024]{3,2,1,0:T(8,128)}, f32[1,4,16,1024]{3,2,1,0:T(8,128)}, u32[]{:S(2)}, u32[]{:S(2)}) collective-permute-start(f32[1,4,16,1024]{3,2,1,0:T(8,128)} %maximum_bitcast_fusion.2), channel_id=1, source_target_pairs={{0,16},{4,20},{8,24},{12,28},{16,0},{20,4},{24,8},{28,12},{1,17},{... | collective-permute-start | bytes 786440 | tf_op jit(solution)/shard_map/ppermute | solution.py:473
  262.5 25.1 %collective-permute-start.38 = (f32[1,4,2,32,1024]{4,3,2,1,0:T(8,128)}, f32[1,4,2,32,1024]{4,3,2,1,0:T(8,128)S(1)}, u32[]{:S(2)}, u32[]{:S(2)}) collective-permute-start(f32[1,4,2,32,1024]{4,3,2,1,0:T(8,128)} %bitcast.198), channel_id=1, source_target_pairs={{0,8},{4,12},{8,0},{12,4},{16,24},{20,28},{24,16},{28,20},{1,9},{5... | collective-permute-start | bytes 3145736 | tf_op jit(solution)/shard_map/ppermute | solution.py:473
  323.9 18.8 %collective-permute-start.47 = (f32[128,256]{1,0:T(8,128)S(1)}, f32[128,256]{1,0:T(8,128)S(1)}, u32[]{:S(2)}, u32[]{:S(2)}) collective-permute-start(f32[128,256]{1,0:T(8,128)S(1)} %collective-permute-done.44.refs_5_.refs_10_), channel_id=1, source_target_pairs={{0,4},{4,0},{8,12},{12,8},{16,20},{20,16},{24,28},{28,24},{1,5},{5... | collective-permute-start | bytes 393224 | tf_op jit(solution)/shard_map/ppermute | solution.py:473
  324.0 18.7 %collective-permute-start.46 = (f32[128,512]{1,0:T(8,128)S(1)}, f32[128,512]{1,0:T(8,128)S(1)}, u32[]{:S(2)}, u32[]{:S(2)}) collective-permute-start(f32[128,512]{1,0:T(8,128)S(1)} %constant_dynamic-slice_fusion.2), channel_id=1, source_target_pairs={{0,16},{4,20},{8,24},{12,28},{16,0},{20,4},{24,8},{28,12},{1,17},{... | collective-permute-start | bytes 786440 | tf_op jit(solution)/shard_map/ppermute | solution.py:473
  345.9 22.6 %collective-permute-start.52 = (f32[2,4,16,1024]{3,2,1,0:T(8,128)}, f32[2,4,16,1024]{3,2,1,0:T(8,128)S(1)}, u32[]{:S(2)}, u32[]{:S(2)}) collective-permute-start(f32[2,4,16,1024]{3,2,1,0:T(8,128)} %copy-done.58), channel_id=1, source_target_pairs={{0,8},{4,12},{8,0},{12,4},{16,24},{20,28},{24,16},{28,20},{1,9},{5... | collective-permute-start | bytes 1572872 | tf_op jit(solution)/shard_map/ppermute | solution.py:473
  346.4 22.1 %collective-permute-start.51 = (f32[128,1024]{1,0:T(8,128)S(1)}, f32[128,1024]{1,0:T(8,128)S(1)}, u32[]{:S(2)}, u32[]{:S(2)}) collective-permute-start(f32[128,1024]{1,0:T(8,128)S(1)} %constant_dynamic-slice_fusion), channel_id=1, source_target_pairs={{0,16},{4,20},{8,24},{12,28},{16,0},{20,4},{24,8},{28,12},{1,17},{... | collective-permute-start | bytes 1572872 | tf_op jit(solution)/shard_map/ppermute | solution.py:473
  347.9 20.6 %collective-permute-start.50 = (f32[128,768]{1,0:T(8,128)S(1)}, f32[128,768]{1,0:T(8,128)S(1)}, u32[]{:S(2)}, u32[]{:S(2)}) collective-permute-start(f32[128,768]{1,0:T(8,128)S(1)} %constant_dynamic-slice_fusion.1), channel_id=1, source_target_pairs={{0,16},{4,20},{8,24},{12,28},{16,0},{20,4},{24,8},{28,12},{1,17},{... | collective-permute-start | bytes 1179656 | tf_op jit(solution)/shard_map/ppermute | solution.py:473
  381.6 25.0 %collective-permute-start.58 = (f32[4,4,16,1024]{3,2,1,0:T(8,128)S(1)}, f32[4,4,16,1024]{3,2,1,0:T(8,128)S(1)}, u32[]{:S(2)}, u32[]{:S(2)}) collective-permute-start(f32[4,4,16,1024]{3,2,1,0:T(8,128)S(1)} %pad_maximum_fusion.8.refs_2_), channel_id=1, source_target_pairs={{0,4},{4,0},{8,12},{12,8},{16,20},{20,16},{24,28},{28,24},{1,5},{5... | collective-permute-start | bytes 3145736 | tf_op jit(solution)/shard_map/ppermute | solution.py:473
  381.7 24.8 %collective-permute-start.57 = (f32[2,4,16,1024]{3,2,1,0:T(8,128)S(1)}, f32[2,4,16,1024]{3,2,1,0:T(8,128)S(1)}, u32[]{:S(2)}, u32[]{:S(2)}) collective-permute-start(f32[2,4,16,1024]{3,2,1,0:T(8,128)S(1)} %copy-done.63), channel_id=1, source_target_pairs={{0,8},{4,12},{8,0},{12,4},{16,24},{20,28},{24,16},{28,20},{1,9},{5... | collective-permute-start | bytes 1572872 | tf_op jit(solution)/shard_map/ppermute | solution.py:473
  (117 other events, 1744.2 us)
Sparse Core Ops, SparseCore 0:
  45.6 28.5 all-gather.8
  76.1 36.7 all-gather.10
  115.9 55.9 all-gather.12
  175.4 32.4 all-gather.14

commit v4 on v3

--- a/solution.py
+++ b/solution.py
@@ -155,24 +155,62 @@
     lax.fori_loop(0, steps, step, 0)
 
 
-def start_copies(plan, position_ref, source, blocks, portion, width, first, target_ref, sems):
+class Here:
+    def __init__(self, plan, routes_ref):
+        height = plan["height"]
+        leaf = lax.axis_index("leaf")
+        self.front = lax.axis_index("front")
+        self.core = leaf & 1
+        self.members = leaf & 2**height - 1
+        self.height = height
+        self.parent = leaf >> height
+        self.child = leaf >> height - 1 & 1
+        self.routes_ref = routes_ref
+
+    def piece(self, member):
+        return reversed_bits(self.members ^ member, self.height)
+
+    def to_pivot(self, child, block):
+        route = self.routes_ref[self.parent, self.child ^ child, block]
+        return jnp.where(route < PIVOT_BLOCKS, 1.0, 0.0)
+
+
+def reversed_bits(number, bit_count):
+    result = 0
+    for bit_index in range(bit_count):
+        result = result + (number >> bit_index & 1) * (1 << bit_count - 1 - bit_index)
+    return result
+
+
+def start_copies(plan, here, source, blocks, portion, width, first, target_ref, sems):
     copies = []
     rows = plan["piece_rows"]
     members = 2 ** plan["height"]
-    for order, block in enumerate(blocks):
-        slot = block % plan["front_count"]
-        if plan["where"][(portion, block // plan["front_count"])][0] in plan["direct"]:
-            slot = position_ref[slot]
+    count = plan["front_count"]
+    blocks = list(blocks)
+    for slab in sorted({block // count for block in blocks}):
+        fronts = [block % count for block in blocks if block // count == slab]
+        order = blocks.index(slab * count + fronts[0])
+        group, index = plan["where"][(portion, slab)]
         for member in range(members):
-            place = position_ref[plan["front_count"] + member]
-            start = pl.multiple_of(order * BLK + place * rows, rows)
-            copy = pltpu.make_async_copy(
-                source(member, portion, block, slot).at[:, pl.ds(first, width)],
-                target_ref.at[pl.ds(start, rows), pl.ds(0, width)],
-                sems.at[order * members + member],
-            )
-            copy.start()
-            copies.append(copy)
+            start = pl.multiple_of(here.piece(member) * rows, rows)
+            ref = source(group, member)
+            if group in plan["direct"]:
+                spans = [(front, 1, here.front ^ front) for front in fronts]
+            else:
+                spans = [(fronts[0], len(fronts), fronts[0])]
+            for front, length, slot in spans:
+                at = order + front - fronts[0]
+                slots = ref.at[pl.ds(slot, length)]
+                if index is not None:
+                    slots = slots.at[:, index]
+                copy = pltpu.make_async_copy(
+                    slots.at[:, :, pl.ds(first, width)],
+                    target_ref.at[pl.ds(at, length), pl.ds(start, rows), pl.ds(0, width)],
+                    sems.at[at * members + member],
+                )
+                copy.start()
+                copies.append(copy)
     return copies
 
 
@@ -205,26 +243,23 @@
 def make_source(plan, refs):
     height = plan["height"]
 
-    def source(member, portion, block, slot):
-        group, index = plan["where"][(portion, block // plan["front_count"])]
-        ref = refs[(group, member & 1)].at[stack_index(member, height), slot]
-        return ref if index is None else ref.at[index]
+    def source(group, member):
+        return refs[(group, member & 1)].at[stack_index(member, height)]
 
     return source
 
 
 def unpack(plan, refs, portions, blocks, strips):
     refs = list(refs)
-    position_ref, mask_ref = refs.pop(0), refs.pop(0)
+    here = Here(plan, refs.pop(0))
     names = piece_names(plan, portions, blocks)
     pieces = {name: refs.pop(0) for name in names}
     children = []
     if plan["height"] > 1:
         own = {strip: refs.pop(0) for strip in strips}
         other = {strip: (refs.pop(0), refs.pop(0)) for strip in strips}
-        core = position_ref[plan["front_count"] + 2 ** plan["height"]]
-        children = [Child(own, None, core), Child(None, other, core)]
-    return position_ref, mask_ref, make_source(plan, pieces), children, refs
+        children = own, other, here.core
+    return here, make_source(plan, pieces), children, refs
 
 
 def piece_names(plan, portions, blocks):
@@ -233,12 +268,12 @@
     return [(group, c) for group in groups for c in (0, 1)]
 
 
-def leading(plan, state, portions, blocks, strips):
+def leading(plan, state, portions, blocks, strips, space=pltpu.VMEM):
     smem = pl.BlockSpec(memory_space=pltpu.SMEM)
     anywhere = pl.BlockSpec(memory_space=pl.ANY)
-    vmem = pl.BlockSpec(memory_space=pltpu.VMEM)
-    operands = [state["position"], state["masks"]]
-    specs = [smem, smem]
+    vmem = pl.BlockSpec(memory_space=space)
+    operands = [state["routes"]]
+    specs = [smem]
     for name in piece_names(plan, portions, blocks):
         operands.append(state["pieces"][name])
         specs.append(anywhere)
@@ -260,21 +295,22 @@
     earlier = plan["chunks"][:chunk]
 
     def kernel(*refs):
-        position_ref, mask_ref, source, children, refs = unpack(plan, refs, (0,), blocks, strips)
+        here, source, children, refs = unpack(plan, refs, (0,), blocks, strips)
         old_factors, old_inverses = refs[:chunk], refs[chunk : 2 * chunk]
-        factor_ref, inverse_ref, rows_ref, work_ref, block_ref, spare_ref, sems = refs[2 * chunk :]
-        copies = start_copies(plan, position_ref, source, blocks, 0, width, 0, rows_ref, sems)
+        factor_ref, inverse_ref, pieces_ref, work_ref, block_ref, spare_ref, sems = refs[2 * chunk :]
+        copies = start_copies(plan, here, source, blocks, 0, width, 0, pieces_ref, sems)
         for copy in copies:
             copy.wait()
         if children:
+            own, other, core = children
+            children = [Child(own, None, core), Child(None, other, core)]
             for order, i in enumerate(blocks):
                 for j in range(width // BLK):
                     weights = [
-                        mask_ref[c * PIVOT_BLOCKS + i] * mask_ref[c * PIVOT_BLOCKS + j] for c in (0, 1)
+                        here.to_pivot(c, i) * here.to_pivot(c, j) for c in (0, 1)
                     ]
-                    rows_ref[pl.ds(order * BLK, BLK), pl.ds(j * BLK, BLK)] += child_sum(
-                        children, i, j, weights
-                    )
+                    pieces_ref[order, :, pl.ds(j * BLK, BLK)] += child_sum(children, i, j, weights)
+        rows_ref = pieces_ref.reshape(size, width)
         corner = rows_ref[:, pl.ds(low, size)]
         for index, (first, last) in enumerate(earlier):
             part = rows_ref[:, pl.ds(first, last - first)]
@@ -305,15 +341,15 @@
         in_specs=specs,
         out_specs=[vmem, vmem],
         scratch_shapes=[
-            pltpu.VMEM((size, width), jnp.float32),
+            pltpu.VMEM((len(blocks), BLK, width), jnp.float32),
             pltpu.VMEM((size, size), jnp.float32),
             pltpu.VMEM((BLK, BLK), jnp.float32),
             pltpu.VMEM((SUB * (4 * SUB + 2), BLK), jnp.float32),
             pltpu.SemaphoreType.DMA((len(blocks) * 2 ** plan["height"],)),
         ],
-        compiler_params=pltpu.CompilerParams(vmem_limit_bytes=48 * 2**20),
+        compiler_params=pltpu.CompilerParams(vmem_limit_bytes=(10 + 12 * size // 1024) * 2**20),
         cost_estimate=pl.CostEstimate(
-            flops=60_000_000_000 * size // 1024, bytes_accessed=8 * size * width, transcendentals=0
+            flops=1, bytes_accessed=1, transcendentals=0
         ),
         name=f"factor_chunk_{chunk}",
     )(*operands)
@@ -334,7 +370,7 @@
     slabs = PIVOT_BLOCKS // plan["front_count"]
 
     def kernel(*refs):
-        position_ref, mask_ref, source, children, refs = unpack(plan, refs, (1,), blocks, everything)
+        here, source, children, refs = unpack(plan, refs, (1,), blocks, everything)
         factor_refs, inverse_refs = refs[:count], refs[count : 2 * count]
         refs = refs[2 * count :]
         before_refs, refs = refs[: len(before)], refs[len(before) :]
@@ -345,43 +381,29 @@
             schur_refs, refs = refs[: len(strips)], refs[len(strips) :]
         if final:
             own_ref, refs = refs[0], refs[1:]
-        rows_ref, corner_ref, sems, corner_sems = refs
-        copies = start_copies(plan, position_ref, source, blocks, 1, pivot_size, 0, rows_ref, sems)
-        corner_copies = []
-        if first_level:
-            members = 2 ** plan["height"]
-            for order, block in enumerate(blocks):
-                limit = (block // plan["front_count"] + 1) * plan["front_count"] * BLK
-                corner_copies += start_copies(
-                    plan,
-                    position_ref,
-                    source,
-                    [block],
-                    1,
-                    limit,
-                    pivot_size,
-                    corner_ref.at[pl.ds(order * BLK, BLK)],
-                    corner_sems.at[pl.ds(order * members, members)],
-                )
+        pieces_ref, corner3_ref, sems = refs
+        rows_ref = pieces_ref.reshape(size, pivot_size)
+        corner_ref = corner3_ref.reshape(corner3_ref.shape[0] * BLK, pivot_size)
+        copies = start_copies(plan, here, source, blocks, 1, pivot_size, 0, pieces_ref, sems)
+        if children:
+            own, other, core = children
+            children = [Child(own, None, core), Child(None, other, core)]
         for copy in copies:
             copy.wait()
         if children:
             for order, i in enumerate(blocks):
                 for j in range(PIVOT_BLOCKS):
                     weights = [
-                        (1.0 - mask_ref[c * PIVOT_BLOCKS + i]) * mask_ref[c * PIVOT_BLOCKS + j]
+                        (1.0 - here.to_pivot(c, i)) * here.to_pivot(c, j)
                         for c in (0, 1)
                     ]
-                    rows_ref[pl.ds(order * BLK, BLK), pl.ds(j * BLK, BLK)] += child_sum(
-                        children, i, j, weights
-                    )
+                    pieces_ref[order, :, pl.ds(j * BLK, BLK)] += child_sum(children, i, j, weights)
                     if last or j // 2 <= i // 2:
                         weights = [
-                            (1.0 - mask_ref[c * PIVOT_BLOCKS + i])
-                            * (1.0 - mask_ref[c * PIVOT_BLOCKS + j])
+                            (1.0 - here.to_pivot(c, i)) * (1.0 - here.to_pivot(c, j))
                             for c in (0, 1)
                         ]
-                        corner_ref[pl.ds(order * BLK, BLK), pl.ds(j * BLK, BLK)] = child_sum(
+                        corner3_ref[order, :, pl.ds(j * BLK, BLK)] = child_sum(
                             children, i, j, weights
                         )
         for index, (low, high) in enumerate(chunks):
@@ -391,8 +413,6 @@
                     panel_ref[:, pl.ds(0, low)], factor_refs[index][:, pl.ds(0, low)], True
                 )
             panel_ref[:, pl.ds(low, high - low)] = product_3(part, inverse_refs[index][...], True)
-        for copy in corner_copies:
-            copy.wait()
         if not last:
             for order, strip in enumerate(strips):
                 mine = panel_ref[pl.ds(order * STRIP, STRIP), :]
@@ -401,15 +421,16 @@
                         other = before_refs[0][pl.ds(column * STRIP, STRIP), :]
                     else:
                         other = panel_ref[pl.ds(column * STRIP - start, STRIP), :]
-                    schur_refs[order][:, pl.ds(column * STRIP, STRIP)] = corner_ref[
-                        pl.ds(order * STRIP, STRIP), pl.ds(column * STRIP, STRIP)
-                    ] - product_3(mine, other, True)
+                    span = pl.ds(column * STRIP, STRIP)
+                    value = -product_3(mine, other, True)
+                    if not first_level:
+                        value = value + corner_ref[pl.ds(order * STRIP, STRIP), span]
+                    schur_refs[order][:, span] = value
         if not final:
             return
-        base = plan["front_count"] + 2 ** plan["height"] + 1
-        piece = pl.multiple_of(position_ref[base + 1] * rows, rows)
+        piece = pl.multiple_of(here.piece(0) * rows, rows)
         for slab in range(slabs):
-            block = position_ref[base] + plan["front_count"] * slab
+            block = here.front + plan["front_count"] * slab
             line = pl.multiple_of(block * BLK + piece, rows)
             for index, (low, high) in enumerate(chunks):
 
@@ -454,30 +475,64 @@
         in_specs=specs,
         out_specs=[vmem] * len(shapes),
         scratch_shapes=[
-            pltpu.VMEM((size, pivot_size), jnp.float32),
-            pltpu.VMEM((size, pivot_size), jnp.float32),
-            pltpu.SemaphoreType.DMA((copy_count,)),
+            pltpu.VMEM((len(blocks), BLK, pivot_size), jnp.float32),
+            pltpu.VMEM((1 if first_level else len(blocks), BLK, pivot_size), jnp.float32),
             pltpu.SemaphoreType.DMA((copy_count,)),
         ],
-        compiler_params=pltpu.CompilerParams(vmem_limit_bytes=56 * 2**20),
+        compiler_params=pltpu.CompilerParams(vmem_limit_bytes=(14 + 16 * size // 1024) * 2**20),
         cost_estimate=pl.CostEstimate(
-            flops=20_000_000_000 * size // 1024, bytes_accessed=8 * size * pivot_size, transcendentals=0
+            flops=1, bytes_accessed=1, transcendentals=0
         ),
         name=f"panel_{strips[0]}",
     )(*operands)
+
+
+def assemble_rows(plan, routes, entries, kept, received):
+    slabs, rows, size = kept.shape
+    width = plan["front_count"] * BLK
+
+    def kernel(routes_ref, entries_ref, kept_ref, received_ref, *outs):
+        here = Here(plan, routes_ref)
+        pivot_refs, (update_ref, left_ref) = outs[:slabs], outs[slabs:]
+        columns = [[here.to_pivot(c, j) for c in (0, 1)] for j in range(PIVOT_BLOCKS)]
+        for slab in range(slabs):
+            line = [here.to_pivot(c, here.front + plan["front_count"] * slab) for c in (0, 1)]
+            for j in range(PIVOT_BLOCKS):
+                span = pl.ds(j * BLK, BLK)
+                parts = (kept_ref[slab, :, span], received_ref[slab, :, span])
+
+                def total(weights):
+                    return parts[0] * weights[0] + parts[1] * weights[1]
+
+                if j * BLK < (slab + 1) * width:
+                    pivot_refs[slab][:, span] = entries_ref[0, slab, :, span] + total(
+                        [line[c] * columns[j][c] for c in (0, 1)]
+                    )
+                update_ref[slab, :, span] = entries_ref[1, slab, :, span] + total(
+                    [(1.0 - line[c]) * columns[j][c] for c in (0, 1)]
+                )
+                left_ref[slab, :, span] = total(
+                    [(1.0 - line[c]) * (1.0 - columns[j][c]) for c in (0, 1)]
+                )
+
+    vmem = pl.BlockSpec(memory_space=pltpu.VMEM)
+    shapes = [(rows, (slab + 1) * width) for slab in range(slabs)] + [kept.shape] * 2
+    outputs = pl.pallas_call(
+        kernel,
+        out_shape=[jax.ShapeDtypeStruct(shape, jnp.float32) for shape in shapes],
+        in_specs=[pl.BlockSpec(memory_space=pltpu.SMEM)] + [vmem] * 3,
+        out_specs=[vmem] * len(shapes),
+        compiler_params=pltpu.CompilerParams(vmem_limit_bytes=16 * 2**20),
+        cost_estimate=pl.CostEstimate(flops=1, bytes_accessed=1, transcendentals=0),
+        name="assemble_rows",
+    )(routes, entries, kept, received)
+    return outputs[:slabs], outputs[slabs], outputs[slabs + 1]
 
 
 def partner_2(value, axis, stride):
     mask = 2**stride
     pairs = [(source, source ^ mask) for source in range(lax.axis_size(axis))]
     return lax.ppermute(value, axis, pairs)
-
-
-def reversed_bits(number, bit_count):
-    result = jnp.zeros((), jnp.int32)
-    for bit_index in range(bit_count):
-        result = result + (number >> bit_index & 1) * (1 << bit_count - 1 - bit_index)
-    return result
 
 
 def all_front(value):
@@ -506,19 +561,17 @@
     front_count = lax.axis_size("front")
     slabs = PIVOT_BLOCKS // front_count
     leaf_index = lax.axis_index("leaf")
-    front_index = lax.axis_index("front")
     pivot_size = leaf_contrib.shape[1]
     core = leaf_index & 1
-    my_blocks = front_index + front_count * jnp.arange(slabs, dtype=jnp.int32)
     chunks = [(0, STRIP), (STRIP, 2 * STRIP), (2 * STRIP, pivot_size)]
     plans, states, entry_slabs = {}, {}, {}
     names = [(p, t) for p in (0, 1) for t in range(slabs)]
     where = {
-        1: {name: (order, None) for order, name in enumerate(names)},
-        2: {(p, t): (slabs, t) if p else (t, None) for p, t in names},
-        3: {(p, t): (p * slabs + t, None) for p, t in names},
+        1: {(p, t): (slabs, t) if p else (t, None) for p, t in names},
+        2: {(p, t): (p, t) for p, t in names},
+        3: {(p, t): (1, t) if p else (2 + t, None) for p, t in names},
     }
-    direct = {1: (0,), 2: range(slabs), 3: range(2 * slabs)}
+    direct = {1: (0,), 2: (), 3: ()}
     for height, entries, routes in (
         (1, entries_lower, assembly_lower),
         (2, entries_middle, assembly_middle),
@@ -534,56 +587,25 @@
             where=where[height],
             direct=direct[height],
         )
-        child_bit = leaf_index >> height - 1 & 1
-        route_pair = lax.dynamic_index_in_dim(routes, leaf_index >> height, 0, keepdims=False)
-        pivot_masks = (route_pair < PIVOT_BLOCKS).astype(jnp.float32)
-        masks = jnp.where(child_bit == 0, pivot_masks, pivot_masks[::-1])
-        position = jnp.concatenate(
-            [
-                front_index ^ jnp.arange(front_count, dtype=jnp.int32),
-                jnp.stack(
-                    [
-                        reversed_bits((leaf_index ^ m) & 2**height - 1, height)
-                        for m in range(2**height)
-                    ]
-                    + [core, front_index, reversed_bits(leaf_index & 2**height - 1, height)]
-                ),
-            ]
-        ).astype(jnp.int32)
-        states[height] = dict(position=position, masks=masks.reshape(-1), pieces={})
+        states[height] = dict(routes=routes, pieces={})
         entry_slabs[height] = entries.reshape(2, slabs, piece_rows, pivot_size)
-
-    piece_rows = BLK // 2
-    update = leaf_contrib.reshape(slabs, BLK, pivot_size)
-    low_rows, high_rows = update[:, :piece_rows], update[:, piece_rows:]
-    kept = jnp.where(core == 0, low_rows, high_rows)
-    received = partner_2(jnp.where(core == 0, high_rows, low_rows), "leaf", 0)
-    masks = states[1]["masks"].reshape(2, PIVOT_BLOCKS)
-    row_masks = masks[:, my_blocks]
-    spread = jnp.repeat(masks, BLK, axis=1)
-
-    def term(slab, width, row_pivot, column_pivot):
-        total = 0.0
-        for child, rows in enumerate((kept, received)):
-            row = row_masks[child, slab] if row_pivot else 1.0 - row_masks[child, slab]
-            column = spread[child] if column_pivot else 1.0 - spread[child]
-            total = total + rows[slab, :, :width] * (row * column[:width])[None]
-        return total
 
     def slab_width(slab):
         return (slab + 1) * front_count * BLK
 
-    lower_values = {}
-    for slab in range(slabs):
-        width = slab_width(slab)
-        lower_values[(0, slab)] = entry_slabs[1][0, slab, :, :width] + term(slab, width, True, True)
-        lower_values[(1, slab)] = jnp.concatenate(
-            [
-                entry_slabs[1][1, slab] + term(slab, pivot_size, False, True),
-                term(slab, width, False, False),
-            ],
-            axis=1,
+    def assemble(height, rows):
+        half = BLK // 2**height
+        child_bit = leaf_index >> height - 1 & 1
+        low_rows, high_rows = rows[:, :half], rows[:, half:]
+        kept = jnp.where(child_bit == 0, low_rows, high_rows)
+        received = partner_2(
+            jnp.where(child_bit == 0, high_rows, low_rows), "leaf", height - 1
         )
+        return assemble_rows(
+            plans[height], states[height]["routes"], entry_slabs[height], kept, received
+        )
+
+    lower_pivots, lower_updates, carried = assemble(1, leaf_contrib.reshape(slabs, BLK, pivot_size))
 
     for height in (2, 3):
         states[height]["own"], states[height]["other"] = {}, {}
@@ -603,6 +625,9 @@
     def across(value, bit):
         value = ready(value)
         return value, partner_2(value, "leaf", bit)
+
+    def pad_columns(value):
+        return jnp.pad(value, ((0, 0), (0, pivot_size - value.shape[1])))
 
     def joined(pair):
         return jnp.concatenate(pair, axis=0)
@@ -624,7 +649,7 @@
         return theirs
 
     def factor(height, chunk):
-        states[height]["position"] = ready(states[height]["position"])
+        states[height]["routes"] = ready(states[height]["routes"])
         one, other = factor_chunk(
             plans[height], states[height], chunk, factors[height], inverses[height]
         )
@@ -633,7 +658,7 @@
         return other
 
     def panel(height, strips, before, last=False):
-        states[height]["position"] = ready(states[height]["position"])
+        states[height]["routes"] = ready(states[height]["routes"])
         outputs = panel_and_schur(
             plans[height], states[height], strips, factors[height], inverses[height], before, last
         )
@@ -644,105 +669,96 @@
 
     strips = list(range(pivot_size // STRIP))
     later = range(1, slabs)
-    middle = all_front(entry_slabs[2][0, 0, :, : slab_width(0)])[None]
-    first = all_front(lower_values[(0, 0)])
-    end_step(middle, first)
+    first = all_front(lower_pivots[0])
+    end_step(first)
     end_step(place(1, 0, first[None]))
 
-    pair = across(middle, 1)
-    pivots = [gather(after(lower_values[(0, t)], first)) for t in later]
-    end_step(factor(1, 0), pair)
-
-    taken = place(2, 0, joined(pair))
-    updates = [gather(lower_values[(1, 0)])]
-    end_step(factor(1, 1), taken)
+    pivots = [gather(after(lower_pivots[t], first)) for t in later]
+    middle_pivots, middle_updates, carried = assemble(2, ready(carried))
+    end_step(factor(1, 0), middle_pivots)
+
+    middle = gather(jnp.stack([pad_columns(value) for value in middle_pivots]))
+    upper_pivots, upper_updates, carried = assemble(3, ready(carried))
+    end_step(factor(1, 1), upper_pivots)
 
     end_step(*[place(1, t, ready(value)[None]) for t, value in zip(later, pivots)])
 
-    updates += [gather(lower_values[(1, t)]) for t in later]
+    updates = gather(lower_updates)
     end_step(factor(1, 2))
 
-    middle_update = gather(entry_slabs[2][1])
-    end_step(place(1, slabs, ready(updates[0])[None]))
+    pair = across(middle[None], 1)
+    end_step(pair)
+    end_step(place(2, 0, joined(pair)))
+
+    rows = entry_slabs[2].shape[2] // 2
+    rest = jnp.concatenate(
+        [middle_updates.reshape(-1, rows, pivot_size)]
+        + [pad_columns(value)[None] for value in upper_pivots]
+        + [upper_updates]
+    )
+    rest = gather(rest)
+    end_step(place(1, slabs, ready(updates)[None]))
 
     panel_0, _ = panel(1, [0], None)
     end_step(panel_0)
 
     mine_0 = offer(2, 0)
-    panel_1, _ = panel(1, [1], panel_0)
-    end_step(panel_1, mine_0)
-
+    panel_rest, _, _, _, lower_own = panel(1, strips[1:], panel_0)
+    end_step(panel_rest, mine_0)
+
+    mine_1 = offer(2, 1)
     end_step(swap(2, 0, mine_0))
 
-    mine_1 = offer(2, 1)
-    middle = [all_front(ready(entry_slabs[2][0, t]))[None] for t in later]
-    end_step(factor(2, 0), mine_1, middle)
+    mine_2 = offer(2, 2)
+    end_step(factor(2, 0), mine_1, mine_2)
 
     taken = swap(2, 1, mine_1)
+    mine_3 = offer(2, 3)
     end_step(taken)
 
-    pairs = [across(value, 1) for value in middle]
-    taken = [place(1, slabs + t, ready(updates[t])[None]) for t in later]
-    end_step(factor(2, 1), pairs, taken)
-
-    taken = [place(2, t, joined(pair)) for t, pair in zip(later, pairs)]
-    upper = [all_front(ready(entry_slabs[3][0, t]))[None] for t in range(slabs)]
-    before = jnp.concatenate([panel_0, panel_1], axis=0)
-    panel_2, _ = panel(1, [2], before)
-    end_step(panel_2, taken, upper)
-
-    mine_2 = offer(2, 2)
-    upper_update = [all_front(ready(entry_slabs[3][1, t]))[None] for t in range(slabs)]
-    before = jnp.concatenate([before, panel_2], axis=0)
-    panel_3, _, lower_own = panel(1, [3], before)
-    end_step(panel_3, mine_2, upper_update)
-
-    mine_3 = offer(2, 3)
     taken = swap(2, 2, mine_2)
-    end_step(mine_3, taken)
+    end_step(factor(2, 1), mine_3, taken)
     end_step(swap(2, 3, mine_3))
 
+    front_count_now = rest.shape[0]
+    middle_update = rest[:, : 2 * slabs].reshape(front_count_now, slabs, -1, pivot_size)
+    upper = rest[:, 2 * slabs :].reshape(front_count_now, 2, slabs, rows, pivot_size)
     pair = across(middle_update[None], 1)
-    pairs = [across(value, 2) for value in upper + upper_update]
-    end_step(factor(2, 2), pair, pairs)
-
-    taken = place(2, slabs, joined(pair))
-    upper = [joined(pair) for pair in pairs]
-    end_step(taken, upper)
+    upper_pair = across(upper[None], 2)
+    end_step(factor(2, 2), pair, upper_pair)
+
+    upper = joined(upper_pair)
+    taken = place(2, 1, joined(pair))
+    end_step(taken)
 
     panel_0, _ = panel(2, [0], None)
     end_step(panel_0)
 
     mine_0 = offer(3, 0)
+    pair = across(upper[:, :, 0, 0], 1)
     panel_1, _ = panel(2, [1], panel_0)
-    end_step(panel_1, mine_0)
+    end_step(panel_1, mine_0, pair)
 
     mine_1 = offer(3, 1)
-    taken = swap(3, 0, mine_0)
-    pair = across(upper[0], 1)
+    taken = swap(3, 0, mine_0), place(3, 2, joined(pair))
+    pairs = [across(upper[:, :, 0, t], 1) for t in later]
     before = jnp.concatenate([panel_0, panel_1], axis=0)
     _, _, _, middle_own = panel(2, [2, 3], before)
-    end_step(middle_own, mine_1, taken, pair)
-
-    taken = place(3, 0, joined(pair)), swap(3, 1, mine_1)
-    end_step(taken)
+    end_step(middle_own, mine_1, taken, pairs)
 
     mine_2, mine_3 = offer(3, 2), offer(3, 3)
-    pairs = [across(upper[t], 1) for t in later]
-    end_step(factor(3, 0), mine_2, mine_3, pairs)
+    taken = swap(3, 1, mine_1), [place(3, 2 + t, joined(pair)) for t, pair in zip(later, pairs)]
+    end_step(factor(3, 0), mine_2, mine_3, taken)
 
     taken = swap(3, 2, mine_2), swap(3, 3, mine_3)
-    taken += tuple(place(3, t, joined(pair)) for t, pair in zip(later, pairs))
-    pair = across(upper[slabs], 1)
-    end_step(factor(3, 1), taken, pair)
-
-    taken = place(3, slabs, joined(pair))
-    pairs = [across(upper[slabs + t], 1) for t in later]
-    end_step(factor(3, 2), taken, pairs)
-
-    end_step(*[place(3, slabs + t, joined(pair)) for t, pair in zip(later, pairs)])
+    end_step(factor(3, 1), taken)
+
+    pair = across(upper[:, :, 1], 1)
+    end_step(factor(3, 2), pair)
+
+    end_step(place(3, 1, joined(pair)))
     _, top, upper_own = panel(3, strips, None, True)
-    return (lower_own, middle_own, upper_own, top)
+    return (lower_own, middle_own, upper_own, top + carried.reshape(-1, pivot_size))
 
 
 def solution(mesh):

time: 445 us -> 353 us (0.79)
  Pallas kernels: 203 us -> 154 us
  waiting for transfers between devices: 91.5 us -> 121 us
  starting transfers between devices: 55.7 us -> 29.3 us
  other arithmetic: 28.3 us -> 7.91 us
  local copies, waits for them, and re-layouts: 39.5 us -> 20.8 us
    ppermute x39 -> x33, waiting for transfers between devices: 33.9 us -> 80.4 us  [partner_2(): return lax.ppermute(value, axis, pairs)]
    pallas_call x8 -> x6, Pallas kernels: 94.4 us -> 53.3 us  [panel_and_schur(): pl.pallas_call(kernel, out_shape=[jax.ShapeDtypeStruct(shape, jnp.float32...]
    ppermute x21 -> x3, starting transfers between devices: 32.2 us -> 5.68 us  [all_front(): slots.append(lax.ppermute(value, 'front', pairs))]
    ppermute x21 -> x3, waiting for transfers between devices: 23.2 us -> 10.7 us  [all_front(): slots.append(lax.ppermute(value, 'front', pairs))]
    pallas_call x9, Pallas kernels: 109 us -> 98.7 us  [factor_chunk(): pl.pallas_call(kernel, out_shape=[jax.ShapeDtypeStruct((size, plan['pivot...]
    broadcast_in_dim x6 -> x0, other arithmetic: 5.37 us -> none  [the longest x2 3.14 us: local(): all_front(ready(entry_slabs[3][1, t]))[None]]
    concatenate x3 -> x1, other arithmetic: 6.86 us -> 1.82 us  [local(): jnp.concatenate([middle_updates.reshape(-1, rows, pivot_size)] + [pad_col...]
    dynamic_slice x8, local copies, waits for them, and re-layouts: 5.1 us -> 0.22 us  [offer(): lax.dynamic_slice_in_dim(states[height]['own'][strip], core * BLK, BLK, 0)]
  transfers between devices with their start and end apart: 64 -> 40, of which waited for: 23 -> 23; matrix products, arithmetic and copies ran while one was open for 11% -> 3% of each run, Pallas kernels for 40% -> 39%
where the time goes in v4:
time: 353 us; the launch traced here: 349 us
  Pallas kernels  154 us (44%)
  waiting for transfers between devices  121 us (34%)
  starting transfers between devices  29.3 us (8%)
  local copies, waits for them, and re-layouts  20.8 us (6%)
  between operations  15.5 us (4%)
  other arithmetic  7.91 us (2%)
    pallas_call x9, Pallas kernels, factor_chunk(): pl.pallas_call(kernel, out_shape=[jax.ShapeDtypeStruct((size, plan['pivot...  98.7 us
    ppermute x33, waiting for transfers between devices, partner_2(): return lax.ppermute(value, axis, pairs)  80.4 us
    pallas_call x6, Pallas kernels, panel_and_schur(): pl.pallas_call(kernel, out_shape=[jax.ShapeDtypeStruct(shape, jnp.float32...  53.3 us
    all_gather x4, waiting for transfers between devices, gather(): return lax.all_gather(ready(value), 'front')  29.7 us
    ppermute x33, starting transfers between devices, partner_2(): return lax.ppermute(value, axis, pairs)  23.1 us
    unnamed x108, local copies, waits for them, and re-layouts  17.3 us
    ppermute x3, waiting for transfers between devices, all_front(): slots.append(lax.ppermute(value, 'front', pairs))  10.7 us
  transfers between devices with their start and end apart: 40, of which 23 were waited for; matrix products, arithmetic and copies ran while one was open for 3% of the time, Pallas kernels for 39%

profile of v4, /device:TPU:0, one launch (start us, length us, event | category | flops | bytes accessed | tf_op | source)
XLA Modules:
  0.0 348.7 jit_solution(14438576258198711437)
XLA Ops:
  11.6 5.0 %collective-permute-start.3 = (f32[64,512]{1,0:T(8,128)S(1)}, f32[64,512]{1,0:T(8,128)S(1)}, u32[]{:S(2)}, u32[]{:S(2)}) collective-permute-start(f32[64,512]{1,0:T(8,128)S(1)} %get-tuple-element.103), channel_id=1, source_target_pairs={{0,3},{1,2},{2,1},{3,0},{4,7},{5,6},{6,5},{7,4},{8,11},{9,10},{10,... | collective-permute-start | bytes 393224 | tf_op jit(solution)/shard_map/ppermute | solution.py:543
  21.0 7.0 %collective-permute-done.2 = f32[64,512]{1,0:T(8,128)S(1)} collective-permute-done((f32[64,512]{1,0:T(8,128)S(1)}, f32[64,512]{1,0:T(8,128)S(1)}, u32[]{:S(2)}, u32[]{:S(2)}) %collective-permute-start.2) | collective-permute-done | bytes 131104 | tf_op jit(solution)/shard_map/ppermute | solution.py:543
  31.9 6.8 %factor_chunk_0.3 = (f32[256,1024]{1,0:T(8,128)S(1)}, f32[256,256]{1,0:T(8,128)S(1)}) custom-call(s32[4,2,8]{2,1,0:T(2,128)S(1)} %copy-done.44, f32[1,4,64,512]{3,2,1,0:T(8,128)S(1)} %get-tuple-element.104.refs_1_, f32[1,4,64,512]{3,2,1,0:T(8,128)S(1)} %collective-permute-done.4.refs_2_), custom_call_target="tpu_custom_call" | custom-call | flops 1 | bytes 1 | tf_op jit(solution)/shard_map/factor_chunk_0/pallas_call | solution.py:335
  44.2 8.0 %factor_chunk_1.3 = (f32[256,1024]{1,0:T(8,128)S(1)}, f32[256,256]{1,0:T(8,128)S(1)}) custom-call(s32[4,2,8]{2,1,0:T(2,128)S(1)} %copy-done.44, f32[1,4,64,512]{3,2,1,0:T(8,128)S(1)} %get-tuple-element.104.refs_1_, f32[1,4,64,512]{3,2,1,0:T(8,128)S(1)} %copy-done.37, f32[256,1024]{1,0:T(8,128)S(1)} %get-tuple-element.114.refs_3_, ...), custom_call_target="tpu_custom_call" | custom-call | flops 1 | bytes 1 | tf_op jit(solution)/shard_map/factor_chunk_1/pallas_call | solution.py:335
  62.7 16.8 %factor_chunk_2.3 = (f32[512,1024]{1,0:T(8,128)S(1)}, f32[512,512]{1,0:T(8,128)S(1)}) custom-call(s32[4,2,8]{2,1,0:T(2,128)S(1)} %copy-done.44, f32[1,4,64,1024]{3,2,1,0:T(8,128)S(1)} %bitcast.41, f32[1,4,64,1024]{3,2,1,0:T(8,128)S(1)} %collective-permute-done.7.refs_2_, f32[256,1024]{1,0:T(8,128)S(1)} %get-tuple-element.114.refs_3_, ...), custom_call_target="tpu_custom_call" | custom-call | flops 1 | bytes 1 | tf_op jit(solution)/shard_map/factor_chunk_2/pallas_call | solution.py:335
  81.8 5.8 %all-gather.13.cloned.1.call-done = f32[8,32,1024]{2,1,0:T(8,128)} async-done(((f32[2,32,1024]{2,1,0:T(8,128)}), f32[8,32,1024]{2,1,0:T(8,128)}) %all-gather.13.cloned.1.call-update) | async-done | bytes 1048592 | tf_op jit(solution)/shard_map/all_gather | solution.py:623
  89.4 23.3 %collective-permute-done.8 = f32[1,4,2,32,1024]{4,3,2,1,0:T(8,128)} collective-permute-done((f32[1,4,2,32,1024]{4,3,2,1,0:T(8,128)}, f32[1,4,2,32,1024]{4,3,2,1,0:T(8,128)}, u32[]{:S(2)}, u32[]{:S(2)}) %collective-permute-start.8) | collective-permute-done | bytes 1048608 | tf_op jit(solution)/shard_map/ppermute | solution.py:535
  114.5 20.7 %all-gather.11.cloned.1.call-done = f32[8,64,1024]{2,1,0:T(8,128)} async-done(((f32[2,64,1024]{2,1,0:T(8,128)}), f32[8,64,1024]{2,1,0:T(8,128)}) %all-gather.11.cloned.1.call-update) | async-done | bytes 2097168 | tf_op jit(solution)/shard_map/all_gather | solution.py:623
  146.5 5.3 %panel_0.3 = (f32[256,1024]{1,0:T(8,128)S(1)}, f32[256,256]{1,0:T(8,128)S(1)}) custom-call(s32[4,2,8]{2,1,0:T(2,128)S(1)} %copy-done.44, f32[1,4,2,64,1024]{4,3,2,1,0:T(8,128)S(1)} %bitcast.37, f32[1,4,2,64,1024]{4,3,2,1,0:T(8,128)} %collective-permute-done.10.refs_2_, f32[256,1024]{1,0:T(8,128)S(1)} %get-tuple-element.114.refs_3_, ...), custom_call_target="tpu_custom_call" | custom-call | flops 1 | bytes 1 | tf_op jit(solution)/shard_map/panel_0/pallas_call | solution.py:472
  153.4 14.7 %panel_1.2 = (f32[768,1024]{1,0:T(8,128)}, f32[256,512]{1,0:T(8,128)S(1)}, f32[256,768]{1,0:T(8,128)S(1)}, f32[256,1024]{1,0:T(8,128)S(1)}, f32[256,1024]{1,0:T(8,128)}) custom-call(s32[4,2,8]{2,1,0:T(2,128)S(1)} %copy-done.44, f32[1,4,2,64,1024]{4,3,2,1,0:T(8,128)S(1)} %bitcast.38, f32[1,4,2,64,1024]{4,3,2,1,0:T(8,128)} %collective-permute-done.10.refs_2_, ...), custom_call_target="tpu_custom_call" | custom-call | flops 1 | bytes 1 | tf_op jit(solution)/shard_map/panel_1/pallas_call | solution.py:472
  171.7 7.6 %factor_chunk_0.4 = (f32[256,1024]{1,0:T(8,128)S(1)}, f32[256,256]{1,0:T(8,128)S(1)}) custom-call(s32[2,2,8]{2,1,0:T(2,128)S(1)} %copy-done.49, f32[2,4,2,32,1024]{4,3,2,1,0:T(8,128)S(1)} %pad_maximum_fusion.refs_1_, f32[2,4,2,32,1024]{4,3,2,1,0:T(8,128)} %collective-permute-done.9.refs_2_, f32[256,256]{1,0:T(8,128)S(1)} %get-tuple-element.137.refs_3_, ...), custom_call_target="tpu_custom_call" | custom-call | flops 1 | bytes 1 | tf_op jit(solution)/shard_map/factor_chunk_0/pallas_call | solution.py:335
  179.4 7.0 %collective-permute-done.13.refs_4_.refs_9_ = f32[128,512]{1,0:T(8,128)S(1)} collective-permute-done((f32[128,512]{1,0:T(8,128)S(1)}, f32[128,512]{1,0:T(8,128)S(1)}, u32[]{:S(2)}, u32[]{:S(2)}) %collective-permute-start.13) | collective-permute-done | bytes 262176 | tf_op jit(solution)/shard_map/ppermute | solution.py:535
  188.1 8.4 %factor_chunk_1.4 = (f32[256,1024]{1,0:T(8,128)S(1)}, f32[256,256]{1,0:T(8,128)S(1)}) custom-call(s32[2,2,8]{2,1,0:T(2,128)S(1)} %copy-done.49, f32[2,4,2,32,1024]{4,3,2,1,0:T(8,128)S(1)} %pad_maximum_fusion.refs_1_, f32[2,4,2,32,1024]{4,3,2,1,0:T(8,128)} %collective-permute-done.9.refs_2_, f32[256,512]{1,0:T(8,128)S(1)} %get-tuple-element.142.refs_3_.refs_4_, ...), custom_call_target="tpu_custom_call" | custom-call | flops 1 | bytes 1 | tf_op jit(solution)/shard_map/factor_chunk_1/pallas_call | solution.py:335
  206.3 18.8 %factor_chunk_2.4 = (f32[512,1024]{1,0:T(8,128)S(1)}, f32[512,512]{1,0:T(8,128)S(1)}) custom-call(s32[2,2,8]{2,1,0:T(2,128)S(1)} %copy-done.49, f32[2,4,2,32,1024]{4,3,2,1,0:T(8,128)S(1)} %pad_maximum_fusion.refs_1_, f32[2,4,2,32,1024]{4,3,2,1,0:T(8,128)} %collective-permute-done.9.refs_2_, f32[256,768]{1,0:T(8,128)S(1)} %copy-done.5, ...), custom_call_target="tpu_custom_call" | custom-call | flops 1 | bytes 1 | tf_op jit(solution)/shard_map/factor_chunk_2/pallas_call | solution.py:335
  233.9 4.7 %panel_0.4 = (f32[256,1024]{1,0:T(8,128)S(1)}, f32[256,256]{1,0:T(8,128)S(1)}) custom-call(s32[2,2,8]{2,1,0:T(2,128)S(1)} %copy-done.49, f32[2,4,2,32,1024]{4,3,2,1,0:T(8,128)S(1)} %pad_maximum_fusion.1.refs_1_, f32[2,4,2,32,1024]{4,3,2,1,0:T(8,128)S(1)} %collective-permute-done.21.refs_2_, f32[256,256]{1,0:T(8,128)S(1)} %copy-done.21, ...), custom_call_target="tpu_custom_call" | custom-call | flops 1 | bytes 1 | tf_op jit(solution)/shard_map/panel_0/pallas_call | solution.py:472
  241.7 4.8 %panel_1.3 = (f32[256,1024]{1,0:T(8,128)S(1)}, f32[256,512]{1,0:T(8,128)S(1)}) custom-call(s32[2,2,8]{2,1,0:T(2,128)S(1)} %copy-done.49, f32[2,4,2,32,1024]{4,3,2,1,0:T(8,128)S(1)} %pad_maximum_fusion.1.refs_1_, f32[2,4,2,32,1024]{4,3,2,1,0:T(8,128)S(1)} %collective-permute-done.21.refs_2_, f32[256,256]{1,0:T(8,128)S(1)} %copy-done.21, ...), custom_call_target="tpu_custom_call" | custom-call | flops 1 | bytes 1 | tf_op jit(solution)/shard_map/panel_1/pallas_call | solution.py:472
  246.5 6.1 %collective-permute-done.23 = f32[2,4,16,1024]{3,2,1,0:T(8,128)S(1)} collective-permute-done((f32[2,4,16,1024]{3,2,1,0:T(8,128)S(1)}, f32[2,4,16,1024]{3,2,1,0:T(8,128)S(1)}, u32[]{:S(2)}, u32[]{:S(2)}) %collective-permute-start.23) | collective-permute-done | bytes 524320 | tf_op jit(solution)/shard_map/ppermute | solution.py:535
  256.2 10.8 %panel_2.1 = (f32[512,1024]{1,0:T(8,128)}, f32[256,768]{1,0:T(8,128)S(1)}, f32[256,1024]{1,0:T(8,128)S(1)}, f32[128,1024]{1,0:T(8,128)}) custom-call(s32[2,2,8]{2,1,0:T(2,128)S(1)} %copy-done.49, f32[2,4,2,32,1024]{4,3,2,1,0:T(8,128)S(1)} %pad_maximum_fusion.1.refs_1_, f32[2,4,2,32,1024]{4,3,2,1,0:T(8,128)S(1)} %collective-permute-done.21.refs_2_, ...), custom_call_target="tpu_custom_call" | custom-call | flops 1 | bytes 1 | tf_op jit(solution)/shard_map/panel_2/pallas_call | solution.py:472
  269.9 7.3 %factor_chunk_0.5 = (f32[256,1024]{1,0:T(8,128)S(1)}, f32[256,256]{1,0:T(8,128)S(1)}) custom-call(s32[1,2,8]{2,1,0:T(2,128)S(1)} %copy-done.52, f32[4,4,16,1024]{3,2,1,0:T(8,128)S(1)} %pad_maximum_fusion.4.refs_1_, f32[4,4,16,1024]{3,2,1,0:T(8,128)S(1)} %collective-permute-done.26.refs_2_, f32[256,256]{1,0:T(8,128)S(1)} %get-tuple-element.169.refs_3_, ...), custom_call_target="tpu_custom_call" | custom-call | flops 1 | bytes 1 | tf_op jit(solution)/shard_map/factor_chunk_0/pallas_call | solution.py:335
  277.2 12.9 %collective-permute-done.28.refs_5_.refs_11_ = f32[128,768]{1,0:T(8,128)S(1)} collective-permute-done((f32[128,768]{1,0:T(8,128)S(1)}, f32[128,768]{1,0:T(8,128)S(1)}, u32[]{:S(2)}, u32[]{:S(2)}) %collective-permute-start.28) | collective-permute-done | bytes 393248 | tf_op jit(solution)/shard_map/ppermute | solution.py:535
  290.8 7.6 %factor_chunk_1.5 = (f32[256,1024]{1,0:T(8,128)S(1)}, f32[256,256]{1,0:T(8,128)S(1)}) custom-call(s32[1,2,8]{2,1,0:T(2,128)S(1)} %copy-done.52, f32[4,4,16,1024]{3,2,1,0:T(8,128)S(1)} %pad_maximum_fusion.4.refs_1_, f32[4,4,16,1024]{3,2,1,0:T(8,128)S(1)} %collective-permute-done.26.refs_2_, f32[256,512]{1,0:T(8,128)S(1)} %get-tuple-element.174.refs_3_.refs_4_, ...), custom_call_target="tpu_custom_call" | custom-call | flops 1 | bytes 1 | tf_op jit(solution)/shard_map/factor_chunk_1/pallas_call | solution.py:335
  300.1 17.3 %factor_chunk_2.5 = (f32[512,1024]{1,0:T(8,128)S(1)}, f32[512,512]{1,0:T(8,128)S(1)}) custom-call(s32[1,2,8]{2,1,0:T(2,128)S(1)} %copy-done.52, f32[4,4,16,1024]{3,2,1,0:T(8,128)S(1)} %pad_maximum_fusion.5.refs_1_, f32[4,4,16,1024]{3,2,1,0:T(8,128)S(1)} %collective-permute-done.31.refs_2_, f32[256,768]{1,0:T(8,128)S(1)} %get-tuple-element.181.refs_3_.refs_5_, ...), custom_call_target="tpu_custom_call" | custom-call | flops 1 | bytes 1 | tf_op jit(solution)/shard_map/factor_chunk_2/pallas_call | solution.py:335
  317.3 6.3 %collective-permute-done.34 = f32[2,4,2,16,1024]{4,3,2,1,0:T(8,128)S(1)} collective-permute-done((f32[2,4,2,16,1024]{4,3,2,1,0:T(8,128)S(1)}, f32[2,4,2,16,1024]{4,3,2,1,0:T(8,128)S(1)}, u32[]{:S(2)}, u32[]{:S(2)}) %collective-permute-start.34) | collective-permute-done | bytes 1048608 | tf_op jit(solution)/shard_map/ppermute | solution.py:535
  328.1 13.1 %panel_0.5 = (f32[1024,1024]{1,0:T(8,128)}, f32[32,1024]{1,0:T(8,128)S(1)}, f32[64,1024]{1,0:T(8,128)}) custom-call(s32[1,2,8]{2,1,0:T(2,128)S(1)} %copy-done.52, f32[4,4,2,16,1024]{4,3,2,1,0:T(8,128)S(1)} %pad_maximum_fusion.3.refs_1_, f32[4,4,2,16,1024]{4,3,2,1,0:T(8,128)S(1)} %collective-permute-done.35.refs_2_, ...), custom_call_target="tpu_custom_call" | custom-call | flops 1 | bytes 1 | tf_op jit(solution)/shard_map/panel_0/pallas_call | solution.py:472
  (215 shorter events, 86.9 us)
Async XLA Ops:
  7.2 51.4 %all-gather.9.cloned.1.call-start = ((), (), s32[]{:S(2)}) async-start(), calls=%async_computation | async-start | bytes 1310720 | tf_op jit(solution)/shard_map/all_gather | solution.py:623
  16.6 11.4 %collective-permute-start.2 = (f32[64,512]{1,0:T(8,128)S(1)}, f32[64,512]{1,0:T(8,128)S(1)}, u32[]{:S(2)}, u32[]{:S(2)}) collective-permute-start(f32[64,512]{1,0:T(8,128)S(1)} %get-tuple-element.103), channel_id=1, source_target_pairs={{0,2},{1,3},{2,0},{3,1},{4,6},{5,7},{6,4},{7,5},{8,10},{9,11},{10,... | collective-permute-start | bytes 393224 | tf_op jit(solution)/shard_map/ppermute | solution.py:543
  16.6 11.4 %collective-permute-start.1 = (f32[64,512]{1,0:T(8,128)S(1)}, f32[64,512]{1,0:T(8,128)S(1)}, u32[]{:S(2)}, u32[]{:S(2)}) collective-permute-start(f32[64,512]{1,0:T(8,128)S(1)} %get-tuple-element.103), channel_id=1, source_target_pairs={{0,1},{1,0},{2,3},{3,2},{4,5},{5,4},{6,7},{7,6},{8,9},{9,8},{10,11... | collective-permute-start | bytes 393224 | tf_op jit(solution)/shard_map/ppermute | solution.py:543
  30.2 57.4 %all-gather.13.cloned.1.call-start = ((), (), s32[]{:S(2)}) async-start(), calls=%async_computation.2 | async-start | bytes 1310720 | tf_op jit(solution)/shard_map/all_gather | solution.py:623
  41.3 93.9 %all-gather.11.cloned.1.call-start = ((), (), s32[]{:S(2)}) async-start(), calls=%async_computation.1 | async-start | bytes 2621440 | tf_op jit(solution)/shard_map/all_gather | solution.py:623
  87.6 25.1 %collective-permute-start.8 = (f32[1,4,2,32,1024]{4,3,2,1,0:T(8,128)}, f32[1,4,2,32,1024]{4,3,2,1,0:T(8,128)}, u32[]{:S(2)}, u32[]{:S(2)}) collective-permute-start(f32[1,4,2,32,1024]{4,3,2,1,0:T(8,128)} %bitcast.54), channel_id=1, source_target_pairs={{0,8},{4,12},{8,0},{12,4},{16,24},{20,28},{24,16},{28,20},{1,9},{5... | collective-permute-start | bytes 3145736 | tf_op jit(solution)/shard_map/ppermute | solution.py:535
  89.1 112.6 %all-gather.15.cloned.1.call-start = ((), (), s32[]{:S(2)}) async-start(), calls=%async_computation.3 | async-start | bytes 2621440 | tf_op jit(solution)/shard_map/all_gather | solution.py:623
  114.4 20.8 %collective-permute-start.9 = (f32[2,4,2,32,1024]{4,3,2,1,0:T(8,128)S(1)}, f32[2,4,2,32,1024]{4,3,2,1,0:T(8,128)}, u32[]{:S(2)}, u32[]{:S(2)}) collective-permute-start(f32[2,4,2,32,1024]{4,3,2,1,0:T(8,128)S(1)} %pad_maximum_fusion.refs_1_), channel_id=1, source_target_pairs={{0,4},{4,0},{8,12},{12,8},{16,20},{20,16},{24,28},{28,24},{1,5},{5... | collective-permute-start | bytes 6291464 | tf_op jit(solution)/shard_map/ppermute | solution.py:535
  151.8 16.3 %collective-permute-start.11 = (f32[128,256]{1,0:T(8,128)S(1)}, f32[128,256]{1,0:T(8,128)S(1)}, u32[]{:S(2)}, u32[]{:S(2)}) collective-permute-start(f32[128,256]{1,0:T(8,128)S(1)} %constant_dynamic-slice_fusion.7), channel_id=1, source_target_pairs={{0,8},{4,12},{8,0},{12,4},{16,24},{20,28},{24,16},{28,20},{1,9},{5... | collective-permute-start | bytes 393224 | tf_op jit(solution)/shard_map/ppermute | solution.py:535
  169.6 16.8 %collective-permute-start.14 = (f32[128,768]{1,0:T(8,128)S(1)}, f32[128,768]{1,0:T(8,128)S(1)}, u32[]{:S(2)}, u32[]{:S(2)}) collective-permute-start(f32[128,768]{1,0:T(8,128)S(1)} %constant_dynamic-slice_fusion.5), channel_id=1, source_target_pairs={{0,8},{4,12},{8,0},{12,4},{16,24},{20,28},{24,16},{28,20},{1,9},{5... | collective-permute-start | bytes 1179656 | tf_op jit(solution)/shard_map/ppermute | solution.py:535
  170.1 16.2 %collective-permute-start.13 = (f32[128,512]{1,0:T(8,128)S(1)}, f32[128,512]{1,0:T(8,128)S(1)}, u32[]{:S(2)}, u32[]{:S(2)}) collective-permute-start(f32[128,512]{1,0:T(8,128)S(1)} %constant_dynamic-slice_fusion.6), channel_id=1, source_target_pairs={{0,8},{4,12},{8,0},{12,4},{16,24},{20,28},{24,16},{28,20},{1,9},{5... | collective-permute-start | bytes 786440 | tf_op jit(solution)/shard_map/ppermute | solution.py:535
  186.5 14.5 %collective-permute-start.16 = (f32[128,1024]{1,0:T(8,128)S(1)}, f32[128,1024]{1,0:T(8,128)}, u32[]{:S(2)}, u32[]{:S(2)}) collective-permute-start(f32[128,1024]{1,0:T(8,128)S(1)} %constant_dynamic-slice_fusion.4), channel_id=1, source_target_pairs={{0,8},{4,12},{8,0},{12,4},{16,24},{20,28},{24,16},{28,20},{1,9},{5... | collective-permute-start | bytes 1572872 | tf_op jit(solution)/shard_map/ppermute | solution.py:535
  188.0 13.0 %collective-permute-start.17 = (f32[128,768]{1,0:T(8,128)S(1)}, f32[128,768]{1,0:T(8,128)S(1)}, u32[]{:S(2)}, u32[]{:S(2)}) collective-permute-start(f32[128,768]{1,0:T(8,128)S(1)} %collective-permute-done.14.refs_5_.refs_11_), channel_id=1, source_target_pairs={{0,4},{4,0},{8,12},{12,8},{16,20},{20,16},{24,28},{28,24},{1,5},{5... | collective-permute-start | bytes 1179656 | tf_op jit(solution)/shard_map/ppermute | solution.py:535
  204.0 25.2 %collective-permute-start.19 = (f32[1,4,2,32,1024]{4,3,2,1,0:T(8,128)S(1)}, f32[1,4,2,32,1024]{4,3,2,1,0:T(8,128)S(1)}, u32[]{:S(2)}, u32[]{:S(2)}) collective-permute-start(f32[1,4,2,32,1024]{4,3,2,1,0:T(8,128)S(1)} %bitcast.49), channel_id=1, source_target_pairs={{0,8},{4,12},{8,0},{12,4},{16,24},{20,28},{24,16},{28,20},{1,9},{5... | collective-permute-start | bytes 3145736 | tf_op jit(solution)/shard_map/ppermute | solution.py:535
  204.7 25.0 %collective-permute-start.20 = (f32[1,4,2,2,16,1024]{5,4,3,1,0,2:T(8,128)S(1)}, f32[1,4,2,2,16,1024]{5,4,3,1,0,2:T(8,128)S(1)}, u32[]{:S(2)}, u32[]{:S(2)}) collective-permute-start(f32[1,4,2,2,16,1024]{5,4,3,1,0,2:T(8,128)S(1)} %get-tuple-element.207), channel_id=1, source_target_pairs={{0,16},{4,20},{8,24},{12,28},{16,0},{20,4},{24,8},{28,12},{1,17},{... | collective-permute-start | bytes 3145736 | tf_op jit(solution)/shard_map/ppermute | solution.py:535
  238.5 14.0 %collective-permute-start.23 = (f32[2,4,16,1024]{3,2,1,0:T(8,128)S(1)}, f32[2,4,16,1024]{3,2,1,0:T(8,128)S(1)}, u32[]{:S(2)}, u32[]{:S(2)}) collective-permute-start(f32[2,4,16,1024]{3,2,1,0:T(8,128)S(1)} %get-tuple-element.171), channel_id=1, source_target_pairs={{0,8},{4,12},{8,0},{12,4},{16,24},{20,28},{24,16},{28,20},{1,9},{5... | collective-permute-start | bytes 1572872 | tf_op jit(solution)/shard_map/ppermute | solution.py:535
  240.1 12.5 %collective-permute-start.22 = (f32[128,256]{1,0:T(8,128)S(1)}, f32[128,256]{1,0:T(8,128)S(1)}, u32[]{:S(2)}, u32[]{:S(2)}) collective-permute-start(f32[128,256]{1,0:T(8,128)S(1)} %constant_dynamic-slice_fusion.3), channel_id=1, source_target_pairs={{0,16},{4,20},{8,24},{12,28},{16,0},{20,4},{24,8},{28,12},{1,17},{... | collective-permute-start | bytes 393224 | tf_op jit(solution)/shard_map/ppermute | solution.py:535
  252.7 14.6 %collective-permute-start.26 = (f32[4,4,16,1024]{3,2,1,0:T(8,128)S(1)}, f32[4,4,16,1024]{3,2,1,0:T(8,128)S(1)}, u32[]{:S(2)}, u32[]{:S(2)}) collective-permute-start(f32[4,4,16,1024]{3,2,1,0:T(8,128)S(1)} %pad_maximum_fusion.4.refs_1_), channel_id=1, source_target_pairs={{0,4},{4,0},{8,12},{12,8},{16,20},{20,16},{24,28},{28,24},{1,5},{5... | collective-permute-start | bytes 3145736 | tf_op jit(solution)/shard_map/ppermute | solution.py:535
  252.8 14.3 %collective-permute-start.27 = (f32[2,4,16,1024]{3,2,1,0:T(8,128)S(1)}, f32[2,4,16,1024]{3,2,1,0:T(8,128)S(1)}, u32[]{:S(2)}, u32[]{:S(2)}) collective-permute-start(f32[2,4,16,1024]{3,2,1,0:T(8,128)S(1)} %get-tuple-element.178), channel_id=1, source_target_pairs={{0,8},{4,12},{8,0},{12,4},{16,24},{20,28},{24,16},{28,20},{1,9},{5... | collective-permute-start | bytes 1572872 | tf_op jit(solution)/shard_map/ppermute | solution.py:535
  254.4 12.9 %collective-permute-start.24 = (f32[128,512]{1,0:T(8,128)S(1)}, f32[128,512]{1,0:T(8,128)S(1)}, u32[]{:S(2)}, u32[]{:S(2)}) collective-permute-start(f32[128,512]{1,0:T(8,128)S(1)} %constant_dynamic-slice_fusion.2), channel_id=1, source_target_pairs={{0,16},{4,20},{8,24},{12,28},{16,0},{20,4},{24,8},{28,12},{1,17},{... | collective-permute-start | bytes 786440 | tf_op jit(solution)/shard_map/ppermute | solution.py:535
  267.2 23.0 %collective-permute-start.31 = (f32[4,4,16,1024]{3,2,1,0:T(8,128)S(1)}, f32[4,4,16,1024]{3,2,1,0:T(8,128)S(1)}, u32[]{:S(2)}, u32[]{:S(2)}) collective-permute-start(f32[4,4,16,1024]{3,2,1,0:T(8,128)S(1)} %pad_maximum_fusion.5.refs_1_), channel_id=1, source_target_pairs={{0,4},{4,0},{8,12},{12,8},{16,20},{20,16},{24,28},{28,24},{1,5},{5... | collective-permute-start | bytes 3145736 | tf_op jit(solution)/shard_map/ppermute | solution.py:535
  267.7 22.5 %collective-permute-start.29 = (f32[128,1024]{1,0:T(8,128)S(1)}, f32[128,1024]{1,0:T(8,128)S(1)}, u32[]{:S(2)}, u32[]{:S(2)}) collective-permute-start(f32[128,1024]{1,0:T(8,128)S(1)} %constant_dynamic-slice_fusion), channel_id=1, source_target_pairs={{0,16},{4,20},{8,24},{12,28},{16,0},{20,4},{24,8},{28,12},{1,17},{... | collective-permute-start | bytes 1572872 | tf_op jit(solution)/shard_map/ppermute | solution.py:535
  269.0 21.2 %collective-permute-start.28 = (f32[128,768]{1,0:T(8,128)S(1)}, f32[128,768]{1,0:T(8,128)S(1)}, u32[]{:S(2)}, u32[]{:S(2)}) collective-permute-start(f32[128,768]{1,0:T(8,128)S(1)} %constant_dynamic-slice_fusion.1), channel_id=1, source_target_pairs={{0,16},{4,20},{8,24},{12,28},{16,0},{20,4},{24,8},{28,12},{1,17},{... | collective-permute-start | bytes 1179656 | tf_op jit(solution)/shard_map/ppermute | solution.py:535
  298.5 25.2 %collective-permute-start.34 = (f32[2,4,2,16,1024]{4,3,2,1,0:T(8,128)S(1)}, f32[2,4,2,16,1024]{4,3,2,1,0:T(8,128)S(1)}, u32[]{:S(2)}, u32[]{:S(2)}) collective-permute-start(f32[2,4,2,16,1024]{4,3,2,1,0:T(8,128)S(1)} %slice_bitcast_fusion), channel_id=1, source_target_pairs={{0,8},{4,12},{8,0},{12,4},{16,24},{20,28},{24,16},{28,20},{1,9},{5... | collective-permute-start | bytes 3145736 | tf_op jit(solution)/shard_map/ppermute | solution.py:535
  (69 other events, 484.6 us)
Sparse Core Ops, SparseCore 0:
  30.3 28.2 all-gather.8
  60.2 27.4 all-gather.12
  89.8 45.3 all-gather.10
  138.0 44.8 all-gather.14
